TPU v7x, 128 devices: a whole 4x4x4 slice. The times are simulated.
128 devices in a mesh: seq: 64 (over z, x, y), dp: 2 (over core).
Axes of the slice: x: 4, y: 4, z: 4, core: 2. Of those that a mesh axis runs over, the one named last changes fastest.
Arguments:
- queries: bfloat16 [262144, 128], P(('dp', 'seq')), parts along dimension 0, may hold values from -42 to 42
- keys: bfloat16 [262144, 128], P(('dp', 'seq')), parts along dimension 0, may hold values from -4 to 4
- values: bfloat16 [262144, 128], P(('dp', 'seq')), parts along dimension 0, may hold values from -6 to 6
- grad_out: bfloat16 [262144, 128], P(('dp', 'seq')), parts along dimension 0, may hold values from -6 to 6
- block_lists: int32 [2048, 30], P(('dp', 'seq')), parts along dimension 0, may hold values from 0 to 15, as said below
Outputs:
- attn_out: bfloat16 [262144, 128], P(('dp', 'seq')), parts along dimension 0
- grad_query: bfloat16 [262144, 128], P(('dp', 'seq')), parts along dimension 0
- grad_key: bfloat16 [262144, 128], P(('dp', 'seq')), parts along dimension 0
- grad_value: bfloat16 [262144, 128], P(('dp', 'seq')), parts along dimension 0
There are 2 independent parts, one for each index of `dp`. A program takes and returns all parts, laid end to end along the dimension named above; each array names one. Nothing has to cross between parts.
Inputs may be any that keep to these rules, and one draw needn't show every extreme that they name: `block_lists`: the columns of band k and one side hold (16) / 2**k distinct local block numbers, each a multiple of 2**(k-1).
All inputs are finite; a program needn't handle non-finite values.
Results may differ from a plain program's by a relative error of at most 0.03.
Values may be sent and summed in bfloat16 or wider, within the bound.
No kernel may reach another device: no remote copies, remote signals or barrier semaphores. Data moves between devices by JAX's collectives and lax.ppermute only.
A program may use at most 192 MiB of HBM per device.

v0:
```python
from functools import reduce
import math

import jax
import jax.numpy as jnp
from jax import lax
from jax.sharding import PartitionSpec as P

BLOCK = 128
FAR = 4


def from_behind(value, axis, steps):
    count = lax.axis_size(axis)
    leading, last = (max(0, -steps), min(count, count - steps))
    return lax.ppermute(value, axis, [(source, source + steps) for source in range(leading, last)])


def band_plan(nblk):
    plan = []
    start = 0
    for band in range(1, FAR + 1):
        stride = 2 ** (band - 1)
        sel = nblk >> band
        for sign in (1, -1):
            plan.append((stride, sel, start, sign * stride))
            start += sel
    return plan


def score_terms(query_blocks, key_group, shared, scale):
    form = "qrd,ncd->qrnc" if shared else "qrd,qncd->qrnc"
    return scale * jnp.einsum(form, query_blocks, key_group, preferred_element_type=jnp.float32)


def local(queries, keys, values, grad_out, block_lists):
    head = queries.shape[1]
    nblk = queries.shape[0] // BLOCK
    scale = 1.0 / math.sqrt(head)
    query_blocks = queries.reshape(nblk, BLOCK, head)
    key_blocks = keys.reshape(nblk, BLOCK, head)
    value_blocks = values.reshape(nblk, BLOCK, head)
    grad_blocks = grad_out.reshape(nblk, BLOCK, head)
    position = lax.axis_index("seq")
    devices = lax.axis_size("seq")
    plan = band_plan(nblk)
    remote = []
    for stride, sel, start, by in plan:
        picked = block_lists[:, start : start + sel]
        source = position - by
        valid = jnp.logical_and(source >= 0, source < devices)
        stacked = jnp.stack((key_blocks, value_blocks))
        fetched = from_behind(stacked, "seq", by)
        remote.append((fetched, picked, valid))
    per_step = min(nblk, max(1, 512 // BLOCK))
    step_count = nblk // per_step

    def one_step(carry, step):
        local_key, local_value, far_parts = carry
        first = step * per_step
        query_now = lax.dynamic_slice_in_dim(query_blocks, first, per_step, 0)
        grad_now = lax.dynamic_slice_in_dim(grad_blocks, first, per_step, 0)
        groups = [(key_blocks, value_blocks, jnp.array(True), None, 0)]
        for fetched, index, valid in remote:
            rows = lax.dynamic_slice_in_dim(index, first, per_step, 0)
            groups.append((fetched[0][rows], fetched[1][rows], valid, rows, fetched.shape[1]))
        highs = []
        totals = []
        for key_group, value_group, valid, rows, count in groups:
            score = score_terms(query_now, key_group, rows is None, scale)
            top = jnp.max(score, axis=(2, 3))
            totals.append(jnp.sum(jnp.exp(score - top[:, :, None, None]), axis=(2, 3)))
            highs.append(jnp.where(valid, top, -jnp.inf))
        peak = reduce(jnp.maximum, highs)
        total = reduce(jnp.add, [part * jnp.exp(high - peak) for part, high in zip(totals, highs)])
        lse = peak + jnp.log(total)
        acc = jnp.zeros((per_step, BLOCK, head), jnp.float32)
        for key_group, value_group, valid, rows, count in groups:
            score = score_terms(query_now, key_group, rows is None, scale)
            weight = jnp.where(valid, jnp.exp(score - lse[:, :, None, None]), 0.0).astype(
                jnp.bfloat16
            )
            form = "qrnc,ncd->qrd" if rows is None else "qrnc,qncd->qrd"
            acc = acc + jnp.einsum(form, weight, value_group, preferred_element_type=jnp.float32)
        out_now = acc.astype(jnp.bfloat16)
        delta = jnp.sum(grad_now.astype(jnp.float32) * out_now.astype(jnp.float32), axis=-1)
        dquery = jnp.zeros((per_step, BLOCK, head), jnp.float32)
        new_parts = []
        for slot, (key_group, value_group, valid, rows, count) in enumerate(groups):
            shared = rows is None
            score = score_terms(query_now, key_group, shared, scale)
            prob = jnp.where(valid, jnp.exp(score - lse[:, :, None, None]), 0.0)
            weight = prob.astype(jnp.bfloat16)
            form = "qrd,ncd->qrnc" if shared else "qrd,qncd->qrnc"
            dweight = jnp.einsum(form, grad_now, value_group, preferred_element_type=jnp.float32)
            dscore = (prob * (dweight - delta[:, :, None, None])).astype(jnp.bfloat16)
            back = "qrnc,ncd->qrd" if shared else "qrnc,qncd->qrd"
            dquery = dquery + jnp.einsum(
                back, dscore, key_group, preferred_element_type=jnp.float32
            )
            if shared:
                local_key = local_key + jnp.einsum(
                    "qrnc,qrd->ncd", dscore, query_now, preferred_element_type=jnp.float32
                )
                local_value = local_value + jnp.einsum(
                    "qrnc,qrd->ncd", weight, grad_now, preferred_element_type=jnp.float32
                )
            else:
                part_key = jnp.einsum(
                    "qrnc,qrd->qncd", dscore, query_now, preferred_element_type=jnp.float32
                )
                part_value = jnp.einsum(
                    "qrnc,qrd->qncd", weight, grad_now, preferred_element_type=jnp.float32
                )
                both = jnp.stack((part_key, part_value)).reshape(2, -1, BLOCK, head)
                new_parts.append(far_parts[slot - 1].at[:, rows.reshape(-1)].add(both))
        return (
            (local_key, local_value, tuple(new_parts)),
            (out_now, (scale * dquery).astype(jnp.bfloat16)),
        )

    empty = jnp.zeros((nblk, BLOCK, head), jnp.float32)
    far_init = tuple(
        (
            jnp.zeros((2, fetched.shape[1], BLOCK, head), jnp.float32)
            for fetched, index, valid in remote
        )
    )
    (local_key, local_value, far_parts), (outs, dqueries) = lax.scan(
        one_step, (empty, empty, far_init), jnp.arange(step_count, dtype=jnp.int32)
    )
    key_total = local_key
    value_total = local_value
    for (stride, sel, start, by), part in zip(plan, far_parts):
        returned = from_behind(part, "seq", -by)
        key_total = key_total + returned[0]
        value_total = value_total + returned[1]
    tokens_here = nblk * BLOCK
    attn_out = outs.reshape(tokens_here, head)
    grad_query = dqueries.reshape(tokens_here, head)
    grad_key = (scale * key_total).astype(jnp.bfloat16).reshape(tokens_here, head)
    grad_value = value_total.astype(jnp.bfloat16).reshape(tokens_here, head)
    return (attn_out, grad_query, grad_key, grad_value)


def solution(mesh):
    placed = (
        P(("dp", "seq"), None),
        P(("dp", "seq"), None),
        P(("dp", "seq"), None),
        P(("dp", "seq"), None),
        P(("dp", "seq"), None),
    )
    return jax.shard_map(
        local,
        mesh=mesh,
        in_specs=placed,
        out_specs=(
            P(("dp", "seq"), None),
            P(("dp", "seq"), None),
            P(("dp", "seq"), None),
            P(("dp", "seq"), None),
        ),
        check_vma=False,
    )
```

profile of v0, /device:TPU:96, one launch (start us, length us, event | category | flops | bytes accessed | tf_op | source)
XLA Modules:
  0.0 1084.8 jit_solution(11941200424646460787)
XLA Ops:
  2.0 4.8 collective-permute-start.7
  6.8 3.5 collective-permute-start.6
  10.3 4.5 collective-permute-start.5
  16.7 8.7 collective-permute-start.3
  25.4 6.2 collective-permute-done.7
  31.6 5.1 collective-permute-start.2
  36.7 17.3 %collective-permute-done.6 = bf16[2,16,128,128]{3,2,1,0:T(8,128)(2,1)} collective-permute-done((bf16[2,16,128,128]{3,2,1,0:T(8,128)(2,1)S(1)}, bf16[2,16,128,128]{3,2,1,0:T(8,128)(2,1)}, u32[]{:S(2)}, u32[]{:S(2)}) %collective-permute-start.6) | collective-permute-done | bytes 1048608 | tf_op jit(solution)/shard_map/ppermute | solution.py:16
  53.9 6.7 collective-permute-start.1
  60.6 15.9 %collective-permute-done.5 = bf16[2,16,128,128]{3,2,1,0:T(8,128)(2,1)} collective-permute-done((bf16[2,16,128,128]{3,2,1,0:T(8,128)(2,1)S(1)}, bf16[2,16,128,128]{3,2,1,0:T(8,128)(2,1)}, u32[]{:S(2)}, u32[]{:S(2)}) %collective-permute-start.5) | collective-permute-done | bytes 1048608 | tf_op jit(solution)/shard_map/ppermute | solution.py:16
  76.5 3.5 collective-permute-start
  82.6 14.2 %collective-permute-done.3 = bf16[2,16,128,128]{3,2,1,0:T(8,128)(2,1)} collective-permute-done((bf16[2,16,128,128]{3,2,1,0:T(8,128)(2,1)S(1)}, bf16[2,16,128,128]{3,2,1,0:T(8,128)(2,1)}, u32[]{:S(2)}, u32[]{:S(2)}) %collective-permute-start.3) | collective-permute-done | bytes 1048608 | tf_op jit(solution)/shard_map/ppermute | solution.py:16
  96.8 3.8 collective-permute-done.2
  100.6 19.6 %collective-permute-done.1 = bf16[2,16,128,128]{3,2,1,0:T(8,128)(2,1)} collective-permute-done((bf16[2,16,128,128]{3,2,1,0:T(8,128)(2,1)S(1)}, bf16[2,16,128,128]{3,2,1,0:T(8,128)(2,1)}, u32[]{:S(2)}, u32[]{:S(2)}) %collective-permute-start.1) | collective-permute-done | bytes 1048608 | tf_op jit(solution)/shard_map/ppermute | solution.py:16
  120.2 2.7 collective-permute-done
  136.2 612.3 %while.33 = (s32[]{:T(128)}, f32[16,128,128]{2,1,0:T(8,128)}, f32[16,128,128]{2,1,0:T(8,128)}, f32[2,16,128,128]{3,2,1,0:T(8,128)}, f32[2,16,128,128]{3,2,1,0:T(...) while((s32[]{:T(128)}, f32[16,128,128]{2,1,0:T(8,128)}, ...), condition=%wide.region_28.29_spmd.clone, body=%wide.region_0.28_spmd.clone.sunk | while | flops 4691415552 | bytes 413883328 | solution.py:129
  185.7 2.7 slice_bitcast_fusion.38
  198.9 2.9 slice_bitcast_fusion.39
  207.0 2.7 gather_fusion.7
  209.7 2.7 gather_fusion.11
  245.5 4.3 scatter_fusion.3
  251.2 3.2 scatter_fusion.4
  254.3 3.2 scatter_fusion.5
  261.6 6.8 scatter_fusion
  273.6 6.8 scatter_fusion.1
  284.1 5.1 scatter_fusion.2
  289.2 4.2 fusion.444
  333.1 2.7 slice_bitcast_fusion.38
  346.4 2.9 slice_bitcast_fusion.39
  354.4 2.7 gather_fusion.7
  357.1 2.7 gather_fusion.11
  392.9 4.3 scatter_fusion.3
  398.6 3.2 scatter_fusion.4
  401.8 3.2 scatter_fusion.5
  409.1 6.8 scatter_fusion
  421.0 6.8 scatter_fusion.1
  431.5 5.1 scatter_fusion.2
  436.6 4.5 fusion.444
  494.2 2.9 slice_bitcast_fusion.39
  502.2 2.7 gather_fusion.7
  540.7 4.3 scatter_fusion.3
  546.4 3.2 scatter_fusion.4
  549.6 3.2 scatter_fusion.5
  556.9 6.8 scatter_fusion
  568.8 6.8 scatter_fusion.1
  579.4 5.1 scatter_fusion.2
  584.4 4.5 fusion.444
  641.9 2.9 slice_bitcast_fusion.39
  649.9 2.7 gather_fusion.7
  688.5 4.3 scatter_fusion.3
  694.2 3.2 scatter_fusion.4
  697.4 3.2 scatter_fusion.5
  704.7 6.8 scatter_fusion
  716.6 6.8 scatter_fusion.1
  727.1 5.1 scatter_fusion.2
  732.2 4.5 fusion.444
  748.5 6.3 collective-permute-start.8
  756.7 3.4 collective-permute-start.10
  760.0 4.0 collective-permute-start.11
  766.0 98.3 %collective-permute-done.8 = f32[2,16,128,128]{3,2,1,0:T(8,128)S(1)} collective-permute-done((f32[2,16,128,128]{3,2,1,0:T(8,128)}, f32[2,16,128,128]{3,2,1,0:T(8,128)S(1)}, u32[]{:S(2)}, u32[]{:S(2)}) %collective-permute-start.8) | collective-permute-done | bytes 2097184 | tf_op jit(solution)/shard_map/ppermute | solution.py:16
  866.2 32.2 %collective-permute-start.14 = (f32[2,16,128,128]{3,2,1,0:T(8,128)}, f32[2,16,128,128]{3,2,1,0:T(8,128)S(1)}, u32[]{:S(2)}, u32[]{:S(2)}) collective-permute-start(f32[2,16,128,128]{3,2,1,0:T(8,128)} %get-tuple-element.236), channel_id=1, source_target_pairs={{16,0},{18,2},{20,4},{22,6},{24,8},{26,10},{28,12},{30,14},{32,16}... | collective-permute-start | bytes 6291464 | tf_op jit(solution)/shard_map/ppermute | solution.py:16
  898.3 130.2 %collective-permute-done.10 = f32[2,16,128,128]{3,2,1,0:T(8,128)S(1)} collective-permute-done((f32[2,16,128,128]{3,2,1,0:T(8,128)}, f32[2,16,128,128]{3,2,1,0:T(8,128)S(1)}, u32[]{:S(2)}, u32[]{:S(2)}) %collective-permute-start.10) | collective-permute-done | bytes 2097184 | tf_op jit(solution)/shard_map/ppermute | solution.py:16
  1030.4 42.3 %collective-permute-done.12 = f32[2,16,128,128]{3,2,1,0:T(8,128)S(1)} collective-permute-done((f32[2,16,128,128]{3,2,1,0:T(8,128)}, f32[2,16,128,128]{3,2,1,0:T(8,128)S(1)}, u32[]{:S(2)}, u32[]{:S(2)}) %collective-permute-start.12) | collective-permute-done | bytes 2097184 | tf_op jit(solution)/shard_map/ppermute | solution.py:16
  1072.7 6.5 collective-permute-done.15
  1079.2 5.3 fusion.135
  (1215 shorter events, 441.9 us)
Async XLA Ops:
  0.6 80.7 %copy-start.52 = (bf16[2048,128]{1,0:T(8,128)(2,1)S(1)}, bf16[2048,128]{1,0:T(8,128)(2,1)}, u32[]{:S(2)}) copy-start(bf16[2048,128]{1,0:T(8,128)(2,1)} %param.9) | copy-start | bytes 1572868
  0.6 79.4 %copy-start.53 = (s32[16,30]{1,0:T(8,128)S(1)}, s32[16,30]{1,0:T(8,128)}, u32[]{:S(2)}) copy-start(s32[16,30]{1,0:T(8,128)} %param.11) | copy-start | bytes 5764
  2.0 29.5 %collective-permute-start.7 = (bf16[2,16,128,128]{3,2,1,0:T(8,128)(2,1)S(1)}, bf16[2,16,128,128]{3,2,1,0:T(8,128)(2,1)}, u32[]{:S(2)}, u32[]{:S(2)}) collective-permute-start(bf16[2,16,128,128]{3,2,1,0:T(8,128)(2,1)S(1)} %pad_maximum_fusion), channel_id=1, source_target_pairs={{16,0},{18,2},{20,4},{22,6},{24,8},{26,10},{28,12},{30,14},{32,16}... | collective-permute-start | bytes 3145736 | tf_op jit(solution)/shard_map/ppermute | solution.py:16
  6.8 47.1 %collective-permute-start.6 = (bf16[2,16,128,128]{3,2,1,0:T(8,128)(2,1)S(1)}, bf16[2,16,128,128]{3,2,1,0:T(8,128)(2,1)}, u32[]{:S(2)}, u32[]{:S(2)}) collective-permute-start(bf16[2,16,128,128]{3,2,1,0:T(8,128)(2,1)S(1)} %pad_maximum_fusion), channel_id=1, source_target_pairs={{0,16},{2,18},{4,20},{6,22},{8,24},{10,26},{12,28},{14,30},{16,32}... | collective-permute-start | bytes 3145736 | tf_op jit(solution)/shard_map/ppermute | solution.py:16
  10.3 66.1 %collective-permute-start.5 = (bf16[2,16,128,128]{3,2,1,0:T(8,128)(2,1)S(1)}, bf16[2,16,128,128]{3,2,1,0:T(8,128)(2,1)}, u32[]{:S(2)}, u32[]{:S(2)}) collective-permute-start(bf16[2,16,128,128]{3,2,1,0:T(8,128)(2,1)S(1)} %pad_maximum_fusion), channel_id=1, source_target_pairs={{8,0},{10,2},{12,4},{14,6},{16,8},{18,10},{20,12},{22,14},{24,16},... | collective-permute-start | bytes 3145736 | tf_op jit(solution)/shard_map/ppermute | solution.py:16
  14.8 67.8 %collective-permute-start.4 = (bf16[2,16,128,128]{3,2,1,0:T(8,128)(2,1)S(1)}, bf16[2,16,128,128]{3,2,1,0:T(8,128)(2,1)}, u32[]{:S(2)}, u32[]{:S(2)}) collective-permute-start(bf16[2,16,128,128]{3,2,1,0:T(8,128)(2,1)S(1)} %pad_maximum_fusion), channel_id=1, source_target_pairs={{0,8},{2,10},{4,12},{6,14},{8,16},{10,18},{12,20},{14,22},{16,24},... | collective-permute-start | bytes 3145736 | tf_op jit(solution)/shard_map/ppermute | solution.py:16
  16.7 80.1 %collective-permute-start.3 = (bf16[2,16,128,128]{3,2,1,0:T(8,128)(2,1)S(1)}, bf16[2,16,128,128]{3,2,1,0:T(8,128)(2,1)}, u32[]{:S(2)}, u32[]{:S(2)}) collective-permute-start(bf16[2,16,128,128]{3,2,1,0:T(8,128)(2,1)S(1)} %pad_maximum_fusion), channel_id=1, source_target_pairs={{4,0},{6,2},{8,4},{10,6},{12,8},{14,10},{16,12},{18,14},{20,16},{2... | collective-permute-start | bytes 3145736 | tf_op jit(solution)/shard_map/ppermute | solution.py:16
  31.6 69.0 %collective-permute-start.2 = (bf16[2,16,128,128]{3,2,1,0:T(8,128)(2,1)S(1)}, bf16[2,16,128,128]{3,2,1,0:T(8,128)(2,1)}, u32[]{:S(2)}, u32[]{:S(2)}) collective-permute-start(bf16[2,16,128,128]{3,2,1,0:T(8,128)(2,1)S(1)} %pad_maximum_fusion), channel_id=1, source_target_pairs={{0,4},{2,6},{4,8},{6,10},{8,12},{10,14},{12,16},{14,18},{16,20},{1... | collective-permute-start | bytes 3145736 | tf_op jit(solution)/shard_map/ppermute | solution.py:16
  53.9 66.2 %collective-permute-start.1 = (bf16[2,16,128,128]{3,2,1,0:T(8,128)(2,1)S(1)}, bf16[2,16,128,128]{3,2,1,0:T(8,128)(2,1)}, u32[]{:S(2)}, u32[]{:S(2)}) collective-permute-start(bf16[2,16,128,128]{3,2,1,0:T(8,128)(2,1)S(1)} %pad_maximum_fusion), channel_id=1, source_target_pairs={{2,0},{4,2},{6,4},{8,6},{10,8},{12,10},{14,12},{16,14},{18,16},{20... | collective-permute-start | bytes 3145736 | tf_op jit(solution)/shard_map/ppermute | solution.py:16
  76.5 46.4 %collective-permute-start = (bf16[2,16,128,128]{3,2,1,0:T(8,128)(2,1)S(1)}, bf16[2,16,128,128]{3,2,1,0:T(8,128)(2,1)}, u32[]{:S(2)}, u32[]{:S(2)}) collective-permute-start(bf16[2,16,128,128]{3,2,1,0:T(8,128)(2,1)S(1)} %pad_maximum_fusion), channel_id=1, source_target_pairs={{0,2},{2,4},{4,6},{6,8},{8,10},{10,12},{12,14},{14,16},{16,18},{18... | collective-permute-start | bytes 3145736 | tf_op jit(solution)/shard_map/ppermute | solution.py:16
  157.4 11.9 %copy-start.70 = (s32[16,8]{1,0:T(8,128)}, s32[16,8]{1,0:T(8,128)S(1)}, u32[]{:S(2)}) copy-start(s32[16,8]{1,0:T(8,128)S(1)} %get-tuple-element.1076) | copy-start | bytes 1540 | tf_op jit(solution)/shard_map/while
  157.4 11.9 %copy-start.72 = (s32[16,8]{1,0:T(8,128)}, s32[16,8]{1,0:T(8,128)S(1)}, u32[]{:S(2)}) copy-start(s32[16,8]{1,0:T(8,128)S(1)} %get-tuple-element.1073) | copy-start | bytes 1540 | tf_op jit(solution)/shard_map/while
  157.4 11.9 %copy-start.74 = (s32[16,4]{1,0:T(8,128)}, s32[16,4]{1,0:T(8,128)S(1)}, u32[]{:S(2)}) copy-start(s32[16,4]{1,0:T(8,128)S(1)} %get-tuple-element.1082) | copy-start | bytes 772 | tf_op jit(solution)/shard_map/while
  157.4 11.9 %copy-start.76 = (s32[16,4]{1,0:T(8,128)}, s32[16,4]{1,0:T(8,128)S(1)}, u32[]{:S(2)}) copy-start(s32[16,4]{1,0:T(8,128)S(1)} %get-tuple-element.1079) | copy-start | bytes 772 | tf_op jit(solution)/shard_map/while
  157.4 11.9 %copy-start.78 = (s32[16,2]{1,0:T(8,128)}, s32[16,2]{1,0:T(8,128)S(1)}, u32[]{:S(2)}) copy-start(s32[16,2]{1,0:T(8,128)S(1)} %get-tuple-element.1088) | copy-start | bytes 388 | tf_op jit(solution)/shard_map/while
  157.4 11.9 %copy-start.80 = (s32[16,2]{1,0:T(8,128)}, s32[16,2]{1,0:T(8,128)S(1)}, u32[]{:S(2)}) copy-start(s32[16,2]{1,0:T(8,128)S(1)} %get-tuple-element.1085) | copy-start | bytes 388 | tf_op jit(solution)/shard_map/while
  160.1 9.2 copy-start.66
  160.1 9.2 copy-start.68
  171.0 7.3 copy-start.38
  173.4 50.5 %copy-start.40 = (bf16[4,128,128]{2,1,0:T(8,128)(2,1)}, bf16[4,128,128]{2,1,0:T(8,128)(2,1)S(1)}, u32[]{:S(2)}) copy-start(bf16[4,128,128]{2,1,0:T(8,128)(2,1)S(1)} %gather_fusion.14) | copy-start | bytes 393220 | tf_op jit(solution)/shard_map/while
  185.7 6.8 copy-start.59
  225.9 15.9 %copy-start.41 = (bf16[4,128,128]{1,2,0:T(8,128)(2,1)}, bf16[4,128,128]{1,2,0:T(8,128)(2,1)S(1)}, u32[]{:S(2)}) copy-start(bf16[4,128,128]{1,2,0:T(8,128)(2,1)S(1)} %fusion.467) | copy-start | bytes 393220 | tf_op jit(solution)/shard_map/while
  304.8 11.9 %copy-start.70 = (s32[16,8]{1,0:T(8,128)}, s32[16,8]{1,0:T(8,128)S(1)}, u32[]{:S(2)}) copy-start(s32[16,8]{1,0:T(8,128)S(1)} %get-tuple-element.1076) | copy-start | bytes 1540 | tf_op jit(solution)/shard_map/while
  304.8 11.9 %copy-start.72 = (s32[16,8]{1,0:T(8,128)}, s32[16,8]{1,0:T(8,128)S(1)}, u32[]{:S(2)}) copy-start(s32[16,8]{1,0:T(8,128)S(1)} %get-tuple-element.1073) | copy-start | bytes 1540 | tf_op jit(solution)/shard_map/while
  304.8 11.9 %copy-start.74 = (s32[16,4]{1,0:T(8,128)}, s32[16,4]{1,0:T(8,128)S(1)}, u32[]{:S(2)}) copy-start(s32[16,4]{1,0:T(8,128)S(1)} %get-tuple-element.1082) | copy-start | bytes 772 | tf_op jit(solution)/shard_map/while
  304.9 11.9 %copy-start.76 = (s32[16,4]{1,0:T(8,128)}, s32[16,4]{1,0:T(8,128)S(1)}, u32[]{:S(2)}) copy-start(s32[16,4]{1,0:T(8,128)S(1)} %get-tuple-element.1079) | copy-start | bytes 772 | tf_op jit(solution)/shard_map/while
  304.9 11.9 %copy-start.78 = (s32[16,2]{1,0:T(8,128)}, s32[16,2]{1,0:T(8,128)S(1)}, u32[]{:S(2)}) copy-start(s32[16,2]{1,0:T(8,128)S(1)} %get-tuple-element.1088) | copy-start | bytes 388 | tf_op jit(solution)/shard_map/while
  304.9 11.9 %copy-start.80 = (s32[16,2]{1,0:T(8,128)}, s32[16,2]{1,0:T(8,128)S(1)}, u32[]{:S(2)}) copy-start(s32[16,2]{1,0:T(8,128)S(1)} %get-tuple-element.1085) | copy-start | bytes 388 | tf_op jit(solution)/shard_map/while
  307.5 9.2 copy-start.66
  307.5 9.2 copy-start.68
  318.4 7.3 copy-start.38
  320.8 50.5 %copy-start.40 = (bf16[4,128,128]{2,1,0:T(8,128)(2,1)}, bf16[4,128,128]{2,1,0:T(8,128)(2,1)S(1)}, u32[]{:S(2)}) copy-start(bf16[4,128,128]{2,1,0:T(8,128)(2,1)S(1)} %gather_fusion.14) | copy-start | bytes 393220 | tf_op jit(solution)/shard_map/while
  373.3 15.9 %copy-start.41 = (bf16[4,128,128]{1,2,0:T(8,128)(2,1)}, bf16[4,128,128]{1,2,0:T(8,128)(2,1)S(1)}, u32[]{:S(2)}) copy-start(bf16[4,128,128]{1,2,0:T(8,128)(2,1)S(1)} %fusion.467) | copy-start | bytes 393220 | tf_op jit(solution)/shard_map/while
  452.6 11.9 %copy-start.70 = (s32[16,8]{1,0:T(8,128)}, s32[16,8]{1,0:T(8,128)S(1)}, u32[]{:S(2)}) copy-start(s32[16,8]{1,0:T(8,128)S(1)} %get-tuple-element.1076) | copy-start | bytes 1540 | tf_op jit(solution)/shard_map/while
  452.6 11.9 %copy-start.72 = (s32[16,8]{1,0:T(8,128)}, s32[16,8]{1,0:T(8,128)S(1)}, u32[]{:S(2)}) copy-start(s32[16,8]{1,0:T(8,128)S(1)} %get-tuple-element.1073) | copy-start | bytes 1540 | tf_op jit(solution)/shard_map/while
  452.6 11.9 %copy-start.74 = (s32[16,4]{1,0:T(8,128)}, s32[16,4]{1,0:T(8,128)S(1)}, u32[]{:S(2)}) copy-start(s32[16,4]{1,0:T(8,128)S(1)} %get-tuple-element.1082) | copy-start | bytes 772 | tf_op jit(solution)/shard_map/while
  452.6 11.9 %copy-start.76 = (s32[16,4]{1,0:T(8,128)}, s32[16,4]{1,0:T(8,128)S(1)}, u32[]{:S(2)}) copy-start(s32[16,4]{1,0:T(8,128)S(1)} %get-tuple-element.1079) | copy-start | bytes 772 | tf_op jit(solution)/shard_map/while
  452.6 11.9 %copy-start.78 = (s32[16,2]{1,0:T(8,128)}, s32[16,2]{1,0:T(8,128)S(1)}, u32[]{:S(2)}) copy-start(s32[16,2]{1,0:T(8,128)S(1)} %get-tuple-element.1088) | copy-start | bytes 388 | tf_op jit(solution)/shard_map/while
  452.7 11.9 %copy-start.80 = (s32[16,2]{1,0:T(8,128)}, s32[16,2]{1,0:T(8,128)S(1)}, u32[]{:S(2)}) copy-start(s32[16,2]{1,0:T(8,128)S(1)} %get-tuple-element.1085) | copy-start | bytes 388 | tf_op jit(solution)/shard_map/while
  455.3 9.2 copy-start.66
  455.3 9.2 copy-start.68
  466.2 7.3 copy-start.38
  468.6 50.5 %copy-start.40 = (bf16[4,128,128]{2,1,0:T(8,128)(2,1)}, bf16[4,128,128]{2,1,0:T(8,128)(2,1)S(1)}, u32[]{:S(2)}) copy-start(bf16[4,128,128]{2,1,0:T(8,128)(2,1)S(1)} %gather_fusion.14) | copy-start | bytes 393220 | tf_op jit(solution)/shard_map/while
  480.9 6.8 copy-start.59
  521.1 15.9 %copy-start.41 = (bf16[4,128,128]{1,2,0:T(8,128)(2,1)}, bf16[4,128,128]{1,2,0:T(8,128)(2,1)S(1)}, u32[]{:S(2)}) copy-start(bf16[4,128,128]{1,2,0:T(8,128)(2,1)S(1)} %fusion.467) | copy-start | bytes 393220 | tf_op jit(solution)/shard_map/while
  600.4 11.9 %copy-start.70 = (s32[16,8]{1,0:T(8,128)}, s32[16,8]{1,0:T(8,128)S(1)}, u32[]{:S(2)}) copy-start(s32[16,8]{1,0:T(8,128)S(1)} %get-tuple-element.1076) | copy-start | bytes 1540 | tf_op jit(solution)/shard_map/while
  600.4 11.9 %copy-start.72 = (s32[16,8]{1,0:T(8,128)}, s32[16,8]{1,0:T(8,128)S(1)}, u32[]{:S(2)}) copy-start(s32[16,8]{1,0:T(8,128)S(1)} %get-tuple-element.1073) | copy-start | bytes 1540 | tf_op jit(solution)/shard_map/while
  600.4 11.9 %copy-start.74 = (s32[16,4]{1,0:T(8,128)}, s32[16,4]{1,0:T(8,128)S(1)}, u32[]{:S(2)}) copy-start(s32[16,4]{1,0:T(8,128)S(1)} %get-tuple-element.1082) | copy-start | bytes 772 | tf_op jit(solution)/shard_map/while
  600.4 11.9 %copy-start.76 = (s32[16,4]{1,0:T(8,128)}, s32[16,4]{1,0:T(8,128)S(1)}, u32[]{:S(2)}) copy-start(s32[16,4]{1,0:T(8,128)S(1)} %get-tuple-element.1079) | copy-start | bytes 772 | tf_op jit(solution)/shard_map/while
  600.4 11.9 %copy-start.78 = (s32[16,2]{1,0:T(8,128)}, s32[16,2]{1,0:T(8,128)S(1)}, u32[]{:S(2)}) copy-start(s32[16,2]{1,0:T(8,128)S(1)} %get-tuple-element.1088) | copy-start | bytes 388 | tf_op jit(solution)/shard_map/while
  600.4 11.9 %copy-start.80 = (s32[16,2]{1,0:T(8,128)}, s32[16,2]{1,0:T(8,128)S(1)}, u32[]{:S(2)}) copy-start(s32[16,2]{1,0:T(8,128)S(1)} %get-tuple-element.1085) | copy-start | bytes 388 | tf_op jit(solution)/shard_map/while
  603.1 9.2 copy-start.66
  603.1 9.2 copy-start.68
  614.0 7.3 copy-start.38
  616.4 50.5 %copy-start.40 = (bf16[4,128,128]{2,1,0:T(8,128)(2,1)}, bf16[4,128,128]{2,1,0:T(8,128)(2,1)S(1)}, u32[]{:S(2)}) copy-start(bf16[4,128,128]{2,1,0:T(8,128)(2,1)S(1)} %gather_fusion.14) | copy-start | bytes 393220 | tf_op jit(solution)/shard_map/while
  668.9 15.9 %copy-start.41 = (bf16[4,128,128]{1,2,0:T(8,128)(2,1)}, bf16[4,128,128]{1,2,0:T(8,128)(2,1)S(1)}, u32[]{:S(2)}) copy-start(bf16[4,128,128]{1,2,0:T(8,128)(2,1)S(1)} %fusion.467) | copy-start | bytes 393220 | tf_op jit(solution)/shard_map/while
  748.5 115.8 %collective-permute-start.8 = (f32[2,16,128,128]{3,2,1,0:T(8,128)}, f32[2,16,128,128]{3,2,1,0:T(8,128)S(1)}, u32[]{:S(2)}, u32[]{:S(2)}) collective-permute-start(f32[2,16,128,128]{3,2,1,0:T(8,128)} %get-tuple-element.230), channel_id=1, source_target_pairs={{2,0},{4,2},{6,4},{8,6},{10,8},{12,10},{14,12},{16,14},{18,16},{20... | collective-permute-start | bytes 6291464 | tf_op jit(solution)/shard_map/ppermute | solution.py:16
  754.7 111.4 %collective-permute-start.9 = (f32[2,16,128,128]{3,2,1,0:T(8,128)}, f32[2,16,128,128]{3,2,1,0:T(8,128)S(1)}, u32[]{:S(2)}, u32[]{:S(2)}) collective-permute-start(f32[2,16,128,128]{3,2,1,0:T(8,128)} %get-tuple-element.231), channel_id=1, source_target_pairs={{0,2},{2,4},{4,6},{6,8},{8,10},{10,12},{12,14},{14,16},{16,18},{18... | collective-permute-start | bytes 6291464 | tf_op jit(solution)/shard_map/ppermute | solution.py:16
  756.7 271.8 %collective-permute-start.10 = (f32[2,16,128,128]{3,2,1,0:T(8,128)}, f32[2,16,128,128]{3,2,1,0:T(8,128)S(1)}, u32[]{:S(2)}, u32[]{:S(2)}) collective-permute-start(f32[2,16,128,128]{3,2,1,0:T(8,128)} %get-tuple-element.232), channel_id=1, source_target_pairs={{4,0},{6,2},{8,4},{10,6},{12,8},{14,10},{16,12},{18,14},{20,16},{2... | collective-permute-start | bytes 6291464 | tf_op jit(solution)/shard_map/ppermute | solution.py:16
  760.0 270.4 %collective-permute-start.11 = (f32[2,16,128,128]{3,2,1,0:T(8,128)}, f32[2,16,128,128]{3,2,1,0:T(8,128)S(1)}, u32[]{:S(2)}, u32[]{:S(2)}) collective-permute-start(f32[2,16,128,128]{3,2,1,0:T(8,128)} %get-tuple-element.233), channel_id=1, source_target_pairs={{0,4},{2,6},{4,8},{6,10},{8,12},{10,14},{12,16},{14,18},{16,20},{1... | collective-permute-start | bytes 6291464 | tf_op jit(solution)/shard_map/ppermute | solution.py:16
  764.0 308.7 %collective-permute-start.12 = (f32[2,16,128,128]{3,2,1,0:T(8,128)}, f32[2,16,128,128]{3,2,1,0:T(8,128)S(1)}, u32[]{:S(2)}, u32[]{:S(2)}) collective-permute-start(f32[2,16,128,128]{3,2,1,0:T(8,128)} %get-tuple-element.234), channel_id=1, source_target_pairs={{8,0},{10,2},{12,4},{14,6},{16,8},{18,10},{20,12},{22,14},{24,16},... | collective-permute-start | bytes 6291464 | tf_op jit(solution)/shard_map/ppermute | solution.py:16
  864.2 208.4 %collective-permute-start.13 = (f32[2,16,128,128]{3,2,1,0:T(8,128)}, f32[2,16,128,128]{3,2,1,0:T(8,128)S(1)}, u32[]{:S(2)}, u32[]{:S(2)}) collective-permute-start(f32[2,16,128,128]{3,2,1,0:T(8,128)} %get-tuple-element.235), channel_id=1, source_target_pairs={{0,8},{2,10},{4,12},{6,14},{8,16},{10,18},{12,20},{14,22},{16,24},... | collective-permute-start | bytes 6291464 | tf_op jit(solution)/shard_map/ppermute | solution.py:16
  866.2 206.5 %collective-permute-start.14 = (f32[2,16,128,128]{3,2,1,0:T(8,128)}, f32[2,16,128,128]{3,2,1,0:T(8,128)S(1)}, u32[]{:S(2)}, u32[]{:S(2)}) collective-permute-start(f32[2,16,128,128]{3,2,1,0:T(8,128)} %get-tuple-element.236), channel_id=1, source_target_pairs={{16,0},{18,2},{20,4},{22,6},{24,8},{26,10},{28,12},{30,14},{32,16}... | collective-permute-start | bytes 6291464 | tf_op jit(solution)/shard_map/ppermute | solution.py:16
  1028.5 50.7 %collective-permute-start.15 = (f32[2,16,128,128]{3,2,1,0:T(8,128)}, f32[2,16,128,128]{3,2,1,0:T(8,128)}, u32[]{:S(2)}, u32[]{:S(2)}) collective-permute-start(f32[2,16,128,128]{3,2,1,0:T(8,128)} %get-tuple-element.237), channel_id=1, source_target_pairs={{0,16},{2,18},{4,20},{6,22},{8,24},{10,26},{12,28},{14,30},{16,32}... | collective-permute-start | bytes 6291464 | tf_op jit(solution)/shard_map/ppermute | solution.py:16
  (292 other events, 739.9 us)
where the time goes:
time: 1090 us; the launch traced here: 1080 us
  waiting for transfers between devices  357 us (33%)
  other arithmetic  226 us (21%)
  local copies, waits for them, and re-layouts  223 us (20%)
  matrix products  157 us (14%)
  starting transfers between devices  92 us (8%)
  loops' own time  28.6 us (3%)
    ppermute x16, waiting for transfers between devices, from_behind(): lax.ppermute(value, axis, [(source, source + steps) for source in range(l...  357 us
    scatter-add x32, other arithmetic, one_step(): new_parts.append(far_parts[slot - 1].at[:, rows.reshape(-1)].add(both))  139 us
    ppermute x16, starting transfers between devices, from_behind(): lax.ppermute(value, axis, [(source, source + steps) for source in range(l...  92 us
    gather x32, local copies, waits for them, and re-layouts, one_step(): fetched[0][rows]  55.8 us
    gather x32, local copies, waits for them, and re-layouts, one_step(): fetched[1][rows]  55.4 us
    squeeze x16, local copies, waits for them, and re-layouts, one_step(): fetched[1][rows]  42.2 us
    another operation x24, other arithmetic, one_step(): both = jnp.stack((part_key, part_value)).reshape(2, -1, BLOCK, head)  34.4 us
    while x672, local copies, waits for them, and re-layouts  32.5 us
  transfers between devices with their start and end apart: 16, of which 11 were waited for; matrix products, arithmetic and copies ran while one was open for 0% of the time, Pallas kernels for 0%

commit v1 on v0

v1 whole, which is shorter than its diff:
```python
import functools
import math

import jax
import jax.numpy as jnp
from jax import lax
from jax.experimental import pallas as pl
from jax.experimental.pallas import tpu as pltpu
from jax.sharding import PartitionSpec as P

BLOCK = 128
HEAD = 128
NBLK = 16
FAR = 4
SCALE = 1.0 / math.sqrt(HEAD)
LOG2E = 1.4426950408889634
COEF = SCALE * LOG2E
BIG = 1e30
MIB = 2**20

SLOT_BLOCK = [0, 8, 4, 12, 2, 6, 10, 14, 1, 3, 5, 7, 9, 11, 13, 15]


def band_columns():
    plan = []
    start = 0
    for band in range(1, FAR + 1):
        stride = 2 ** (band - 1)
        sel = NBLK >> band
        for side, sign in enumerate((1, -1)):
            plan.append((band, side, start, sel, sign * stride))
            start += sel
    return plan


PLAN = band_columns()


def nt(a, b):
    return lax.dot_general(a, b, (((1,), (1,)), ((), ())), preferred_element_type=jnp.float32)


def nn(a, b):
    return lax.dot_general(a, b, (((1,), (0,)), ((), ())), preferred_element_type=jnp.float32)


def tn(a, b):
    return lax.dot_general(a, b, (((0,), (0,)), ((), ())), preferred_element_type=jnp.float32)


def shift(value, by):
    count = lax.axis_size("seq")
    first, last = max(0, -by), min(count, count - by)
    return lax.ppermute(value, "seq", [(s, s + by) for s in range(first, last)])


def params(limit=40):
    return pltpu.CompilerParams(vmem_limit_bytes=limit * MIB)


VMEM = pl.BlockSpec(memory_space=pltpu.VMEM)
SMEM = pl.BlockSpec(memory_space=pltpu.SMEM)


def cost(pairs, products, exps, moved):
    return pl.CostEstimate(
        flops=2 * pairs * products * BLOCK * BLOCK * HEAD,
        transcendentals=exps * pairs * BLOCK * BLOCK,
        bytes_accessed=moved,
    )


def pack_kernel(k_ref, v_ref, out_ref):
    for slot, block in enumerate(SLOT_BLOCK):
        out_ref[slot, 0] = k_ref[block]
        out_ref[slot, 1] = v_ref[block]


def pack(key_blocks, value_blocks):
    return pl.pallas_call(
        pack_kernel,
        out_shape=jax.ShapeDtypeStruct((NBLK, 2, BLOCK, HEAD), jnp.bfloat16),
        in_specs=[VMEM, VMEM],
        out_specs=VMEM,
        name="pack",
    )(key_blocks, value_blocks)


def lane_all(x):
    return jnp.broadcast_to(x, (x.shape[0], 128))


def two(ref, a, b, which):
    return jnp.concatenate((ref[a, which], ref[b, which]), axis=0)


def entries_of(group):
    entries = []
    for n, (band, side, start, sel, by) in enumerate(group):
        for c in range(sel):
            entries.append((n, start + c))
    return entries


def forward_local_kernel(q_ref, k_ref, v_ref, m_ref, l_ref, acc_ref, s_ref):
    width = NBLK * BLOCK

    def step(i, carry):
        s = nt(q_ref[i], k_ref[...].reshape(width, HEAD))
        s_ref[...] = s
        top = s[:, :128]
        for j in range(1, NBLK):
            top = jnp.maximum(top, s[:, j * 128 : (j + 1) * 128])
        m = lane_all(jnp.max(top, axis=1, keepdims=True))
        total = jnp.zeros((BLOCK, 128), jnp.float32)
        acc = jnp.zeros((BLOCK, HEAD), jnp.float32)
        for j in range(0, NBLK, 2):
            parts = []
            for h in (j, j + 1):
                p = jnp.exp2((s_ref[:, h * 128 : (h + 1) * 128] - m) * COEF)
                total += p
                parts.append(p.astype(jnp.bfloat16))
            acc += nn(
                jnp.concatenate(parts, axis=1), v_ref[j : j + 2].reshape(2 * BLOCK, HEAD)
            )
        m_ref[i] = m
        l_ref[i] = total
        acc_ref[i] = acc
        return carry

    lax.fori_loop(0, NBLK, step, 0)


STAT = jax.ShapeDtypeStruct((NBLK, BLOCK, 128), jnp.float32)
HALF = jax.ShapeDtypeStruct((NBLK, BLOCK, HEAD), jnp.bfloat16)


def forward_local(q, k, v):
    return pl.pallas_call(
        forward_local_kernel,
        out_shape=(STAT, STAT, STAT),
        in_specs=[VMEM] * 3,
        out_specs=(VMEM,) * 3,
        scratch_shapes=[pltpu.VMEM((BLOCK, NBLK * BLOCK), jnp.float32)],
        compiler_params=params(),
        cost_estimate=cost(256, 2, 1, 5 * MIB),
        name="forward_local",
    )(q, k, v)


def forward_far_kernel(group, last, *refs):
    count = len(group)
    slots, bias, q_ref, mi_ref, li_ref, acci_ref = refs[:6]
    kv = refs[6 : 6 + count]
    rest = refs[6 + count :]
    if last:
        g_ref, out_ref, lse_ref, delta_ref, s_ref = rest
    else:
        m_ref, l_ref, acc_ref, s_ref = rest
    entries = entries_of(group)

    def step(i, carry):
        q = q_ref[i]
        tops = [None] * count
        for e in range(0, len(entries), 2):
            (na, ca), (nb, cb) = entries[e], entries[e + 1]
            keys = jnp.concatenate((kv[na][slots[i, ca], 0], kv[nb][slots[i, cb], 0]), axis=0)
            s = nt(q, keys)
            s_ref[:, e * 128 : (e + 2) * 128] = s
            for n, half in ((na, s[:, :128]), (nb, s[:, 128:])):
                tops[n] = half if tops[n] is None else jnp.maximum(tops[n], half)
        top = tops[0] - bias[group[0][0] * 2 + group[0][1]]
        for n in range(1, count):
            top = jnp.maximum(top, tops[n] - bias[group[n][0] * 2 + group[n][1]])
        before = mi_ref[i]
        m = jnp.maximum(before, lane_all(jnp.max(top, axis=1, keepdims=True)))
        keep = jnp.exp2((before - m) * COEF)
        total = li_ref[i] * keep
        acc = acci_ref[i] * keep
        offsets = [m + bias[band * 2 + side] for band, side, _, _, _ in group]
        for e in range(0, len(entries), 2):
            parts = []
            for h in (e, e + 1):
                p = jnp.exp2((s_ref[:, h * 128 : (h + 1) * 128] - offsets[entries[h][0]]) * COEF)
                total += p
                parts.append(p.astype(jnp.bfloat16))
            (na, ca), (nb, cb) = entries[e], entries[e + 1]
            vals = jnp.concatenate((kv[na][slots[i, ca], 1], kv[nb][slots[i, cb], 1]), axis=0)
            acc += nn(jnp.concatenate(parts, axis=1), vals)
        if last:
            full = lane_all(jnp.sum(total, axis=1, keepdims=True))
            out = (acc / full).astype(jnp.bfloat16)
            out_ref[i] = out
            lse_ref[i] = m * COEF + jnp.log2(full)
            delta = jnp.sum(
                g_ref[i].astype(jnp.float32) * out.astype(jnp.float32), axis=1, keepdims=True
            )
            delta_ref[i] = lane_all(delta)
        else:
            m_ref[i] = m
            l_ref[i] = total
            acc_ref[i] = acc
        return carry

    lax.fori_loop(0, NBLK, step, 0)


def forward_far(group, last, slots, bias, q, stats, kv, grad):
    entries = entries_of(group)
    extra = (grad,) if last else ()
    outs = (HALF, STAT, STAT) if last else (STAT, STAT, STAT)
    return pl.pallas_call(
        functools.partial(forward_far_kernel, group, last),
        out_shape=outs,
        in_specs=[SMEM, SMEM] + [VMEM] * (4 + len(kv) + len(extra)),
        out_specs=(VMEM,) * 3,
        scratch_shapes=[pltpu.VMEM((BLOCK, len(entries) * BLOCK), jnp.float32)],
        compiler_params=params(),
        cost_estimate=cost(16 * len(entries), 2, 1, 8 * MIB),
        name="forward_far",
    )(slots, bias, q, *stats, *kv, *extra)


def backward_pair(q, g, lse_a, lse_b, delta, keys, vals):
    s = nt(q, keys)
    dp = nt(g, vals)
    probs = []
    dss = []
    for h, lse in ((0, lse_a), (1, lse_b)):
        p = jnp.exp2(s[:, h * 128 : (h + 1) * 128] * COEF - lse)
        ds = p * (dp[:, h * 128 : (h + 1) * 128] - delta)
        probs.append(p.astype(jnp.bfloat16))
        dss.append(ds.astype(jnp.bfloat16))
    return jnp.concatenate(probs, axis=1), jnp.concatenate(dss, axis=1)


def backward_far_kernel(group, first, *refs):
    count = len(group)
    slots, bias, q_ref, g_ref, lse_ref, delta_ref = refs[:6]
    kv = refs[6 : 6 + count]
    rest = refs[6 + count :]
    if not first:
        dqi_ref, rest = rest[0], rest[1:]
    dq_ref, part, acc = rest[0], rest[1 : 1 + count], rest[1 + count :]
    entries = entries_of(group)
    for a in acc:
        a[...] = jnp.zeros_like(a)

    def step(i, carry):
        q = q_ref[i]
        g = g_ref[i]
        lse = lse_ref[i]
        delta = delta_ref[i]
        offsets = [lse + bias[band * 2 + side] for band, side, _, _, _ in group]
        dq = jnp.zeros((BLOCK, HEAD), jnp.float32) if first else dqi_ref[i]
        for e in range(0, len(entries), 2):
            (na, ca), (nb, cb) = entries[e], entries[e + 1]
            sa, sb = slots[i, ca], slots[i, cb]
            keys = jnp.concatenate((kv[na][sa, 0], kv[nb][sb, 0]), axis=0)
            vals = jnp.concatenate((kv[na][sa, 1], kv[nb][sb, 1]), axis=0)
            p, ds = backward_pair(q, g, offsets[na], offsets[nb], delta, keys, vals)
            dq += nn(ds, keys)
            dk = tn(ds, q)
            dv = tn(p, g)
            acc[na][sa, 0] += dk[:BLOCK]
            acc[na][sa, 1] += dv[:BLOCK]
            acc[nb][sb, 0] += dk[BLOCK:]
            acc[nb][sb, 1] += dv[BLOCK:]
        dq_ref[i] = dq
        return carry

    lax.fori_loop(0, NBLK, step, 0)
    for out, a in zip(part, acc):
        out[...] = a[...].astype(jnp.bfloat16)


def backward_far(group, slots, bias, q, g, lse, delta, kv, dq):
    entries = entries_of(group)
    extra = () if dq is None else (dq,)
    return pl.pallas_call(
        functools.partial(backward_far_kernel, group, dq is None),
        out_shape=(STAT,) + tuple(jax.ShapeDtypeStruct(x.shape, jnp.bfloat16) for x in kv),
        in_specs=[SMEM, SMEM] + [VMEM] * (4 + len(kv) + len(extra)),
        out_specs=(VMEM,) * (1 + len(kv)),
        scratch_shapes=[pltpu.VMEM(x.shape, jnp.float32) for x in kv],
        compiler_params=params(),
        cost_estimate=cost(16 * len(entries), 5, 1, 8 * MIB),
        name="backward_far",
    )(slots, bias, q, g, lse, delta, *kv, *extra)


def backward_local_kernel(
    q_ref, g_ref, lse_ref, delta_ref, k_ref, v_ref, dqi_ref, dq_ref, dk_ref, dv_ref
):
    dk_ref[...] = jnp.zeros_like(dk_ref)
    dv_ref[...] = jnp.zeros_like(dv_ref)

    def step(i, carry):
        q = q_ref[i]
        g = g_ref[i]
        lse = lse_ref[i]
        delta = delta_ref[i]
        dq = dqi_ref[i]
        for j in range(0, NBLK, 2):
            keys = k_ref[j : j + 2].reshape(2 * BLOCK, HEAD)
            vals = v_ref[j : j + 2].reshape(2 * BLOCK, HEAD)
            p, ds = backward_pair(q, g, lse, lse, delta, keys, vals)
            dq += nn(ds, keys)
            dk_ref[j : j + 2] += tn(ds, q).reshape(2, BLOCK, HEAD)
            dv_ref[j : j + 2] += tn(p, g).reshape(2, BLOCK, HEAD)
        dq_ref[i] = (dq * SCALE).astype(jnp.bfloat16)
        return carry

    lax.fori_loop(0, NBLK, step, 0)


def backward_local(q, g, lse, delta, k, v, dq):
    return pl.pallas_call(
        backward_local_kernel,
        out_shape=(HALF, STAT, STAT),
        in_specs=[VMEM] * 7,
        out_specs=(VMEM,) * 3,
        compiler_params=params(),
        cost_estimate=cost(256, 5, 1, 8 * MIB),
        name="backward_local",
    )(q, g, lse, delta, k, v, dq)


def finish_kernel(dk_ref, dv_ref, *refs):
    parts, (gk_ref, gv_ref) = refs[:-2], refs[-2:]
    for slot, block in enumerate(SLOT_BLOCK):
        dk = dk_ref[block]
        dv = dv_ref[block]
        for part in parts:
            if slot < part.shape[0]:
                dk += part[slot, 0].astype(jnp.float32)
                dv += part[slot, 1].astype(jnp.float32)
        gk_ref[block] = (dk * SCALE).astype(jnp.bfloat16)
        gv_ref[block] = dv.astype(jnp.bfloat16)


def finish(dk, dv, parts):
    return pl.pallas_call(
        finish_kernel,
        out_shape=(HALF, HALF),
        in_specs=[VMEM] * (2 + len(parts)),
        out_specs=(VMEM,) * 2,
        compiler_params=params(),
        name="finish",
    )(dk, dv, *parts)


def slot_of(block):
    return jnp.where(
        block % 2 == 1,
        8 + block // 2,
        jnp.where(
            block % 4 == 2, 4 + block // 4, jnp.where(block % 8 == 4, 2 + block // 8, block // 8)
        ),
    )


FORWARD_GROUPS = ((1, 3, 4), (2,))
BACKWARD_GROUPS = ((2,), (3, 4), (1,))


def local(queries, keys, values, grad_out, block_lists):
    shape = (NBLK, BLOCK, HEAD)
    q, k, v, g = (x.reshape(shape) for x in (queries, keys, values, grad_out))
    position = lax.axis_index("seq")
    devices = lax.axis_size("seq")
    slots = slot_of(block_lists)
    biases = [jnp.float32(0.0)] * 2
    for band, side, start, sel, by in PLAN:
        source = position - by
        valid = jnp.logical_and(source >= 0, source < devices)
        biases.append(jnp.where(valid, 0.0, BIG).astype(jnp.float32))
    bias = jnp.stack(biases)
    packed = pack(k, v)
    fetched = {}
    for entry in sorted(PLAN, key=lambda e: -e[0]):
        band, side, start, sel, by = entry
        fetched[band, side] = shift(packed[: NBLK >> (band - 1)], by)
    stats = forward_local(q, k, v)
    for n, bands in enumerate(FORWARD_GROUPS):
        group = [e for e in PLAN if e[0] in bands]
        last = n == len(FORWARD_GROUPS) - 1
        kv = [fetched[e[0], e[1]] for e in group]
        stats = forward_far(group, last, slots, bias, q, stats, kv, g)
    out, lse, delta = stats
    dq = None
    returned = []
    for bands in BACKWARD_GROUPS:
        group = [e for e in PLAN if e[0] in bands]
        kv = [fetched[e[0], e[1]] for e in group]
        dq, *parts = backward_far(group, slots, bias, q, g, lse, delta, kv, dq)
        for (band, side, start, sel, by), part in zip(group, parts):
            returned.append(shift(part, -by))
    dq, dk, dv = backward_local(q, g, lse, delta, k, v, dq)
    gk, gv = finish(dk, dv, returned)
    flat = (NBLK * BLOCK, HEAD)
    return tuple(x.reshape(flat) for x in (out, dq, gk, gv))


def solution(mesh):
    spec = P(("dp", "seq"), None)
    return jax.shard_map(
        local,
        mesh=mesh,
        in_specs=(spec,) * 5,
        out_specs=(spec,) * 4,
        check_vma=False,
    )
```

time: 1090 us -> 259 us (0.24)
  waiting for transfers between devices: 357 us -> 21.8 us
  other arithmetic: 226 us -> 0.02 us
  local copies, waits for them, and re-layouts: 223 us -> 11.9 us
  matrix products: 157 us -> 0 us
  Pallas kernels: 0 us -> 148 us
  loops' own time: 28.6 us -> 0 us
  starting transfers between devices: 92 us -> 72 us
    ppermute x16, waiting for transfers between devices: 357 us -> 21.8 us  [shift(): return lax.ppermute(value, 'seq', [(s, s + by) for s in range(first, last)])]
    dot_general x216 -> x0, matrix products: 157 us -> none  [the longest x32 27.2 us: one_step(): jnp.einsum('qrnc,qrd->qncd', weight, grad_now, preferred_element_type=jnp...]
    pallas_call x0 -> x9, Pallas kernels: none -> 148 us  [the longest x3 71.7 us: backward_far(): pl.pallas_call(functools.partial(backward_far_kernel, group, dq is None),...]
    scatter-add x32 -> x0, other arithmetic: 139 us -> none  [one_step(): new_parts.append(far_parts[slot - 1].at[:, rows.reshape(-1)].add(both))]
    gather x64 -> x0, local copies, waits for them, and re-layouts: 111 us -> none  [the longest x32 55.8 us: one_step(): fetched[0][rows]]
    squeeze x16 -> x0, local copies, waits for them, and re-layouts: 42.2 us -> none  [one_step(): fetched[1][rows]]
    another operation x27 -> x0, other arithmetic: 35.7 us -> none  [the longest x24 34.4 us: one_step(): both = jnp.stack((part_key, part_value)).reshape(2, -1, BLOCK, head)]
    while x672 -> x0, local copies, waits for them, and re-layouts: 32.5 us -> none
  transfers between devices with their start and end apart: 16 -> 16, of which waited for: 11 -> 3; matrix products, arithmetic and copies ran while one was open for 0% -> 2% of each run, Pallas kernels for 0% -> 24%
where the time goes in v1:
time: 259 us; the launch traced here: 254 us
  Pallas kernels  148 us (57%)
  starting transfers between devices  72 us (28%)
  waiting for transfers between devices  21.8 us (8%)
  local copies, waits for them, and re-layouts  11.9 us (5%)
    ppermute x16, starting transfers between devices, shift(): return lax.ppermute(value, 'seq', [(s, s + by) for s in range(first, last)])  72 us
    pallas_call x3, Pallas kernels, backward_far(): pl.pallas_call(functools.partial(backward_far_kernel, group, dq is None),...  71.7 us
    pallas_call x1, Pallas kernels, backward_local(): pl.pallas_call(backward_local_kernel, out_shape=(HALF, STAT, STAT), in_sp...  35.6 us
    pallas_call x2, Pallas kernels, forward_far(): pl.pallas_call(functools.partial(forward_far_kernel, group, last), out_sh...  25.9 us
    ppermute x16, waiting for transfers between devices, shift(): return lax.ppermute(value, 'seq', [(s, s + by) for s in range(first, last)])  21.8 us
    pallas_call x1, Pallas kernels, forward_local(): pl.pallas_call(forward_local_kernel, out_shape=(STAT, STAT, STAT), in_spe...  10.5 us
    unnamed x22, local copies, waits for them, and re-layouts  7.3 us
  transfers between devices with their start and end apart: 16, of which 3 were waited for; matrix products, arithmetic and copies ran while one was open for 2% of the time, Pallas kernels for 24%

profile of v1, /device:TPU:96, one launch (start us, length us, event | category | flops | bytes accessed | tf_op | source)
XLA Modules:
  0.0 254.3 jit_solution(350655969414425415)
XLA Ops:
  0.6 2.3 pack.1
  2.9 6.9 %collective-permute-start.1 = (bf16[16,2,128,128]{3,2,1,0:T(8,128)(2,1)}, bf16[16,2,128,128]{3,2,1,0:T(8,128)(2,1)}, u32[]{:S(2)}, u32[]{:S(2)}) collective-permute-start(bf16[16,2,128,128]{3,2,1,0:T(8,128)(2,1)} %pack.1), channel_id=1, source_target_pairs={{2,0},{4,2},{6,4},{8,6},{10,8},{12,10},{14,12},{16,14},{18,16},{20... | collective-permute-start | bytes 3145736 | tf_op jit(solution)/shard_map/ppermute | solution.py:54
  9.9 1.9 collective-permute-start
  11.8 0.0 copy-start.2
  11.8 1.7 slice.15
  13.5 2.7 %collective-permute-start.3 = (bf16[4,2,128,128]{3,2,1,0:T(8,128)(2,1)}, bf16[4,2,128,128]{3,2,1,0:T(8,128)(2,1)S(1)}, u32[]{:S(2)}, u32[]{:S(2)}) collective-permute-start(bf16[4,2,128,128]{3,2,1,0:T(8,128)(2,1)} %slice.15), channel_id=1, source_target_pairs={{8,0},{10,2},{12,4},{14,6},{16,8},{18,10},{20,12},{22,14},{24,16},... | collective-permute-start | bytes 786440 | tf_op jit(solution)/shard_map/ppermute | solution.py:54
  16.3 0.9 slice.16
  17.2 0.0 copy-start
  17.2 0.0 copy-start.1
  17.2 2.5 %collective-permute-start.5 = (bf16[2,2,128,128]{3,2,1,0:T(8,128)(2,1)S(1)}, bf16[2,2,128,128]{3,2,1,0:T(8,128)(2,1)S(1)}, u32[]{:S(2)}, u32[]{:S(2)}) collective-permute-start(bf16[2,2,128,128]{3,2,1,0:T(8,128)(2,1)S(1)} %slice.16), channel_id=1, source_target_pairs={{16,0},{18,2},{20,4},{22,6},{24,8},{26,10},{28,12},{30,14},{32,16}... | collective-permute-start | bytes 393224 | tf_op jit(solution)/shard_map/ppermute | solution.py:54
  19.8 4.9 %collective-permute-start.4 = (bf16[2,2,128,128]{3,2,1,0:T(8,128)(2,1)S(1)}, bf16[2,2,128,128]{3,2,1,0:T(8,128)(2,1)S(1)}, u32[]{:S(2)}, u32[]{:S(2)}) collective-permute-start(bf16[2,2,128,128]{3,2,1,0:T(8,128)(2,1)S(1)} %slice.16), channel_id=1, source_target_pairs={{0,16},{2,18},{4,20},{6,22},{8,24},{10,26},{12,28},{14,30},{16,32}... | collective-permute-start | bytes 393224 | tf_op jit(solution)/shard_map/ppermute | solution.py:54
  24.7 1.9 slice.17
  26.6 0.0 collective-permute-done.5.refs_11_.refs_9_
  26.6 18.5 %collective-permute-start.2 = (bf16[4,2,128,128]{3,2,1,0:T(8,128)(2,1)}, bf16[4,2,128,128]{3,2,1,0:T(8,128)(2,1)S(1)}, u32[]{:S(2)}, u32[]{:S(2)}) collective-permute-start(bf16[4,2,128,128]{3,2,1,0:T(8,128)(2,1)} %slice.15), channel_id=1, source_target_pairs={{0,8},{2,10},{4,12},{6,14},{8,16},{10,18},{12,20},{14,22},{16,24},... | collective-permute-start | bytes 786440 | tf_op jit(solution)/shard_map/ppermute | solution.py:54
  45.1 0.0 collective-permute-done.4.refs_10_.refs_8_
  45.1 1.9 collective-permute-start.7
  47.0 3.5 %collective-permute-done.3.refs_9_.refs_7_ = bf16[4,2,128,128]{3,2,1,0:T(8,128)(2,1)S(1)} collective-permute-done((bf16[4,2,128,128]{3,2,1,0:T(8,128)(2,1)}, bf16[4,2,128,128]{3,2,1,0:T(8,128)(2,1)S(1)}, u32[]{:S(2)}, u32[]{:S(2)}) %collective-permute-start.3) | collective-permute-done | bytes 262176 | tf_op jit(solution)/shard_map/ppermute | solution.py:54
  50.6 1.9 collective-permute-start.6
  52.5 0.0 copy-done.2
  52.5 0.0 copy-done
  52.5 0.0 copy-done.1
  52.5 10.5 %forward_local.1 = (f32[16,128,128]{2,1,0:T(8,128)S(1)}, f32[16,128,128]{2,1,0:T(8,128)S(1)}, f32[16,128,128]{2,1,0:T(8,128)S(1)}) custom-call(bf16[16,128,128]{2,1,0:T(8,128)(2,1)S(1)} %bitcast.22, bf16[16,128,128]{2,1,0:T(8,128)(2,1)S(1)} %bitcast.17, bf16[16,128,128]{2,1,0:T(8,128)(2,1)S(1)} %bitcast.20), custom_call_target="tpu_custom_call" | custom-call | flops 2147483648 | bytes 5242880 | tf_op jit(solution)/shard_map/forward_local/pallas_call | solution.py:139
  63.0 0.0 copy-start.4
  63.0 1.0 copy-done.4
  64.0 0.0 copy-start.6
  64.0 1.0 copy-done.6
  65.0 0.0 copy-start.8
  65.0 1.0 copy-done.8
  66.0 0.0 copy-start.10
  66.0 0.1 stack.35.refs_1_
  66.1 0.6 copy-done.10
  66.8 0.0 collective-permute-done.2.refs_8_.refs_6_
  66.8 0.0 collective-permute-done.1.refs_7_
  66.8 0.0 collective-permute-done.refs_6_
  66.8 0.0 copy-start.5
  66.8 1.2 copy-done.5
  68.0 1.2 copy-done.7
  69.2 1.2 copy-done.9
  70.5 14.8 %forward_far.2 = (f32[16,128,128]{2,1,0:T(8,128)S(1)}, f32[16,128,128]{2,1,0:T(8,128)S(1)}, f32[16,128,128]{2,1,0:T(8,128)S(1)}) custom-call(s32[16,30]{1,0:T(8,128)S(1)} %fusion.2.refs_0_, f32[10]{0:T(128)S(1)} %stack.35.refs_1_, bf16[16,128,128]{2,1,0:T(8,128)(2,1)S(1)} %bitcast.23, f32[16,128,128]{2,1,0:T(8,128)S(1)} %copy-done.5, ...), custom_call_target="tpu_custom_call" | custom-call | flops 2952790016 | bytes 8388608 | tf_op jit(solution)/shard_map/forward_far/pallas_call | solution.py:212
  85.2 0.0 collective-permute-done.7.refs_7_
  85.2 0.0 collective-permute-done.6.refs_6_
  85.3 0.0 copy-done.3
  85.3 11.2 %forward_far.3 = (bf16[16,128,128]{2,1,0:T(8,128)(2,1)}, f32[16,128,128]{2,1,0:T(8,128)S(1)}, f32[16,128,128]{2,1,0:T(8,128)S(1)}) custom-call(s32[16,30]{1,0:T(8,128)S(1)} %fusion.2.refs_0_, f32[10]{0:T(128)S(1)} %stack.35.refs_1_, bf16[16,128,128]{2,1,0:T(8,128)(2,1)S(1)} %bitcast.24, f32[16,128,128]{2,1,0:T(8,128)S(1)} %get-tuple-element.32.refs_3_, ...), custom_call_target="tpu_custom_call" | custom-call | flops 1073741824 | bytes 8388608 | tf_op jit(solution)/shard_map/forward_far/pallas_call | solution.py:212
  96.4 19.5 %backward_far.3 = (f32[16,128,128]{2,1,0:T(8,128)S(1)}, bf16[8,2,128,128]{3,2,1,0:T(8,128)(2,1)S(1)}, bf16[8,2,128,128]{3,2,1,0:T(8,128)(2,1)S(1)}) custom-call(s32[16,30]{1,0:T(8,128)S(1)} %fusion.2.refs_0_, f32[10]{0:T(128)S(1)} %stack.35.refs_1_, bf16[16,128,128]{2,1,0:T(8,128)(2,1)S(1)} %bitcast.25, bf16[16,128,128]{2,1,0:T(8,128)(2,1)S(1)} %bitcast.30, ...), custom_call_target="tpu_custom_call" | custom-call | flops 2684354560 | bytes 8388608 | tf_op jit(solution)/shard_map/backward_far/pallas_call | solution.py:280
  115.9 15.4 %backward_far.4 = (f32[16,128,128]{2,1,0:T(8,128)S(1)}, bf16[4,2,128,128]{3,2,1,0:T(8,128)(2,1)S(1)}, bf16[4,2,128,128]{3,2,1,0:T(8,128)(2,1)S(1)}, bf16[2,2,128...) custom-call(s32[16,30]{1,0:T(8,128)S(1)} %fusion.2.refs_0_, f32[10]{0:T(128)S(1)} %stack.35.refs_1_, ...), custom_call_target="tpu_custom_call" | custom-call | flops 2013265920 | bytes 8388608 | tf_op jit(solution)/shard_map/backward_far/pallas_call | solution.py:280
  131.3 36.8 %backward_far.5 = (f32[16,128,128]{2,1,0:T(8,128)S(1)}, bf16[16,2,128,128]{3,2,1,0:T(8,128)(2,1)S(1)}, bf16[16,2,128,128]{3,2,1,0:T(8,128)(2,1)S(1)}) custom-call(s32[16,30]{1,0:T(8,128)S(1)} %fusion.2.refs_0_, f32[10]{0:T(128)S(1)} %stack.35.refs_1_, bf16[16,128,128]{2,1,0:T(8,128)(2,1)S(1)} %bitcast.27, bf16[16,128,128]{2,1,0:T(8,128)(2,1)S(1)} %bitcast.32, ...), custom_call_target="tpu_custom_call" | custom-call | flops 5368709120 | bytes 8388608 | tf_op jit(solution)/shard_map/backward_far/pallas_call | solution.py:280
  168.1 7.8 %collective-permute-start.14 = (bf16[16,2,128,128]{3,2,1,0:T(8,128)(2,1)S(1)}, bf16[16,2,128,128]{3,2,1,0:T(8,128)(2,1)S(1)}, u32[]{:S(2)}, u32[]{:S(2)}) collective-permute-start(bf16[16,2,128,128]{3,2,1,0:T(8,128)(2,1)S(1)} %get-tuple-element.50), channel_id=1, source_target_pairs={{2,0},{4,2},{6,4},{8,6},{10,8},{12,10},{14,12},{16,14},{18,16},{20... | collective-permute-start | bytes 3145736 | tf_op jit(solution)/shard_map/ppermute | solution.py:54
  175.9 1.9 collective-permute-start.15
  177.9 2.5 collective-permute-start.10
  180.4 1.9 collective-permute-start.12
  182.3 5.4 %collective-permute-start.13 = (bf16[2,2,128,128]{3,2,1,0:T(8,128)(2,1)S(1)}, bf16[2,2,128,128]{3,2,1,0:T(8,128)(2,1)S(1)}, u32[]{:S(2)}, u32[]{:S(2)}) collective-permute-start(bf16[2,2,128,128]{3,2,1,0:T(8,128)(2,1)S(1)} %get-tuple-element.49), channel_id=1, source_target_pairs={{0,16},{2,18},{4,20},{6,22},{8,24},{10,26},{12,28},{14,30},{16,32}... | collective-permute-start | bytes 393224 | tf_op jit(solution)/shard_map/ppermute | solution.py:54
  187.8 1.0 collective-permute-done.12.refs_4_
  188.8 7.2 %collective-permute-start.8 = (bf16[8,2,128,128]{3,2,1,0:T(8,128)(2,1)S(1)}, bf16[8,2,128,128]{3,2,1,0:T(8,128)(2,1)S(1)}, u32[]{:S(2)}, u32[]{:S(2)}) collective-permute-start(bf16[8,2,128,128]{3,2,1,0:T(8,128)(2,1)S(1)} %get-tuple-element.44), channel_id=1, source_target_pairs={{4,0},{6,2},{8,4},{10,6},{12,8},{14,10},{16,12},{18,14},{20,16},{2... | collective-permute-start | bytes 1572872 | tf_op jit(solution)/shard_map/ppermute | solution.py:54
  196.0 0.0 collective-permute-done.13.refs_5_
  196.0 1.9 collective-permute-start.9
  197.9 17.2 %collective-permute-done.10.refs_2_ = bf16[4,2,128,128]{3,2,1,0:T(8,128)(2,1)S(1)} collective-permute-done((bf16[4,2,128,128]{3,2,1,0:T(8,128)(2,1)S(1)}, bf16[4,2,128,128]{3,2,1,0:T(8,128)(2,1)S(1)}, u32[]{:S(2)}, u32[]{:S(2)}) %collective-permute-start.10) | collective-permute-done | bytes 262176 | tf_op jit(solution)/shard_map/ppermute | solution.py:54
  215.2 1.9 collective-permute-start.11
  217.1 35.6 %backward_local.1 = (bf16[16,128,128]{2,1,0:T(8,128)(2,1)}, f32[16,128,128]{2,1,0:T(8,128)S(1)}, f32[16,128,128]{2,1,0:T(8,128)S(1)}) custom-call(bf16[16,128,128]{2,1,0:T(8,128)(2,1)S(1)} %bitcast.28, bf16[16,128,128]{2,1,0:T(8,128)(2,1)S(1)} %bitcast.33, f32[16,128,128]{2,1,0:T(8,128)S(1)} %get-tuple-element.36.refs_4_.lse_ref, ...), custom_call_target="tpu_custom_call" | custom-call | flops 5368709120 | bytes 8388608 | tf_op jit(solution)/shard_map/backward_local/pallas_call | solution.py:318
  252.7 0.0 collective-permute-done.11.refs_3_
  252.7 0.0 collective-permute-done.8.refs_0_
  252.7 0.0 collective-permute-done.9.refs_1_
  252.7 0.0 collective-permute-done.14.refs_6_
  252.7 0.0 collective-permute-done.15.refs_7_
  252.7 1.5 finish.1
  (5 shorter events, 0.0 us)
Async XLA Ops:
  2.9 63.9 %collective-permute-start.1 = (bf16[16,2,128,128]{3,2,1,0:T(8,128)(2,1)}, bf16[16,2,128,128]{3,2,1,0:T(8,128)(2,1)}, u32[]{:S(2)}, u32[]{:S(2)}) collective-permute-start(bf16[16,2,128,128]{3,2,1,0:T(8,128)(2,1)} %pack.1), channel_id=1, source_target_pairs={{2,0},{4,2},{6,4},{8,6},{10,8},{12,10},{14,12},{16,14},{18,16},{20... | collective-permute-start | bytes 3145736 | tf_op jit(solution)/shard_map/ppermute | solution.py:54
  9.9 56.9 %collective-permute-start = (bf16[16,2,128,128]{3,2,1,0:T(8,128)(2,1)}, bf16[16,2,128,128]{3,2,1,0:T(8,128)(2,1)}, u32[]{:S(2)}, u32[]{:S(2)}) collective-permute-start(bf16[16,2,128,128]{3,2,1,0:T(8,128)(2,1)} %pack.1), channel_id=1, source_target_pairs={{0,2},{2,4},{4,6},{6,8},{8,10},{10,12},{12,14},{14,16},{16,18},{18... | collective-permute-start | bytes 3145736 | tf_op jit(solution)/shard_map/ppermute | solution.py:54
  11.8 40.7 %copy-start.2 = (bf16[2048,128]{1,0:T(8,128)(2,1)S(1)}, bf16[2048,128]{1,0:T(8,128)(2,1)}, u32[]{:S(2)}) copy-start(bf16[2048,128]{1,0:T(8,128)(2,1)} %param.5) | copy-start | bytes 1572868
  13.5 37.0 %collective-permute-start.3 = (bf16[4,2,128,128]{3,2,1,0:T(8,128)(2,1)}, bf16[4,2,128,128]{3,2,1,0:T(8,128)(2,1)S(1)}, u32[]{:S(2)}, u32[]{:S(2)}) collective-permute-start(bf16[4,2,128,128]{3,2,1,0:T(8,128)(2,1)} %slice.15), channel_id=1, source_target_pairs={{8,0},{10,2},{12,4},{14,6},{16,8},{18,10},{20,12},{22,14},{24,16},... | collective-permute-start | bytes 786440 | tf_op jit(solution)/shard_map/ppermute | solution.py:54
  17.2 35.3 %copy-start = (bf16[2048,128]{1,0:T(8,128)(2,1)S(1)}, bf16[2048,128]{1,0:T(8,128)(2,1)}, u32[]{:S(2)}) copy-start(bf16[2048,128]{1,0:T(8,128)(2,1)} %param.6) | copy-start | bytes 1572868
  17.2 35.3 %copy-start.1 = (bf16[2048,128]{1,0:T(8,128)(2,1)S(1)}, bf16[2048,128]{1,0:T(8,128)(2,1)}, u32[]{:S(2)}) copy-start(bf16[2048,128]{1,0:T(8,128)(2,1)} %param.7) | copy-start | bytes 1572868
  17.2 9.4 %collective-permute-start.5 = (bf16[2,2,128,128]{3,2,1,0:T(8,128)(2,1)S(1)}, bf16[2,2,128,128]{3,2,1,0:T(8,128)(2,1)S(1)}, u32[]{:S(2)}, u32[]{:S(2)}) collective-permute-start(bf16[2,2,128,128]{3,2,1,0:T(8,128)(2,1)S(1)} %slice.16), channel_id=1, source_target_pairs={{16,0},{18,2},{20,4},{22,6},{24,8},{26,10},{28,12},{30,14},{32,16}... | collective-permute-start | bytes 393224 | tf_op jit(solution)/shard_map/ppermute | solution.py:54
  19.8 25.3 %collective-permute-start.4 = (bf16[2,2,128,128]{3,2,1,0:T(8,128)(2,1)S(1)}, bf16[2,2,128,128]{3,2,1,0:T(8,128)(2,1)S(1)}, u32[]{:S(2)}, u32[]{:S(2)}) collective-permute-start(bf16[2,2,128,128]{3,2,1,0:T(8,128)(2,1)S(1)} %slice.16), channel_id=1, source_target_pairs={{0,16},{2,18},{4,20},{6,22},{8,24},{10,26},{12,28},{14,30},{16,32}... | collective-permute-start | bytes 393224 | tf_op jit(solution)/shard_map/ppermute | solution.py:54
  26.6 40.2 %collective-permute-start.2 = (bf16[4,2,128,128]{3,2,1,0:T(8,128)(2,1)}, bf16[4,2,128,128]{3,2,1,0:T(8,128)(2,1)S(1)}, u32[]{:S(2)}, u32[]{:S(2)}) collective-permute-start(bf16[4,2,128,128]{3,2,1,0:T(8,128)(2,1)} %slice.15), channel_id=1, source_target_pairs={{0,8},{2,10},{4,12},{6,14},{8,16},{10,18},{12,20},{14,22},{16,24},... | collective-permute-start | bytes 786440 | tf_op jit(solution)/shard_map/ppermute | solution.py:54
  45.1 40.1 %collective-permute-start.7 = (bf16[8,2,128,128]{3,2,1,0:T(8,128)(2,1)}, bf16[8,2,128,128]{3,2,1,0:T(8,128)(2,1)S(1)}, u32[]{:S(2)}, u32[]{:S(2)}) collective-permute-start(bf16[8,2,128,128]{3,2,1,0:T(8,128)(2,1)} %slice.17), channel_id=1, source_target_pairs={{4,0},{6,2},{8,4},{10,6},{12,8},{14,10},{16,12},{18,14},{20,16},{2... | collective-permute-start | bytes 1572872 | tf_op jit(solution)/shard_map/ppermute | solution.py:54
  50.6 34.7 %collective-permute-start.6 = (bf16[8,2,128,128]{3,2,1,0:T(8,128)(2,1)}, bf16[8,2,128,128]{3,2,1,0:T(8,128)(2,1)S(1)}, u32[]{:S(2)}, u32[]{:S(2)}) collective-permute-start(bf16[8,2,128,128]{3,2,1,0:T(8,128)(2,1)} %slice.17), channel_id=1, source_target_pairs={{0,4},{2,6},{4,8},{6,10},{8,12},{10,14},{12,16},{14,18},{16,20},{1... | collective-permute-start | bytes 1572872 | tf_op jit(solution)/shard_map/ppermute | solution.py:54
  63.0 1.0 copy-start.4
  64.0 1.0 copy-start.6
  65.0 1.0 copy-start.8
  66.0 0.7 copy-start.10
  66.8 1.2 copy-start.5
  68.0 1.2 copy-start.7
  69.2 1.2 copy-start.9
  70.5 14.8 %copy-start.3 = (bf16[2048,128]{1,0:T(8,128)(2,1)S(1)}, bf16[2048,128]{1,0:T(8,128)(2,1)}, u32[]{:S(2)}) copy-start(bf16[2048,128]{1,0:T(8,128)(2,1)} %param.8) | copy-start | bytes 1572868
  168.1 84.6 %collective-permute-start.14 = (bf16[16,2,128,128]{3,2,1,0:T(8,128)(2,1)S(1)}, bf16[16,2,128,128]{3,2,1,0:T(8,128)(2,1)S(1)}, u32[]{:S(2)}, u32[]{:S(2)}) collective-permute-start(bf16[16,2,128,128]{3,2,1,0:T(8,128)(2,1)S(1)} %get-tuple-element.50), channel_id=1, source_target_pairs={{2,0},{4,2},{6,4},{8,6},{10,8},{12,10},{14,12},{16,14},{18,16},{20... | collective-permute-start | bytes 3145736 | tf_op jit(solution)/shard_map/ppermute | solution.py:54
  175.9 76.8 %collective-permute-start.15 = (bf16[16,2,128,128]{3,2,1,0:T(8,128)(2,1)S(1)}, bf16[16,2,128,128]{3,2,1,0:T(8,128)(2,1)S(1)}, u32[]{:S(2)}, u32[]{:S(2)}) collective-permute-start(bf16[16,2,128,128]{3,2,1,0:T(8,128)(2,1)S(1)} %get-tuple-element.51), channel_id=1, source_target_pairs={{0,2},{2,4},{4,6},{6,8},{8,10},{10,12},{12,14},{14,16},{16,18},{18... | collective-permute-start | bytes 3145736 | tf_op jit(solution)/shard_map/ppermute | solution.py:54
  177.9 37.3 %collective-permute-start.10 = (bf16[4,2,128,128]{3,2,1,0:T(8,128)(2,1)S(1)}, bf16[4,2,128,128]{3,2,1,0:T(8,128)(2,1)S(1)}, u32[]{:S(2)}, u32[]{:S(2)}) collective-permute-start(bf16[4,2,128,128]{3,2,1,0:T(8,128)(2,1)S(1)} %get-tuple-element.46), channel_id=1, source_target_pairs={{8,0},{10,2},{12,4},{14,6},{16,8},{18,10},{20,12},{22,14},{24,16},... | collective-permute-start | bytes 786440 | tf_op jit(solution)/shard_map/ppermute | solution.py:54
  180.4 8.4 %collective-permute-start.12 = (bf16[2,2,128,128]{3,2,1,0:T(8,128)(2,1)S(1)}, bf16[2,2,128,128]{3,2,1,0:T(8,128)(2,1)S(1)}, u32[]{:S(2)}, u32[]{:S(2)}) collective-permute-start(bf16[2,2,128,128]{3,2,1,0:T(8,128)(2,1)S(1)} %get-tuple-element.48), channel_id=1, source_target_pairs={{16,0},{18,2},{20,4},{22,6},{24,8},{26,10},{28,12},{30,14},{32,16}... | collective-permute-start | bytes 393224 | tf_op jit(solution)/shard_map/ppermute | solution.py:54
  182.3 13.7 %collective-permute-start.13 = (bf16[2,2,128,128]{3,2,1,0:T(8,128)(2,1)S(1)}, bf16[2,2,128,128]{3,2,1,0:T(8,128)(2,1)S(1)}, u32[]{:S(2)}, u32[]{:S(2)}) collective-permute-start(bf16[2,2,128,128]{3,2,1,0:T(8,128)(2,1)S(1)} %get-tuple-element.49), channel_id=1, source_target_pairs={{0,16},{2,18},{4,20},{6,22},{8,24},{10,26},{12,28},{14,30},{16,32}... | collective-permute-start | bytes 393224 | tf_op jit(solution)/shard_map/ppermute | solution.py:54
  188.8 63.9 %collective-permute-start.8 = (bf16[8,2,128,128]{3,2,1,0:T(8,128)(2,1)S(1)}, bf16[8,2,128,128]{3,2,1,0:T(8,128)(2,1)S(1)}, u32[]{:S(2)}, u32[]{:S(2)}) collective-permute-start(bf16[8,2,128,128]{3,2,1,0:T(8,128)(2,1)S(1)} %get-tuple-element.44), channel_id=1, source_target_pairs={{4,0},{6,2},{8,4},{10,6},{12,8},{14,10},{16,12},{18,14},{20,16},{2... | collective-permute-start | bytes 1572872 | tf_op jit(solution)/shard_map/ppermute | solution.py:54
  196.0 56.7 %collective-permute-start.9 = (bf16[8,2,128,128]{3,2,1,0:T(8,128)(2,1)S(1)}, bf16[8,2,128,128]{3,2,1,0:T(8,128)(2,1)S(1)}, u32[]{:S(2)}, u32[]{:S(2)}) collective-permute-start(bf16[8,2,128,128]{3,2,1,0:T(8,128)(2,1)S(1)} %get-tuple-element.45), channel_id=1, source_target_pairs={{0,4},{2,6},{4,8},{6,10},{8,12},{10,14},{12,16},{14,18},{16,20},{1... | collective-permute-start | bytes 1572872 | tf_op jit(solution)/shard_map/ppermute | solution.py:54
  215.2 37.5 %collective-permute-start.11 = (bf16[4,2,128,128]{3,2,1,0:T(8,128)(2,1)S(1)}, bf16[4,2,128,128]{3,2,1,0:T(8,128)(2,1)S(1)}, u32[]{:S(2)}, u32[]{:S(2)}) collective-permute-start(bf16[4,2,128,128]{3,2,1,0:T(8,128)(2,1)S(1)} %get-tuple-element.47), channel_id=1, source_target_pairs={{0,8},{2,10},{4,12},{6,14},{8,16},{10,18},{12,20},{14,22},{16,24},... | collective-permute-start | bytes 786440 | tf_op jit(solution)/shard_map/ppermute | solution.py:54

commit v2 on v1

v2 whole, which is shorter than its diff:
```python
import functools
import math

import jax
import jax.numpy as jnp
from jax import lax
from jax.experimental import pallas as pl
from jax.experimental.pallas import tpu as pltpu
from jax.sharding import PartitionSpec as P

BLOCK = 128
HEAD = 128
NBLK = 16
FAR = 4
SCALE = 1.0 / math.sqrt(HEAD)
LOG2E = 1.4426950408889634
COEF = SCALE * LOG2E
BIG = 1e30
MIB = 2**20

SLOT_BLOCK = [0, 8, 4, 12, 2, 6, 10, 14, 1, 3, 5, 7, 9, 11, 13, 15]


def band_columns():
    plan = []
    start = 0
    for band in range(1, FAR + 1):
        stride = 2 ** (band - 1)
        sel = NBLK >> band
        for side, sign in enumerate((1, -1)):
            plan.append((band, side, start, sel, sign * stride))
            start += sel
    return plan


PLAN = band_columns()


def nt(a, b):
    return lax.dot_general(a, b, (((1,), (1,)), ((), ())), preferred_element_type=jnp.float32)


def nn(a, b):
    return lax.dot_general(a, b, (((1,), (0,)), ((), ())), preferred_element_type=jnp.float32)


def tn(a, b):
    return lax.dot_general(a, b, (((0,), (0,)), ((), ())), preferred_element_type=jnp.float32)


def shift(value, by):
    count = lax.axis_size("seq")
    first, last = max(0, -by), min(count, count - by)
    return lax.ppermute(value, "seq", [(s, s + by) for s in range(first, last)])


def params(limit=16):
    return pltpu.CompilerParams(vmem_limit_bytes=limit * MIB)


VMEM = pl.BlockSpec(memory_space=pltpu.VMEM)
SMEM = pl.BlockSpec(memory_space=pltpu.SMEM)


def cost(pairs, products, exps, moved):
    return pl.CostEstimate(
        flops=2 * pairs * products * BLOCK * BLOCK * HEAD,
        transcendentals=exps * pairs * BLOCK * BLOCK,
        bytes_accessed=moved,
    )


def slot_of(own):
    return jnp.where(
        (own & 1) == 1,
        8 + (own >> 1),
        jnp.where(
            (own & 3) == 2, 4 + (own >> 2), jnp.where((own & 7) == 4, 2 + (own >> 3), own >> 3)
        ),
    )


def pack_kernel(k_ref, v_ref, lists_ref, slots_ref, *outs):
    slots_ref[...] = slot_of(lists_ref[...])
    for slot, own in enumerate(SLOT_BLOCK):
        for out in outs:
            if slot < out.shape[0]:
                out[slot, 0] = k_ref[own]
                out[slot, 1] = v_ref[own]


def pack(key_blocks, value_blocks, lists, *sizes):
    return pl.pallas_call(
        pack_kernel,
        out_shape=(jax.ShapeDtypeStruct(lists.shape, jnp.int32),)
        + tuple(jax.ShapeDtypeStruct((n, 2, BLOCK, HEAD), jnp.bfloat16) for n in sizes),
        in_specs=[VMEM] * 3,
        out_specs=(VMEM,) * (1 + len(sizes)),
        compiler_params=params(),
        name="pack",
    )(key_blocks, value_blocks, lists)


def hand_on_kernel(a_ref, b_ref, out_a_ref, out_b_ref):
    out_a_ref[...] = a_ref[: NBLK // 2]
    out_b_ref[...] = b_ref[: NBLK // 2]


def hand_on(a, b):
    half = jax.ShapeDtypeStruct((NBLK // 2, 2, BLOCK, HEAD), jnp.bfloat16)
    return pl.pallas_call(
        hand_on_kernel,
        out_shape=(half, half),
        in_specs=[VMEM] * 2,
        out_specs=(VMEM,) * 2,
        compiler_params=params(),
        name="hand_on",
    )(a, b)


def merge_kernel(*refs):
    count = len(refs) // 3
    for base, more, out in zip(refs[:count], refs[count : 2 * count], refs[2 * count :]):
        half = more.shape[0]
        total = base[:half].astype(jnp.float32) + more[...].astype(jnp.float32)
        out[:half] = total.astype(jnp.bfloat16)
        out[half:] = base[half:]


def merge(bases, mores):
    return pl.pallas_call(
        merge_kernel,
        out_shape=tuple(jax.ShapeDtypeStruct(x.shape, x.dtype) for x in bases),
        in_specs=[VMEM] * (2 * len(bases)),
        out_specs=(VMEM,) * len(bases),
        compiler_params=params(),
        name="merge",
    )(*bases, *mores)


def lane_all(x):
    return jnp.broadcast_to(x, (x.shape[0], 128))


def entries_of(group):
    return [
        (n, start + c) for n, (band, side, start, sel, by) in enumerate(group) for c in range(sel)
    ]


def gather(kv, entries, slots, i, which):
    return jnp.concatenate([kv[n][slots[i, c], which] for n, c in entries], axis=0)


def block(e):
    return slice(e * BLOCK, (e + 1) * BLOCK)


def bias_of(bias, entry):
    return bias[entry[0] * 2 + entry[1]]


STAT = jax.ShapeDtypeStruct((NBLK, BLOCK, 128), jnp.float32)
HALF = jax.ShapeDtypeStruct((NBLK, BLOCK, HEAD), jnp.bfloat16)
UNROLL = 4


def staggered(stages, copies=UNROLL):
    for tick in range(copies + len(stages) - 1):
        for n, stage in enumerate(stages):
            if 0 <= tick - n < copies:
                stage(tick - n)


def forward_local_kernel(q_ref, k_ref, v_ref, m_ref, l_ref, acc_ref, *scratch):
    width = NBLK * BLOCK

    def step(t, carry):
        def scores(u):
            scratch[2 * u][...] = nt(q_ref[t * UNROLL + u], k_ref[...].reshape(width, HEAD))

        def weights(u):
            s_ref, p_ref = scratch[2 * u : 2 * u + 2]
            top = s_ref[:, block(0)]
            for e in range(1, NBLK):
                top = jnp.maximum(top, s_ref[:, block(e)])
            m = lane_all(jnp.max(top, axis=1, keepdims=True))
            m_ref[t * UNROLL + u] = m
            total = jnp.zeros((BLOCK, 128), jnp.float32)
            for e in range(NBLK):
                p = jnp.exp2((s_ref[:, block(e)] - m) * COEF)
                total += p
                p_ref[:, block(e)] = p.astype(jnp.bfloat16)
            l_ref[t * UNROLL + u] = total

        def sums(u):
            acc_ref[t * UNROLL + u] = nn(scratch[2 * u + 1][...], v_ref[...].reshape(width, HEAD))

        staggered((scores, weights, sums))
        return carry

    lax.fori_loop(0, NBLK // UNROLL, step, 0)


def forward_scratch(width):
    return [
        pltpu.VMEM((BLOCK, width), jnp.float32),
        pltpu.VMEM((BLOCK, width), jnp.bfloat16),
    ] * UNROLL


def forward_local(q, k, v):
    return pl.pallas_call(
        forward_local_kernel,
        out_shape=(STAT, STAT, STAT),
        in_specs=[VMEM] * 3,
        out_specs=(VMEM,) * 3,
        scratch_shapes=forward_scratch(NBLK * BLOCK),
        compiler_params=params(),
        cost_estimate=cost(256, 2, 1, 5 * MIB),
        name="forward_local",
    )(q, k, v)


def forward_far_kernel(group, last, *refs):
    count = len(group)
    slots, bias, q_ref, mi_ref, li_ref, acci_ref = refs[:6]
    kv = refs[6 : 6 + count]
    rest = refs[6 + count :]
    if last:
        g_ref, out_ref, lse_ref, delta_ref = rest[:4]
        scratch = rest[4:]
    else:
        m_ref, l_ref, acc_ref = rest[:3]
        scratch = rest[3:]
    entries = entries_of(group)

    def step(t, carry):
        highs = [None] * UNROLL
        totals = [None] * UNROLL

        def scores(u):
            i = t * UNROLL + u
            scratch[2 * u][...] = nt(q_ref[i], gather(kv, entries, slots, i, 0))

        def weights(u):
            i = t * UNROLL + u
            s_ref, p_ref = scratch[2 * u : 2 * u + 2]
            top = None
            for n in range(count):
                own = [e for e in range(len(entries)) if entries[e][0] == n]
                part = s_ref[:, block(own[0])]
                for e in own[1:]:
                    part = jnp.maximum(part, s_ref[:, block(e)])
                part = part - bias_of(bias, group[n])
                top = part if top is None else jnp.maximum(top, part)
            m = jnp.maximum(mi_ref[i], lane_all(jnp.max(top, axis=1, keepdims=True)))
            total = li_ref[i] * jnp.exp2((mi_ref[i] - m) * COEF)
            offsets = [m + bias_of(bias, entry) for entry in group]
            for e, (n, c) in enumerate(entries):
                p = jnp.exp2((s_ref[:, block(e)] - offsets[n]) * COEF)
                total += p
                p_ref[:, block(e)] = p.astype(jnp.bfloat16)
            highs[u] = m
            totals[u] = total

        def sums(u):
            i = t * UNROLL + u
            m = highs[u]
            acc = acci_ref[i] * jnp.exp2((mi_ref[i] - m) * COEF)
            acc += nn(scratch[2 * u + 1][...], gather(kv, entries, slots, i, 1))
            if last:
                full = lane_all(jnp.sum(totals[u], axis=1, keepdims=True))
                out = (acc / full).astype(jnp.bfloat16)
                out_ref[i] = out
                lse_ref[i] = m * COEF + jnp.log2(full)
                delta = jnp.sum(
                    g_ref[i].astype(jnp.float32) * out.astype(jnp.float32), axis=1, keepdims=True
                )
                delta_ref[i] = lane_all(delta)
            else:
                m_ref[i] = m
                l_ref[i] = totals[u]
                acc_ref[i] = acc

        staggered((scores, weights, sums))
        return carry

    lax.fori_loop(0, NBLK // UNROLL, step, 0)


def forward_far(group, last, slots, bias, q, stats, kv, grad):
    entries = entries_of(group)
    extra = (grad,) if last else ()
    return pl.pallas_call(
        functools.partial(forward_far_kernel, group, last),
        out_shape=(HALF, STAT, STAT) if last else (STAT, STAT, STAT),
        in_specs=[SMEM, SMEM] + [VMEM] * (4 + len(kv) + len(extra)),
        out_specs=(VMEM,) * 3,
        scratch_shapes=forward_scratch(len(entries) * BLOCK),
        compiler_params=params(),
        cost_estimate=cost(16 * len(entries), 2, 1, 8 * MIB),
        name="forward_far",
    )(slots, bias, q, *stats, *kv, *extra)


def backward_scratch(rows, width, copies):
    return [
        pltpu.VMEM((rows, width), jnp.bfloat16),
        pltpu.VMEM((rows, width), jnp.bfloat16),
    ] * copies


CHUNK = 2
TIE = (4,)


def backward_far_kernel(group, first, *refs):
    count = len(group)
    slots, bias, q_ref, g_ref, lse_ref, delta_ref = refs[:6]
    kv = refs[6 : 6 + count]
    rest = refs[6 + count :]
    if not first:
        dqi_ref, rest = rest[0], rest[1:]
    dq_ref, part, acc = rest[0], rest[1 : 1 + count], rest[1 + count : 1 + 2 * count]
    scratch = rest[1 + 2 * count :]
    entries = entries_of(group)
    for a in acc:
        a[...] = jnp.zeros_like(a)

    def step(t, carry):
        def weights(u):
            i = t * UNROLL + u
            p_ref, ds_ref = scratch[2 * u : 2 * u + 2]
            q = q_ref[i]
            g = g_ref[i]
            lse = lse_ref[i]
            delta = delta_ref[i]
            offsets = [lse + bias_of(bias, entry) for entry in group]
            for e in range(0, len(entries), CHUNK):
                some = entries[e : e + CHUNK]
                s = nt(q, gather(kv, some, slots, i, 0))
                d = nt(g, gather(kv, some, slots, i, 1))
                for f, (n, c) in enumerate(some):
                    p = jnp.exp2(s[:, block(f)] * COEF - offsets[n])
                    p_ref[:, block(e + f)] = p.astype(jnp.bfloat16)
                    ds = p * (d[:, block(f)] - delta)
                    ds_ref[:, block(e + f)] = ds.astype(jnp.bfloat16)

        def sums(u):
            i = t * UNROLL + u
            p_ref, ds_ref = scratch[2 * u : 2 * u + 2]
            dq = nn(ds_ref[...], gather(kv, entries, slots, i, 0))
            dq_ref[i] = dq if first else dq + dqi_ref[i]
            dk = tn(ds_ref[...], q_ref[i])
            dv = tn(p_ref[...], g_ref[i])
            for e, (n, c) in enumerate(entries):
                acc[n][slots[i, c], 0] += dk[block(e)]
                acc[n][slots[i, c], 1] += dv[block(e)]

        staggered((weights, sums))
        return carry

    lax.fori_loop(0, NBLK // UNROLL, step, 0)
    for out, a in zip(part, acc):
        out[...] = a[...].astype(jnp.bfloat16)


def backward_far(group, slots, bias, q, g, lse, delta, kv, dq):
    entries = entries_of(group)
    extra = () if dq is None else (dq,)
    return pl.pallas_call(
        functools.partial(backward_far_kernel, group, dq is None),
        out_shape=(STAT,) + tuple(jax.ShapeDtypeStruct(x.shape, jnp.bfloat16) for x in kv),
        in_specs=[SMEM, SMEM] + [VMEM] * (4 + len(kv) + len(extra)),
        out_specs=(VMEM,) * (1 + len(kv)),
        scratch_shapes=[pltpu.VMEM(x.shape, jnp.float32) for x in kv]
        + backward_scratch(BLOCK, len(entries) * BLOCK, UNROLL),
        compiler_params=params(),
        cost_estimate=cost(16 * len(entries), 5, 1, 8 * MIB),
        name="backward_far",
    )(slots, bias, q, g, lse, delta, *kv, *extra)


LOCAL_ROWS = 2
LOCAL_COPIES = 4


def backward_local_kernel(
    q_ref, g_ref, lse_ref, delta_ref, k_ref, v_ref, dqi_ref, dq_ref, dk_ref, dv_ref, *scratch
):
    rows = LOCAL_ROWS * BLOCK
    width = NBLK * BLOCK
    dk_ref[...] = jnp.zeros_like(dk_ref)
    dv_ref[...] = jnp.zeros_like(dv_ref)

    def step(t, carry):
        def here(ref, u):
            first = (t * LOCAL_COPIES + u) * LOCAL_ROWS
            return ref[pl.ds(first, LOCAL_ROWS)].reshape(rows, 128)

        def weights(u):
            p_ref, ds_ref = scratch[2 * u : 2 * u + 2]
            q = here(q_ref, u)
            g = here(g_ref, u)
            lse = here(lse_ref, u)
            delta = here(delta_ref, u)
            for e in range(0, NBLK, CHUNK):
                s = nt(q, k_ref[e : e + CHUNK].reshape(CHUNK * BLOCK, HEAD))
                d = nt(g, v_ref[e : e + CHUNK].reshape(CHUNK * BLOCK, HEAD))
                for f in range(CHUNK):
                    p = jnp.exp2(s[:, block(f)] * COEF - lse)
                    p_ref[:, block(e + f)] = p.astype(jnp.bfloat16)
                    ds = p * (d[:, block(f)] - delta)
                    ds_ref[:, block(e + f)] = ds.astype(jnp.bfloat16)

        def sums(u):
            p_ref, ds_ref = scratch[2 * u : 2 * u + 2]
            dq = here(dqi_ref, u) + nn(ds_ref[...], k_ref[...].reshape(width, HEAD))
            first = (t * LOCAL_COPIES + u) * LOCAL_ROWS
            dq_ref[pl.ds(first, LOCAL_ROWS)] = (
                (dq * SCALE).astype(jnp.bfloat16).reshape(LOCAL_ROWS, BLOCK, HEAD)
            )
            dk_ref[...] += tn(ds_ref[...], here(q_ref, u)).reshape(NBLK, BLOCK, HEAD)
            dv_ref[...] += tn(p_ref[...], here(g_ref, u)).reshape(NBLK, BLOCK, HEAD)

        staggered((weights, sums), LOCAL_COPIES)
        return carry

    lax.fori_loop(0, NBLK // (LOCAL_ROWS * LOCAL_COPIES), step, 0)


def backward_local(q, g, lse, delta, k, v, dq):
    return pl.pallas_call(
        backward_local_kernel,
        out_shape=(HALF, STAT, STAT),
        in_specs=[VMEM] * 7,
        out_specs=(VMEM,) * 3,
        scratch_shapes=backward_scratch(LOCAL_ROWS * BLOCK, NBLK * BLOCK, LOCAL_COPIES),
        compiler_params=params(),
        cost_estimate=cost(256, 5, 1, 8 * MIB),
        name="backward_local",
    )(q, g, lse, delta, k, v, dq)


def finish_kernel(dk_ref, dv_ref, *refs):
    parts, (gk_ref, gv_ref) = refs[:-2], refs[-2:]
    for slot, own in enumerate(SLOT_BLOCK):
        dk = dk_ref[own]
        dv = dv_ref[own]
        for part in parts:
            if slot < part.shape[0]:
                dk += part[slot, 0].astype(jnp.float32)
                dv += part[slot, 1].astype(jnp.float32)
        gk_ref[own] = (dk * SCALE).astype(jnp.bfloat16)
        gv_ref[own] = dv.astype(jnp.bfloat16)


def finish(dk, dv, parts):
    return pl.pallas_call(
        finish_kernel,
        out_shape=(HALF, HALF),
        in_specs=[VMEM] * (2 + len(parts)),
        out_specs=(VMEM,) * 2,
        compiler_params=params(),
        name="finish",
    )(dk, dv, *parts)


def local(queries, keys, values, grad_out, block_lists):
    shape = (NBLK, BLOCK, HEAD)
    q, k, v, g = (x.reshape(shape) for x in (queries, keys, values, grad_out))
    position = lax.axis_index("seq")
    devices = lax.axis_size("seq")
    biases = [jnp.float32(0.0)] * 2
    for band, side, start, sel, by in PLAN:
        source = position - by
        valid = jnp.logical_and(source >= 0, source < devices)
        biases.append(jnp.where(valid, 0.0, BIG).astype(jnp.float32))
    bias = jnp.stack(biases)
    fetched = {}

    def fetch(sent, bands):
        for band, side, start, sel, by in PLAN:
            if band in bands:
                fetched[band, side] = shift(sent[band], by)

    def group(*bands):
        chosen = [e for e in PLAN if e[0] in bands]
        return chosen, [fetched[e[0], e[1]] for e in chosen]

    def hold(values, *bands):
        keys_of = [(e[0], e[1]) for e in group(*bands)[0]]
        values, got = lax.optimization_barrier((values, [fetched[x] for x in keys_of]))
        fetched.update(zip(keys_of, got))
        return values

    slots, everything, *few = pack(k, v, block_lists, NBLK, 4, 2)
    fetch(dict(zip((3, 4), few)), (3, 4))
    everything = hold(everything, *TIE)
    fetch({1: everything}, (1,))
    stats = forward_local(q, k, v)
    stats = hold(stats, 1)
    handed = hand_on(fetched[1, 0], fetched[1, 1])
    for side, by in ((0, 1), (1, -1)):
        fetched[2, side] = shift(handed[side], by)
    for bands, last in (((1, 3, 4), False), ((2,), True)):
        chosen, kv = group(*bands)
        stats = forward_far(chosen, last, slots, bias, q, stats, kv, g)
    out, lse, delta = stats

    def back(dq, *bands):
        chosen, kv = group(*bands)
        return backward_far(chosen, slots, bias, q, g, lse, delta, kv, dq)

    dq, *parts = back(None, 3, 4)
    returned = [shift(part, -e[4]) for part, e in zip(parts, group(3, 4)[0])]
    dq, *parts = back(dq, 2)
    parts, returned = lax.optimization_barrier((parts, returned))
    hop2 = [shift(part, -by) for part, by in zip(parts, (1, -1))]
    dq, *parts = back(dq, 1)
    parts = merge(parts, hop2)
    returned += [shift(part, -by) for part, by in zip(parts, (1, -1))]
    dq, dk, dv = backward_local(q, g, lse, delta, k, v, dq)
    gk, gv = finish(dk, dv, returned)
    flat = (NBLK * BLOCK, HEAD)
    return tuple(x.reshape(flat) for x in (out, dq, gk, gv))


def solution(mesh):
    spec = P(("dp", "seq"), None)
    return jax.shard_map(
        local,
        mesh=mesh,
        in_specs=(spec,) * 5,
        out_specs=(spec,) * 4,
        check_vma=False,
    )
```

time: 259 us -> 180 us (0.69); the launches traced: 254 us -> 179 us
  Pallas kernels: 148 us -> 73.9 us
  waiting for transfers between devices: 21.8 us -> 35.4 us
  starting transfers between devices: 72 us -> 60 us
  local copies, waits for them, and re-layouts: 11.9 us -> 9.1 us
    pallas_call x3, Pallas kernels: 71.7 us -> 30.2 us  [backward_far(): pl.pallas_call(functools.partial(backward_far_kernel, group, dq is None),...]
    pallas_call x1, Pallas kernels: 35.6 us -> 14.2 us  [backward_local(): pl.pallas_call(backward_local_kernel, out_shape=(HALF, STAT, STAT), in_sp...]
    ppermute x16, waiting for transfers between devices: 21.8 us -> 35.4 us  [shift(): return lax.ppermute(value, 'seq', [(s, s + by) for s in range(first, last)])]
    ppermute x16, starting transfers between devices: 72 us -> 60 us  [shift(): return lax.ppermute(value, 'seq', [(s, s + by) for s in range(first, last)])]
    pallas_call x2, Pallas kernels: 25.9 us -> 18.6 us  [forward_far(): pl.pallas_call(functools.partial(forward_far_kernel, group, last), out_sh...]
    slice x3 -> x0, local copies, waits for them, and re-layouts: 4.53 us -> none  [local(): fetched[band, side] = shift(packed[:NBLK >> band - 1], by)]
    pallas_call x1, Pallas kernels: 10.5 us -> 7.31 us  [forward_local(): pl.pallas_call(forward_local_kernel, out_shape=(STAT, STAT, STAT), in_spe...]
    unnamed x22 -> x30, local copies, waits for them, and re-layouts: 7.3 us -> 9.01 us
  transfers between devices with their start and end apart: 16 -> 16, of which waited for: 3 -> 5; matrix products, arithmetic and copies ran while one was open for 2% -> 0% of each run, Pallas kernels for 24% -> 32%
where the time goes in v2:
time: 180 us; the launch traced here: 179 us
  Pallas kernels  73.9 us (41%)
  starting transfers between devices  60 us (33%)
  waiting for transfers between devices  35.4 us (20%)
  local copies, waits for them, and re-layouts  9.1 us (5%)
    ppermute x16, starting transfers between devices, shift(): return lax.ppermute(value, 'seq', [(s, s + by) for s in range(first, last)])  60 us
    ppermute x16, waiting for transfers between devices, shift(): return lax.ppermute(value, 'seq', [(s, s + by) for s in range(first, last)])  35.4 us
    pallas_call x3, Pallas kernels, backward_far(): pl.pallas_call(functools.partial(backward_far_kernel, group, dq is None),...  30.2 us
    pallas_call x2, Pallas kernels, forward_far(): pl.pallas_call(functools.partial(forward_far_kernel, group, last), out_sh...  18.6 us
    pallas_call x1, Pallas kernels, backward_local(): pl.pallas_call(backward_local_kernel, out_shape=(HALF, STAT, STAT), in_sp...  14.2 us
    unnamed x30, local copies, waits for them, and re-layouts  9.01 us
    pallas_call x1, Pallas kernels, forward_local(): pl.pallas_call(forward_local_kernel, out_shape=(STAT, STAT, STAT), in_spe...  7.31 us
  transfers between devices with their start and end apart: 16, of which 5 were waited for; matrix products, arithmetic and copies ran while one was open for 0% of the time, Pallas kernels for 32%

profile of v2, /device:TPU:96, one launch (start us, length us, event | category | flops | bytes accessed | tf_op | source)
XLA Modules:
  0.0 179.4 jit_solution(13556074526374125141)
XLA Ops:
  0.6 0.0 copy-start
  0.6 1.0 copy-done
  1.7 1.0 copy-done.2
  2.7 0.7 copy-done.6
  3.4 0.8 pack.1
  4.3 4.8 %collective-permute-start.1 = (bf16[2,2,128,128]{3,2,1,0:T(8,128)(2,1)S(1)}, bf16[2,2,128,128]{3,2,1,0:T(8,128)(2,1)S(1)}, u32[]{:S(2)}, u32[]{:S(2)}) collective-permute-start(bf16[2,2,128,128]{3,2,1,0:T(8,128)(2,1)S(1)} %get-tuple-element.56), channel_id=1, source_target_pairs={{16,0},{18,2},{20,4},{22,6},{24,8},{26,10},{28,12},{30,14},{32,16}... | collective-permute-start | bytes 393224 | tf_op jit(solution)/shard_map/ppermute | solution.py:54
  9.0 2.6 %collective-permute-start = (bf16[2,2,128,128]{3,2,1,0:T(8,128)(2,1)S(1)}, bf16[2,2,128,128]{3,2,1,0:T(8,128)(2,1)S(1)}, u32[]{:S(2)}, u32[]{:S(2)}) collective-permute-start(bf16[2,2,128,128]{3,2,1,0:T(8,128)(2,1)S(1)} %get-tuple-element.56), channel_id=1, source_target_pairs={{0,16},{2,18},{4,20},{6,22},{8,24},{10,26},{12,28},{14,30},{16,32}... | collective-permute-start | bytes 393224 | tf_op jit(solution)/shard_map/ppermute | solution.py:54
  11.6 1.3 collective-permute-done.1.refs_11_.refs_9_
  12.9 5.4 %collective-permute-done.refs_10_.refs_8_ = bf16[2,2,128,128]{3,2,1,0:T(8,128)(2,1)S(1)} collective-permute-done((bf16[2,2,128,128]{3,2,1,0:T(8,128)(2,1)S(1)}, bf16[2,2,128,128]{3,2,1,0:T(8,128)(2,1)S(1)}, u32[]{:S(2)}, u32[]{:S(2)}) %collective-permute-start) | collective-permute-done | bytes 131104 | tf_op jit(solution)/shard_map/ppermute | solution.py:54
  18.3 0.7 copy-done.7
  18.9 4.6 %collective-permute-start.3 = (bf16[16,2,128,128]{3,2,1,0:T(8,128)(2,1)S(1)}, bf16[16,2,128,128]{3,2,1,0:T(8,128)(2,1)S(1)}, u32[]{:S(2)}, u32[]{:S(2)}) collective-permute-start(bf16[16,2,128,128]{3,2,1,0:T(8,128)(2,1)S(1)} %get-tuple-element.57), channel_id=1, source_target_pairs={{2,0},{4,2},{6,4},{8,6},{10,8},{12,10},{14,12},{16,14},{18,16},{20... | collective-permute-start | bytes 3145736 | tf_op jit(solution)/shard_map/ppermute | solution.py:54
  23.5 1.9 %collective-permute-start.2 = (bf16[16,2,128,128]{3,2,1,0:T(8,128)(2,1)S(1)}, bf16[16,2,128,128]{3,2,1,0:T(8,128)(2,1)S(1)}, u32[]{:S(2)}, u32[]{:S(2)}) collective-permute-start(bf16[16,2,128,128]{3,2,1,0:T(8,128)(2,1)S(1)} %get-tuple-element.57), channel_id=1, source_target_pairs={{0,2},{2,4},{4,6},{6,8},{8,10},{10,12},{12,14},{14,16},{16,18},{18... | collective-permute-start | bytes 3145736 | tf_op jit(solution)/shard_map/ppermute | solution.py:54
  25.5 2.0 %collective-permute-start.5 = (bf16[4,2,128,128]{3,2,1,0:T(8,128)(2,1)}, bf16[4,2,128,128]{3,2,1,0:T(8,128)(2,1)S(1)}, u32[]{:S(2)}, u32[]{:S(2)}) collective-permute-start(bf16[4,2,128,128]{3,2,1,0:T(8,128)(2,1)} %get-tuple-element.63), channel_id=1, source_target_pairs={{8,0},{10,2},{12,4},{14,6},{16,8},{18,10},{20,12},{22,14},{24,16},... | collective-permute-start | bytes 786440 | tf_op jit(solution)/shard_map/ppermute | solution.py:54
  27.5 3.8 %collective-permute-start.4 = (bf16[4,2,128,128]{3,2,1,0:T(8,128)(2,1)}, bf16[4,2,128,128]{3,2,1,0:T(8,128)(2,1)}, u32[]{:S(2)}, u32[]{:S(2)}) collective-permute-start(bf16[4,2,128,128]{3,2,1,0:T(8,128)(2,1)} %get-tuple-element.63), channel_id=1, source_target_pairs={{0,8},{2,10},{4,12},{6,14},{8,16},{10,18},{12,20},{14,22},{16,24},... | collective-permute-start | bytes 786440 | tf_op jit(solution)/shard_map/ppermute | solution.py:54
  31.3 0.0 copy-done.4
  31.3 7.3 %forward_local.1 = (f32[16,128,128]{2,1,0:T(8,128)S(1)}, f32[16,128,128]{2,1,0:T(8,128)S(1)}, f32[16,128,128]{2,1,0:T(8,128)S(1)}) custom-call(bf16[16,128,128]{2,1,0:T(8,128)(2,1)S(1)} %bitcast.22, bf16[16,128,128]{2,1,0:T(8,128)(2,1)S(1)} %bitcast.17, bf16[16,128,128]{2,1,0:T(8,128)(2,1)S(1)} %bitcast.20), custom_call_target="tpu_custom_call" | custom-call | flops 2147483648 | bytes 5242880 | tf_op jit(solution)/shard_map/forward_local/pallas_call | solution.py:213
  38.7 0.0 copy-start.11
  38.7 1.0 copy-done.11
  39.6 13.0 %collective-permute-done.3.refs_7_.b_ref = bf16[16,2,128,128]{3,2,1,0:T(8,128)(2,1)S(1)} collective-permute-done((bf16[16,2,128,128]{3,2,1,0:T(8,128)(2,1)S(1)}, bf16[16,2,128,128]{3,2,1,0:T(8,128)(2,1)S(1)}, u32[]{:S(2)}, u32[]{:S(2)}) %collective-permute-start.3) | collective-permute-done | bytes 1048608 | tf_op jit(solution)/shard_map/ppermute | solution.py:54
  52.6 8.5 %collective-permute-done.2.refs_6_.a_ref = bf16[16,2,128,128]{3,2,1,0:T(8,128)(2,1)S(1)} collective-permute-done((bf16[16,2,128,128]{3,2,1,0:T(8,128)(2,1)S(1)}, bf16[16,2,128,128]{3,2,1,0:T(8,128)(2,1)S(1)}, u32[]{:S(2)}, u32[]{:S(2)}) %collective-permute-start.2) | collective-permute-done | bytes 1048608 | tf_op jit(solution)/shard_map/ppermute | solution.py:54
  61.2 1.0 hand_on.1
  62.2 0.0 copy-done.9
  62.2 0.0 copy-done.13
  62.2 1.9 %collective-permute-start.6 = (bf16[8,2,128,128]{3,2,1,0:T(8,128)(2,1)}, bf16[8,2,128,128]{3,2,1,0:T(8,128)(2,1)S(1)}, u32[]{:S(2)}, u32[]{:S(2)}) collective-permute-start(bf16[8,2,128,128]{3,2,1,0:T(8,128)(2,1)} %get-tuple-element.69), channel_id=1, source_target_pairs={{0,2},{2,4},{4,6},{6,8},{8,10},{10,12},{12,14},{14,16},{16,18},{18... | collective-permute-start | bytes 1572872 | tf_op jit(solution)/shard_map/ppermute | solution.py:54
  64.1 8.1 %collective-permute-start.7 = (bf16[8,2,128,128]{3,2,1,0:T(8,128)(2,1)}, bf16[8,2,128,128]{3,2,1,0:T(8,128)(2,1)}, u32[]{:S(2)}, u32[]{:S(2)}) collective-permute-start(bf16[8,2,128,128]{3,2,1,0:T(8,128)(2,1)} %get-tuple-element.70), channel_id=1, source_target_pairs={{2,0},{4,2},{6,4},{8,6},{10,8},{12,10},{14,12},{16,14},{18,16},{20... | collective-permute-start | bytes 1572872 | tf_op jit(solution)/shard_map/ppermute | solution.py:54
  72.3 0.1 stack.35.refs_1_
  72.4 0.0 collective-permute-done.5.refs_9_.refs_7_
  72.4 0.0 collective-permute-done.4.refs_8_.refs_6_
  72.4 0.0 copy-start.8
  72.4 0.9 copy-done.8
  73.3 1.2 copy-done.10
  74.6 1.2 copy-done.12
  75.8 1.2 copy-done.14
  77.0 11.7 %forward_far.2 = (f32[16,128,128]{2,1,0:T(8,128)S(1)}, f32[16,128,128]{2,1,0:T(8,128)S(1)}, f32[16,128,128]{2,1,0:T(8,128)S(1)}) custom-call(s32[16,30]{1,0:T(8,128)S(1)} %get-tuple-element.51.refs_0_, f32[10]{0:T(128)S(1)} %stack.35.refs_1_, bf16[16,128,128]{2,1,0:T(8,128)(2,1)S(1)} %bitcast.23, f32[16,128,128]{2,1,0:T(8,128)S(1)} %copy-done.10, ...), custom_call_target="tpu_custom_call" | custom-call | flops 2952790016 | bytes 8388608 | tf_op jit(solution)/shard_map/forward_far/pallas_call | solution.py:295
  88.7 0.0 collective-permute-done.6.refs_6_
  88.8 0.0 collective-permute-done.7.refs_7_
  88.8 0.0 copy-done.5
  88.8 6.9 %forward_far.3 = (bf16[16,128,128]{2,1,0:T(8,128)(2,1)}, f32[16,128,128]{2,1,0:T(8,128)S(1)}, f32[16,128,128]{2,1,0:T(8,128)S(1)}) custom-call(s32[16,30]{1,0:T(8,128)S(1)} %get-tuple-element.51.refs_0_, f32[10]{0:T(128)S(1)} %stack.35.refs_1_, bf16[16,128,128]{2,1,0:T(8,128)(2,1)S(1)} %bitcast.24, f32[16,128,128]{2,1,0:T(8,128)S(1)} %get-tuple-element.66.refs_3_, ...), custom_call_target="tpu_custom_call" | custom-call | flops 1073741824 | bytes 8388608 | tf_op jit(solution)/shard_map/forward_far/pallas_call | solution.py:295
  95.6 6.5 %backward_far.3 = (f32[16,128,128]{2,1,0:T(8,128)S(1)}, bf16[4,2,128,128]{3,2,1,0:T(8,128)(2,1)S(1)}, bf16[4,2,128,128]{3,2,1,0:T(8,128)(2,1)S(1)}, bf16[2,2,128...) custom-call(s32[16,30]{1,0:T(8,128)S(1)} %get-tuple-element.51.refs_0_, f32[10]{0:T(128)S(1)} %stack.35.refs_1_, ...), custom_call_target="tpu_custom_call" | custom-call | flops 2013265920 | bytes 8388608 | tf_op jit(solution)/shard_map/backward_far/pallas_call | solution.py:372
  102.1 1.9 %collective-permute-start.8 = (bf16[4,2,128,128]{3,2,1,0:T(8,128)(2,1)S(1)}, bf16[4,2,128,128]{3,2,1,0:T(8,128)(2,1)S(1)}, u32[]{:S(2)}, u32[]{:S(2)}) collective-permute-start(bf16[4,2,128,128]{3,2,1,0:T(8,128)(2,1)S(1)} %get-tuple-element.82), channel_id=1, source_target_pairs={{8,0},{10,2},{12,4},{14,6},{16,8},{18,10},{20,12},{22,14},{24,16},... | collective-permute-start | bytes 786440 | tf_op jit(solution)/shard_map/ppermute | solution.py:54
  104.1 3.9 %collective-permute-start.9 = (bf16[4,2,128,128]{3,2,1,0:T(8,128)(2,1)S(1)}, bf16[4,2,128,128]{3,2,1,0:T(8,128)(2,1)S(1)}, u32[]{:S(2)}, u32[]{:S(2)}) collective-permute-start(bf16[4,2,128,128]{3,2,1,0:T(8,128)(2,1)S(1)} %get-tuple-element.83), channel_id=1, source_target_pairs={{0,8},{2,10},{4,12},{6,14},{8,16},{10,18},{12,20},{14,22},{16,24},... | collective-permute-start | bytes 786440 | tf_op jit(solution)/shard_map/ppermute | solution.py:54
  108.0 1.9 %collective-permute-start.10 = (bf16[2,2,128,128]{3,2,1,0:T(8,128)(2,1)S(1)}, bf16[2,2,128,128]{3,2,1,0:T(8,128)(2,1)S(1)}, u32[]{:S(2)}, u32[]{:S(2)}) collective-permute-start(bf16[2,2,128,128]{3,2,1,0:T(8,128)(2,1)S(1)} %get-tuple-element.84), channel_id=1, source_target_pairs={{16,0},{18,2},{20,4},{22,6},{24,8},{26,10},{28,12},{30,14},{32,16}... | collective-permute-start | bytes 393224 | tf_op jit(solution)/shard_map/ppermute | solution.py:54
  109.9 5.4 %collective-permute-start.11 = (bf16[2,2,128,128]{3,2,1,0:T(8,128)(2,1)S(1)}, bf16[2,2,128,128]{3,2,1,0:T(8,128)(2,1)S(1)}, u32[]{:S(2)}, u32[]{:S(2)}) collective-permute-start(bf16[2,2,128,128]{3,2,1,0:T(8,128)(2,1)S(1)} %get-tuple-element.85), channel_id=1, source_target_pairs={{0,16},{2,18},{4,20},{6,22},{8,24},{10,26},{12,28},{14,30},{16,32}... | collective-permute-start | bytes 393224 | tf_op jit(solution)/shard_map/ppermute | solution.py:54
  115.3 8.4 %backward_far.4 = (f32[16,128,128]{2,1,0:T(8,128)S(1)}, bf16[8,2,128,128]{3,2,1,0:T(8,128)(2,1)S(1)}, bf16[8,2,128,128]{3,2,1,0:T(8,128)(2,1)S(1)}) custom-call(s32[16,30]{1,0:T(8,128)S(1)} %get-tuple-element.51.refs_0_, f32[10]{0:T(128)S(1)} %stack.35.refs_1_, bf16[16,128,128]{2,1,0:T(8,128)(2,1)S(1)} %bitcast.26, bf16[16,128,128]{2,1,0:T(8,128)(2,1)S(1)} %bitcast.31, ...), custom_call_target="tpu_custom_call" | custom-call | flops 2684354560 | bytes 8388608 | tf_op jit(solution)/shard_map/backward_far/pallas_call | solution.py:372
  123.8 0.0 collective-permute-done.10.refs_2_
  123.8 0.0 collective-permute-done.11.refs_3_
  123.8 0.0 collective-permute-done.8.refs_0_
  123.8 0.0 collective-permute-done.9.refs_1_
  123.8 4.9 %collective-permute-start.12 = (bf16[8,2,128,128]{3,2,1,0:T(8,128)(2,1)S(1)}, bf16[8,2,128,128]{3,2,1,0:T(8,128)(2,1)S(1)}, u32[]{:S(2)}, u32[]{:S(2)}) collective-permute-start(bf16[8,2,128,128]{3,2,1,0:T(8,128)(2,1)S(1)} %get-tuple-element.92), channel_id=1, source_target_pairs={{2,0},{4,2},{6,4},{8,6},{10,8},{12,10},{14,12},{16,14},{18,16},{20... | collective-permute-start | bytes 1572872 | tf_op jit(solution)/shard_map/ppermute | solution.py:54
  128.8 2.1 %collective-permute-start.13 = (bf16[8,2,128,128]{3,2,1,0:T(8,128)(2,1)S(1)}, bf16[8,2,128,128]{3,2,1,0:T(8,128)(2,1)S(1)}, u32[]{:S(2)}, u32[]{:S(2)}) collective-permute-start(bf16[8,2,128,128]{3,2,1,0:T(8,128)(2,1)S(1)} %get-tuple-element.93), channel_id=1, source_target_pairs={{0,2},{2,4},{4,6},{6,8},{8,10},{10,12},{12,14},{14,16},{16,18},{18... | collective-permute-start | bytes 1572872 | tf_op jit(solution)/shard_map/ppermute | solution.py:54
  130.9 15.3 %backward_far.5 = (f32[16,128,128]{2,1,0:T(8,128)S(1)}, bf16[16,2,128,128]{3,2,1,0:T(8,128)(2,1)S(1)}, bf16[16,2,128,128]{3,2,1,0:T(8,128)(2,1)S(1)}) custom-call(s32[16,30]{1,0:T(8,128)S(1)} %get-tuple-element.51.refs_0_, f32[10]{0:T(128)S(1)} %stack.35.refs_1_, bf16[16,128,128]{2,1,0:T(8,128)(2,1)S(1)} %bitcast.27, bf16[16,128,128]{2,1,0:T(8,128)(2,1)S(1)} %bitcast.32, ...), custom_call_target="tpu_custom_call" | custom-call | flops 5368709120 | bytes 8388608 | tf_op jit(solution)/shard_map/backward_far/pallas_call | solution.py:372
  146.2 0.0 collective-permute-done.12.refs_2_
  146.2 0.0 collective-permute-done.13.refs_3_
  146.2 0.0 copy-start.1
  146.2 0.0 copy-start.3
  146.2 0.3 merge.1
  146.5 8.1 %collective-permute-start.14 = (bf16[16,2,128,128]{3,2,1,0:T(8,128)(2,1)S(1)}, bf16[16,2,128,128]{3,2,1,0:T(8,128)(2,1)S(1)}, u32[]{:S(2)}, u32[]{:S(2)}) collective-permute-start(bf16[16,2,128,128]{3,2,1,0:T(8,128)(2,1)S(1)} %get-tuple-element.94), channel_id=1, source_target_pairs={{2,0},{4,2},{6,4},{8,6},{10,8},{12,10},{14,12},{16,14},{18,16},{20... | collective-permute-start | bytes 3145736 | tf_op jit(solution)/shard_map/ppermute | solution.py:54
  154.7 1.9 %collective-permute-start.15 = (bf16[16,2,128,128]{3,2,1,0:T(8,128)(2,1)S(1)}, bf16[16,2,128,128]{3,2,1,0:T(8,128)(2,1)S(1)}, u32[]{:S(2)}, u32[]{:S(2)}) collective-permute-start(bf16[16,2,128,128]{3,2,1,0:T(8,128)(2,1)S(1)} %get-tuple-element.95), channel_id=1, source_target_pairs={{0,2},{2,4},{4,6},{6,8},{8,10},{10,12},{12,14},{14,16},{16,18},{18... | collective-permute-start | bytes 3145736 | tf_op jit(solution)/shard_map/ppermute | solution.py:54
  156.6 0.0 copy-done.1
  156.6 0.0 copy-done.3
  156.6 14.2 %backward_local.1 = (bf16[16,128,128]{2,1,0:T(8,128)(2,1)}, f32[16,128,128]{2,1,0:T(8,128)S(1)}, f32[16,128,128]{2,1,0:T(8,128)S(1)}) custom-call(bf16[16,128,128]{2,1,0:T(8,128)(2,1)S(1)} %bitcast.28, bf16[16,128,128]{2,1,0:T(8,128)(2,1)S(1)} %bitcast.33, f32[16,128,128]{2,1,0:T(8,128)S(1)} %get-tuple-element.72.refs_4_.lse_ref, ...), custom_call_target="tpu_custom_call" | custom-call | flops 5368709120 | bytes 8388608 | tf_op jit(solution)/shard_map/backward_local/pallas_call | solution.py:434
  170.8 0.0 collective-permute-done.14.refs_4_
  170.8 7.2 %collective-permute-done.15.refs_5_ = bf16[16,2,128,128]{3,2,1,0:T(8,128)(2,1)S(1)} collective-permute-done((bf16[16,2,128,128]{3,2,1,0:T(8,128)(2,1)S(1)}, bf16[16,2,128,128]{3,2,1,0:T(8,128)(2,1)S(1)}, u32[]{:S(2)}, u32[]{:S(2)}) %collective-permute-start.15) | collective-permute-done | bytes 1048608 | tf_op jit(solution)/shard_map/ppermute | solution.py:54
  178.0 1.4 finish.1
  (11 shorter events, 0.0 us)
Async XLA Ops:
  0.6 1.0 copy-start
  1.7 1.0 copy-start.2
  2.7 0.7 copy-start.6
  3.4 27.9 %copy-start.4 = (bf16[2048,128]{1,0:T(8,128)(2,1)S(1)}, bf16[2048,128]{1,0:T(8,128)(2,1)}, u32[]{:S(2)}) copy-start(bf16[2048,128]{1,0:T(8,128)(2,1)} %param.5) | copy-start | bytes 1572868
  4.3 8.6 %collective-permute-start.1 = (bf16[2,2,128,128]{3,2,1,0:T(8,128)(2,1)S(1)}, bf16[2,2,128,128]{3,2,1,0:T(8,128)(2,1)S(1)}, u32[]{:S(2)}, u32[]{:S(2)}) collective-permute-start(bf16[2,2,128,128]{3,2,1,0:T(8,128)(2,1)S(1)} %get-tuple-element.56), channel_id=1, source_target_pairs={{16,0},{18,2},{20,4},{22,6},{24,8},{26,10},{28,12},{30,14},{32,16}... | collective-permute-start | bytes 393224 | tf_op jit(solution)/shard_map/ppermute | solution.py:54
  9.0 9.3 %collective-permute-start = (bf16[2,2,128,128]{3,2,1,0:T(8,128)(2,1)S(1)}, bf16[2,2,128,128]{3,2,1,0:T(8,128)(2,1)S(1)}, u32[]{:S(2)}, u32[]{:S(2)}) collective-permute-start(bf16[2,2,128,128]{3,2,1,0:T(8,128)(2,1)S(1)} %get-tuple-element.56), channel_id=1, source_target_pairs={{0,16},{2,18},{4,20},{6,22},{8,24},{10,26},{12,28},{14,30},{16,32}... | collective-permute-start | bytes 393224 | tf_op jit(solution)/shard_map/ppermute | solution.py:54
  18.3 0.7 copy-start.7
  18.9 33.7 %collective-permute-start.3 = (bf16[16,2,128,128]{3,2,1,0:T(8,128)(2,1)S(1)}, bf16[16,2,128,128]{3,2,1,0:T(8,128)(2,1)S(1)}, u32[]{:S(2)}, u32[]{:S(2)}) collective-permute-start(bf16[16,2,128,128]{3,2,1,0:T(8,128)(2,1)S(1)} %get-tuple-element.57), channel_id=1, source_target_pairs={{2,0},{4,2},{6,4},{8,6},{10,8},{12,10},{14,12},{16,14},{18,16},{20... | collective-permute-start | bytes 3145736 | tf_op jit(solution)/shard_map/ppermute | solution.py:54
  23.5 37.6 %collective-permute-start.2 = (bf16[16,2,128,128]{3,2,1,0:T(8,128)(2,1)S(1)}, bf16[16,2,128,128]{3,2,1,0:T(8,128)(2,1)S(1)}, u32[]{:S(2)}, u32[]{:S(2)}) collective-permute-start(bf16[16,2,128,128]{3,2,1,0:T(8,128)(2,1)S(1)} %get-tuple-element.57), channel_id=1, source_target_pairs={{0,2},{2,4},{4,6},{6,8},{8,10},{10,12},{12,14},{14,16},{16,18},{18... | collective-permute-start | bytes 3145736 | tf_op jit(solution)/shard_map/ppermute | solution.py:54
  25.5 46.9 %collective-permute-start.5 = (bf16[4,2,128,128]{3,2,1,0:T(8,128)(2,1)}, bf16[4,2,128,128]{3,2,1,0:T(8,128)(2,1)S(1)}, u32[]{:S(2)}, u32[]{:S(2)}) collective-permute-start(bf16[4,2,128,128]{3,2,1,0:T(8,128)(2,1)} %get-tuple-element.63), channel_id=1, source_target_pairs={{8,0},{10,2},{12,4},{14,6},{16,8},{18,10},{20,12},{22,14},{24,16},... | collective-permute-start | bytes 786440 | tf_op jit(solution)/shard_map/ppermute | solution.py:54
  27.5 44.9 %collective-permute-start.4 = (bf16[4,2,128,128]{3,2,1,0:T(8,128)(2,1)}, bf16[4,2,128,128]{3,2,1,0:T(8,128)(2,1)}, u32[]{:S(2)}, u32[]{:S(2)}) collective-permute-start(bf16[4,2,128,128]{3,2,1,0:T(8,128)(2,1)} %get-tuple-element.63), channel_id=1, source_target_pairs={{0,8},{2,10},{4,12},{6,14},{8,16},{10,18},{12,20},{14,22},{16,24},... | collective-permute-start | bytes 786440 | tf_op jit(solution)/shard_map/ppermute | solution.py:54
  38.7 1.0 copy-start.11
  39.6 22.5 %copy-start.9 = (f32[16,128,128]{2,1,0:T(8,128)}, f32[16,128,128]{2,1,0:T(8,128)S(1)}, u32[]{:S(2)}) copy-start(f32[16,128,128]{2,1,0:T(8,128)S(1)} %get-tuple-element.58.refs_3_) | copy-start | bytes 3145732
  39.6 22.5 %copy-start.13 = (f32[16,128,128]{2,1,0:T(8,128)}, f32[16,128,128]{2,1,0:T(8,128)S(1)}, u32[]{:S(2)}) copy-start(f32[16,128,128]{2,1,0:T(8,128)S(1)} %get-tuple-element.60.refs_5_) | copy-start | bytes 3145732
  62.2 26.6 %collective-permute-start.6 = (bf16[8,2,128,128]{3,2,1,0:T(8,128)(2,1)}, bf16[8,2,128,128]{3,2,1,0:T(8,128)(2,1)S(1)}, u32[]{:S(2)}, u32[]{:S(2)}) collective-permute-start(bf16[8,2,128,128]{3,2,1,0:T(8,128)(2,1)} %get-tuple-element.69), channel_id=1, source_target_pairs={{0,2},{2,4},{4,6},{6,8},{8,10},{10,12},{12,14},{14,16},{16,18},{18... | collective-permute-start | bytes 1572872 | tf_op jit(solution)/shard_map/ppermute | solution.py:54
  64.1 24.7 %collective-permute-start.7 = (bf16[8,2,128,128]{3,2,1,0:T(8,128)(2,1)}, bf16[8,2,128,128]{3,2,1,0:T(8,128)(2,1)}, u32[]{:S(2)}, u32[]{:S(2)}) collective-permute-start(bf16[8,2,128,128]{3,2,1,0:T(8,128)(2,1)} %get-tuple-element.70), channel_id=1, source_target_pairs={{2,0},{4,2},{6,4},{8,6},{10,8},{12,10},{14,12},{16,14},{18,16},{20... | collective-permute-start | bytes 1572872 | tf_op jit(solution)/shard_map/ppermute | solution.py:54
  72.4 0.9 copy-start.8
  73.3 1.2 copy-start.10
  74.6 1.2 copy-start.12
  75.8 1.2 copy-start.14
  77.0 11.8 %copy-start.5 = (bf16[2048,128]{1,0:T(8,128)(2,1)S(1)}, bf16[2048,128]{1,0:T(8,128)(2,1)}, u32[]{:S(2)}) copy-start(bf16[2048,128]{1,0:T(8,128)(2,1)} %param.8) | copy-start | bytes 1572868
  102.1 21.7 %collective-permute-start.8 = (bf16[4,2,128,128]{3,2,1,0:T(8,128)(2,1)S(1)}, bf16[4,2,128,128]{3,2,1,0:T(8,128)(2,1)S(1)}, u32[]{:S(2)}, u32[]{:S(2)}) collective-permute-start(bf16[4,2,128,128]{3,2,1,0:T(8,128)(2,1)S(1)} %get-tuple-element.82), channel_id=1, source_target_pairs={{8,0},{10,2},{12,4},{14,6},{16,8},{18,10},{20,12},{22,14},{24,16},... | collective-permute-start | bytes 786440 | tf_op jit(solution)/shard_map/ppermute | solution.py:54
  104.1 19.8 %collective-permute-start.9 = (bf16[4,2,128,128]{3,2,1,0:T(8,128)(2,1)S(1)}, bf16[4,2,128,128]{3,2,1,0:T(8,128)(2,1)S(1)}, u32[]{:S(2)}, u32[]{:S(2)}) collective-permute-start(bf16[4,2,128,128]{3,2,1,0:T(8,128)(2,1)S(1)} %get-tuple-element.83), channel_id=1, source_target_pairs={{0,8},{2,10},{4,12},{6,14},{8,16},{10,18},{12,20},{14,22},{16,24},... | collective-permute-start | bytes 786440 | tf_op jit(solution)/shard_map/ppermute | solution.py:54
  108.0 15.8 %collective-permute-start.10 = (bf16[2,2,128,128]{3,2,1,0:T(8,128)(2,1)S(1)}, bf16[2,2,128,128]{3,2,1,0:T(8,128)(2,1)S(1)}, u32[]{:S(2)}, u32[]{:S(2)}) collective-permute-start(bf16[2,2,128,128]{3,2,1,0:T(8,128)(2,1)S(1)} %get-tuple-element.84), channel_id=1, source_target_pairs={{16,0},{18,2},{20,4},{22,6},{24,8},{26,10},{28,12},{30,14},{32,16}... | collective-permute-start | bytes 393224 | tf_op jit(solution)/shard_map/ppermute | solution.py:54
  109.9 13.9 %collective-permute-start.11 = (bf16[2,2,128,128]{3,2,1,0:T(8,128)(2,1)S(1)}, bf16[2,2,128,128]{3,2,1,0:T(8,128)(2,1)S(1)}, u32[]{:S(2)}, u32[]{:S(2)}) collective-permute-start(bf16[2,2,128,128]{3,2,1,0:T(8,128)(2,1)S(1)} %get-tuple-element.85), channel_id=1, source_target_pairs={{0,16},{2,18},{4,20},{6,22},{8,24},{10,26},{12,28},{14,30},{16,32}... | collective-permute-start | bytes 393224 | tf_op jit(solution)/shard_map/ppermute | solution.py:54
  123.8 22.4 %collective-permute-start.12 = (bf16[8,2,128,128]{3,2,1,0:T(8,128)(2,1)S(1)}, bf16[8,2,128,128]{3,2,1,0:T(8,128)(2,1)S(1)}, u32[]{:S(2)}, u32[]{:S(2)}) collective-permute-start(bf16[8,2,128,128]{3,2,1,0:T(8,128)(2,1)S(1)} %get-tuple-element.92), channel_id=1, source_target_pairs={{2,0},{4,2},{6,4},{8,6},{10,8},{12,10},{14,12},{16,14},{18,16},{20... | collective-permute-start | bytes 1572872 | tf_op jit(solution)/shard_map/ppermute | solution.py:54
  128.8 17.4 %collective-permute-start.13 = (bf16[8,2,128,128]{3,2,1,0:T(8,128)(2,1)S(1)}, bf16[8,2,128,128]{3,2,1,0:T(8,128)(2,1)S(1)}, u32[]{:S(2)}, u32[]{:S(2)}) collective-permute-start(bf16[8,2,128,128]{3,2,1,0:T(8,128)(2,1)S(1)} %get-tuple-element.93), channel_id=1, source_target_pairs={{0,2},{2,4},{4,6},{6,8},{8,10},{10,12},{12,14},{14,16},{16,18},{18... | collective-permute-start | bytes 1572872 | tf_op jit(solution)/shard_map/ppermute | solution.py:54
  146.2 10.4 %copy-start.1 = (bf16[2048,128]{1,0:T(8,128)(2,1)S(1)}, bf16[2048,128]{1,0:T(8,128)(2,1)}, u32[]{:S(2)}) copy-start(bf16[2048,128]{1,0:T(8,128)(2,1)} %param.6) | copy-start | bytes 1572868
  146.2 10.4 %copy-start.3 = (bf16[2048,128]{1,0:T(8,128)(2,1)S(1)}, bf16[2048,128]{1,0:T(8,128)(2,1)}, u32[]{:S(2)}) copy-start(bf16[2048,128]{1,0:T(8,128)(2,1)} %param.7) | copy-start | bytes 1572868
  146.5 24.3 %collective-permute-start.14 = (bf16[16,2,128,128]{3,2,1,0:T(8,128)(2,1)S(1)}, bf16[16,2,128,128]{3,2,1,0:T(8,128)(2,1)S(1)}, u32[]{:S(2)}, u32[]{:S(2)}) collective-permute-start(bf16[16,2,128,128]{3,2,1,0:T(8,128)(2,1)S(1)} %get-tuple-element.94), channel_id=1, source_target_pairs={{2,0},{4,2},{6,4},{8,6},{10,8},{12,10},{14,12},{16,14},{18,16},{20... | collective-permute-start | bytes 3145736 | tf_op jit(solution)/shard_map/ppermute | solution.py:54
  154.7 23.3 %collective-permute-start.15 = (bf16[16,2,128,128]{3,2,1,0:T(8,128)(2,1)S(1)}, bf16[16,2,128,128]{3,2,1,0:T(8,128)(2,1)S(1)}, u32[]{:S(2)}, u32[]{:S(2)}) collective-permute-start(bf16[16,2,128,128]{3,2,1,0:T(8,128)(2,1)S(1)} %get-tuple-element.95), channel_id=1, source_target_pairs={{0,2},{2,4},{4,6},{6,8},{8,10},{10,12},{12,14},{14,16},{16,18},{18... | collective-permute-start | bytes 3145736 | tf_op jit(solution)/shard_map/ppermute | solution.py:54

commit v3 on v2

--- a/solution.py
+++ b/solution.py
@@ -101,21 +101,23 @@
     )(key_blocks, value_blocks, lists)
 
 
-def hand_on_kernel(a_ref, b_ref, out_a_ref, out_b_ref):
-    out_a_ref[...] = a_ref[: NBLK // 2]
-    out_b_ref[...] = b_ref[: NBLK // 2]
-
-
-def hand_on(a, b):
-    half = jax.ShapeDtypeStruct((NBLK // 2, 2, BLOCK, HEAD), jnp.bfloat16)
+def hand_on_kernel(*refs):
+    count = len(refs) // 2
+    for ref, out_ref in zip(refs[:count], refs[count:]):
+        out_ref[...] = ref[: out_ref.shape[0]]
+
+
+def hand_on(values):
     return pl.pallas_call(
         hand_on_kernel,
-        out_shape=(half, half),
-        in_specs=[VMEM] * 2,
-        out_specs=(VMEM,) * 2,
+        out_shape=tuple(
+            jax.ShapeDtypeStruct((x.shape[0] // 2,) + x.shape[1:], x.dtype) for x in values
+        ),
+        in_specs=[VMEM] * len(values),
+        out_specs=(VMEM,) * len(values),
         compiler_params=params(),
         name="hand_on",
-    )(a, b)
+    )(*values)
 
 
 def merge_kernel(*refs):
@@ -312,7 +314,6 @@
 
 
 CHUNK = 2
-TIE = (4,)
 
 
 def backward_far_kernel(group, first, *refs):
@@ -495,16 +496,16 @@
         fetched.update(zip(keys_of, got))
         return values
 
-    slots, everything, *few = pack(k, v, block_lists, NBLK, 4, 2)
-    fetch(dict(zip((3, 4), few)), (3, 4))
-    everything = hold(everything, *TIE)
-    fetch({1: everything}, (1,))
+    slots, near, next_near, far = pack(k, v, block_lists, NBLK, 4, 2)
+    fetch({1: near, 4: far}, (1, 4))
     stats = forward_local(q, k, v)
-    stats = hold(stats, 1)
-    handed = hand_on(fetched[1, 0], fetched[1, 1])
-    for side, by in ((0, 1), (1, -1)):
-        fetched[2, side] = shift(handed[side], by)
-    for bands, last in (((1, 3, 4), False), ((2,), True)):
+    stats, next_near = hold((stats, next_near), 1)
+    hops = ((1, 0, 1), (1, 1, -1), (3, 0, 4), (3, 1, -4))
+    handed = hand_on([fetched[1, 0], fetched[1, 1]])
+    for (band, side, by), part in zip(hops, handed):
+        fetched[band + 1, side] = shift(part, by)
+    fetch({3: next_near}, (3,))
+    for bands, last in (((1,), False), ((2, 3, 4), True)):
         chosen, kv = group(*bands)
         stats = forward_far(chosen, last, slots, bias, q, stats, kv, g)
     out, lse, delta = stats
@@ -513,14 +514,11 @@
         chosen, kv = group(*bands)
         return backward_far(chosen, slots, bias, q, g, lse, delta, kv, dq)
 
-    dq, *parts = back(None, 3, 4)
-    returned = [shift(part, -e[4]) for part, e in zip(parts, group(3, 4)[0])]
-    dq, *parts = back(dq, 2)
-    parts, returned = lax.optimization_barrier((parts, returned))
-    hop2 = [shift(part, -by) for part, by in zip(parts, (1, -1))]
-    dq, *parts = back(dq, 1)
-    parts = merge(parts, hop2)
-    returned += [shift(part, -by) for part, by in zip(parts, (1, -1))]
+    dq, *parts = back(None, 2, 4)
+    hop = [shift(part, -by) for part, (band, side, by) in zip(parts, hops)]
+    dq, *parts = back(dq, 1, 3)
+    parts = merge(parts, hop)
+    returned = [shift(part, -by) for part, (band, side, by) in zip(parts, hops)]
     dq, dk, dv = backward_local(q, g, lse, delta, k, v, dq)
     gk, gv = finish(dk, dv, returned)
     flat = (NBLK * BLOCK, HEAD)

time: 180 us -> 176 us (0.978)
  waiting for transfers between devices: 35.4 us -> 32.9 us
  Pallas kernels: 73.9 us -> 71.8 us
    ppermute x16, waiting for transfers between devices: 35.4 us -> 32.9 us  [shift(): return lax.ppermute(value, 'seq', [(s, s + by) for s in range(first, last)])]
    pallas_call x3 -> x2, Pallas kernels: 30.2 us -> 28 us  [backward_far(): pl.pallas_call(functools.partial(backward_far_kernel, group, dq is None),...]
    unnamed x30 -> x26, local copies, waits for them, and re-layouts: 9.01 us -> 7.43 us
  transfers between devices with their start and end apart: 16 -> 16, of which waited for: 5 -> 5; matrix products, arithmetic and copies ran while one was open for 0% -> 0% of each run, Pallas kernels for 32% -> 28%
where the time goes in v3:
time: 176 us; the launch traced here: 175 us
  Pallas kernels  71.8 us (41%)
  starting transfers between devices  61.6 us (35%)
  waiting for transfers between devices  32.9 us (19%)
  local copies, waits for them, and re-layouts  7.52 us (4%)
    ppermute x16, starting transfers between devices, shift(): return lax.ppermute(value, 'seq', [(s, s + by) for s in range(first, last)])  61.6 us
    ppermute x16, waiting for transfers between devices, shift(): return lax.ppermute(value, 'seq', [(s, s + by) for s in range(first, last)])  32.9 us
    pallas_call x2, Pallas kernels, backward_far(): pl.pallas_call(functools.partial(backward_far_kernel, group, dq is None),...  28 us
    pallas_call x2, Pallas kernels, forward_far(): pl.pallas_call(functools.partial(forward_far_kernel, group, last), out_sh...  18.6 us
    pallas_call x1, Pallas kernels, backward_local(): pl.pallas_call(backward_local_kernel, out_shape=(HALF, STAT, STAT), in_sp...  14.4 us
    unnamed x26, local copies, waits for them, and re-layouts  7.43 us
    pallas_call x1, Pallas kernels, forward_local(): pl.pallas_call(forward_local_kernel, out_shape=(STAT, STAT, STAT), in_spe...  7.32 us
  transfers between devices with their start and end apart: 16, of which 5 were waited for; matrix products, arithmetic and copies ran while one was open for 0% of the time, Pallas kernels for 28%

profile of v3, /device:TPU:96, one launch (start us, length us, event | category | flops | bytes accessed | tf_op | source)
XLA Modules:
  0.0 174.9 jit_solution(12734266530272586311)
XLA Ops:
  0.6 0.0 copy-start
  0.6 1.0 copy-done
  1.7 0.0 copy-start.2
  1.7 1.0 copy-done.2
  2.7 0.0 copy-start.4
  2.7 0.7 copy-done.4
  3.4 0.0 copy-start.5
  3.4 0.8 pack.1
  4.3 6.9 %collective-permute-start.1 = (bf16[16,2,128,128]{3,2,1,0:T(8,128)(2,1)S(1)}, bf16[16,2,128,128]{3,2,1,0:T(8,128)(2,1)S(1)}, u32[]{:S(2)}, u32[]{:S(2)}) collective-permute-start(bf16[16,2,128,128]{3,2,1,0:T(8,128)(2,1)S(1)} %get-tuple-element.49), channel_id=1, source_target_pairs={{2,0},{4,2},{6,4},{8,6},{10,8},{12,10},{14,12},{16,14},{18,16},{20... | collective-permute-start | bytes 3145736 | tf_op jit(solution)/shard_map/ppermute | solution.py:54
  11.2 1.9 %collective-permute-start = (bf16[16,2,128,128]{3,2,1,0:T(8,128)(2,1)S(1)}, bf16[16,2,128,128]{3,2,1,0:T(8,128)(2,1)S(1)}, u32[]{:S(2)}, u32[]{:S(2)}) collective-permute-start(bf16[16,2,128,128]{3,2,1,0:T(8,128)(2,1)S(1)} %get-tuple-element.49), channel_id=1, source_target_pairs={{0,2},{2,4},{4,6},{6,8},{8,10},{10,12},{12,14},{14,16},{16,18},{18... | collective-permute-start | bytes 3145736 | tf_op jit(solution)/shard_map/ppermute | solution.py:54
  13.1 0.0 copy-done.5
  13.1 7.3 %forward_local.1 = (f32[16,128,128]{2,1,0:T(8,128)S(1)}, f32[16,128,128]{2,1,0:T(8,128)S(1)}, f32[16,128,128]{2,1,0:T(8,128)S(1)}) custom-call(bf16[16,128,128]{2,1,0:T(8,128)(2,1)S(1)} %bitcast.22, bf16[16,128,128]{2,1,0:T(8,128)(2,1)S(1)} %bitcast.17, bf16[16,128,128]{2,1,0:T(8,128)(2,1)S(1)} %bitcast.20), custom_call_target="tpu_custom_call" | custom-call | flops 2147483648 | bytes 5242880 | tf_op jit(solution)/shard_map/forward_local/pallas_call | solution.py:215
  20.5 0.0 copy-start.9
  20.5 1.0 copy-done.9
  21.4 12.2 %collective-permute-done.1.refs_7_.refs_1_ = bf16[16,2,128,128]{3,2,1,0:T(8,128)(2,1)S(1)} collective-permute-done((bf16[16,2,128,128]{3,2,1,0:T(8,128)(2,1)S(1)}, bf16[16,2,128,128]{3,2,1,0:T(8,128)(2,1)S(1)}, u32[]{:S(2)}, u32[]{:S(2)}) %collective-permute-start.1) | collective-permute-done | bytes 1048608 | tf_op jit(solution)/shard_map/ppermute | solution.py:54
  33.6 8.3 %collective-permute-done.refs_6_.refs_0_ = bf16[16,2,128,128]{3,2,1,0:T(8,128)(2,1)S(1)} collective-permute-done((bf16[16,2,128,128]{3,2,1,0:T(8,128)(2,1)S(1)}, bf16[16,2,128,128]{3,2,1,0:T(8,128)(2,1)S(1)}, u32[]{:S(2)}, u32[]{:S(2)}) %collective-permute-start) | collective-permute-done | bytes 1048608 | tf_op jit(solution)/shard_map/ppermute | solution.py:54
  41.9 1.0 hand_on.1
  43.0 0.0 copy-done.7
  43.0 0.0 copy-done.11
  43.0 1.9 %collective-permute-start.2 = (bf16[8,2,128,128]{3,2,1,0:T(8,128)(2,1)}, bf16[8,2,128,128]{3,2,1,0:T(8,128)(2,1)S(1)}, u32[]{:S(2)}, u32[]{:S(2)}) collective-permute-start(bf16[8,2,128,128]{3,2,1,0:T(8,128)(2,1)} %get-tuple-element.58), channel_id=1, source_target_pairs={{0,2},{2,4},{4,6},{6,8},{8,10},{10,12},{12,14},{14,16},{16,18},{18... | collective-permute-start | bytes 1572872 | tf_op jit(solution)/shard_map/ppermute | solution.py:54
  44.9 8.1 %collective-permute-start.3 = (bf16[8,2,128,128]{3,2,1,0:T(8,128)(2,1)}, bf16[8,2,128,128]{3,2,1,0:T(8,128)(2,1)}, u32[]{:S(2)}, u32[]{:S(2)}) collective-permute-start(bf16[8,2,128,128]{3,2,1,0:T(8,128)(2,1)} %get-tuple-element.59), channel_id=1, source_target_pairs={{2,0},{4,2},{6,4},{8,6},{10,8},{12,10},{14,12},{16,14},{18,16},{20... | collective-permute-start | bytes 1572872 | tf_op jit(solution)/shard_map/ppermute | solution.py:54
  53.0 1.9 %collective-permute-start.7 = (bf16[2,2,128,128]{3,2,1,0:T(8,128)(2,1)S(1)}, bf16[2,2,128,128]{3,2,1,0:T(8,128)(2,1)}, u32[]{:S(2)}, u32[]{:S(2)}) collective-permute-start(bf16[2,2,128,128]{3,2,1,0:T(8,128)(2,1)S(1)} %get-tuple-element.61), channel_id=1, source_target_pairs={{16,0},{18,2},{20,4},{22,6},{24,8},{26,10},{28,12},{30,14},{32,16}... | collective-permute-start | bytes 393224 | tf_op jit(solution)/shard_map/ppermute | solution.py:54
  55.0 1.9 %collective-permute-start.5 = (bf16[4,2,128,128]{3,2,1,0:T(8,128)(2,1)}, bf16[4,2,128,128]{3,2,1,0:T(8,128)(2,1)S(1)}, u32[]{:S(2)}, u32[]{:S(2)}) collective-permute-start(bf16[4,2,128,128]{3,2,1,0:T(8,128)(2,1)} %get-tuple-element.60), channel_id=1, source_target_pairs={{8,0},{10,2},{12,4},{14,6},{16,8},{18,10},{20,12},{22,14},{24,16},... | collective-permute-start | bytes 786440 | tf_op jit(solution)/shard_map/ppermute | solution.py:54
  56.9 3.9 %collective-permute-start.4 = (bf16[4,2,128,128]{3,2,1,0:T(8,128)(2,1)}, bf16[4,2,128,128]{3,2,1,0:T(8,128)(2,1)}, u32[]{:S(2)}, u32[]{:S(2)}) collective-permute-start(bf16[4,2,128,128]{3,2,1,0:T(8,128)(2,1)} %get-tuple-element.60), channel_id=1, source_target_pairs={{0,8},{2,10},{4,12},{6,14},{8,16},{10,18},{12,20},{14,22},{16,24},... | collective-permute-start | bytes 786440 | tf_op jit(solution)/shard_map/ppermute | solution.py:54
  60.9 0.1 stack.35.refs_1_
  61.0 0.5 collective-permute-done.7.refs_11_.refs_9_
  61.5 5.6 %collective-permute-start.6 = (bf16[2,2,128,128]{3,2,1,0:T(8,128)(2,1)S(1)}, bf16[2,2,128,128]{3,2,1,0:T(8,128)(2,1)S(1)}, u32[]{:S(2)}, u32[]{:S(2)}) collective-permute-start(bf16[2,2,128,128]{3,2,1,0:T(8,128)(2,1)S(1)} %get-tuple-element.61), channel_id=1, source_target_pairs={{0,16},{2,18},{4,20},{6,22},{8,24},{10,26},{12,28},{14,30},{16,32}... | collective-permute-start | bytes 393224 | tf_op jit(solution)/shard_map/ppermute | solution.py:54
  67.1 0.0 copy-start.8
  67.1 1.2 copy-done.8
  68.3 1.2 copy-done.10
  69.5 1.2 copy-done.12
  70.8 8.7 %forward_far.2 = (f32[16,128,128]{2,1,0:T(8,128)S(1)}, f32[16,128,128]{2,1,0:T(8,128)S(1)}, f32[16,128,128]{2,1,0:T(8,128)S(1)}) custom-call(s32[16,30]{1,0:T(8,128)S(1)} %get-tuple-element.44.refs_0_, f32[10]{0:T(128)S(1)} %stack.35.refs_1_, bf16[16,128,128]{2,1,0:T(8,128)(2,1)S(1)} %bitcast.23, f32[16,128,128]{2,1,0:T(8,128)S(1)} %copy-done.8, ...), custom_call_target="tpu_custom_call" | custom-call | flops 2147483648 | bytes 8388608 | tf_op jit(solution)/shard_map/forward_far/pallas_call | solution.py:297
  79.4 0.0 collective-permute-done.6.refs_10_.refs_8_
  79.4 0.0 collective-permute-done.5.refs_9_
  79.4 0.0 collective-permute-done.4.refs_8_
  79.5 0.0 collective-permute-done.2.refs_6_
  79.5 0.0 collective-permute-done.3.refs_7_
  79.5 0.0 copy-done.6
  79.5 10.0 %forward_far.3 = (bf16[16,128,128]{2,1,0:T(8,128)(2,1)}, f32[16,128,128]{2,1,0:T(8,128)S(1)}, f32[16,128,128]{2,1,0:T(8,128)S(1)}) custom-call(s32[16,30]{1,0:T(8,128)S(1)} %get-tuple-element.44.refs_0_, f32[10]{0:T(128)S(1)} %stack.35.refs_1_, bf16[16,128,128]{2,1,0:T(8,128)(2,1)S(1)} %bitcast.24, f32[16,128,128]{2,1,0:T(8,128)S(1)} %get-tuple-element.55.refs_3_, ...), custom_call_target="tpu_custom_call" | custom-call | flops 1879048192 | bytes 8388608 | tf_op jit(solution)/shard_map/forward_far/pallas_call | solution.py:297
  89.4 9.9 %backward_far.2 = (f32[16,128,128]{2,1,0:T(8,128)S(1)}, bf16[8,2,128,128]{3,2,1,0:T(8,128)(2,1)S(1)}, bf16[8,2,128,128]{3,2,1,0:T(8,128)(2,1)S(1)}, bf16[2,2,128...) custom-call(s32[16,30]{1,0:T(8,128)S(1)} %get-tuple-element.44.refs_0_, f32[10]{0:T(128)S(1)} %stack.35.refs_1_, ...), custom_call_target="tpu_custom_call" | custom-call | flops 3355443200 | bytes 8388608 | tf_op jit(solution)/shard_map/backward_far/pallas_call | solution.py:373
  99.3 6.9 %collective-permute-start.10 = (bf16[2,2,128,128]{3,2,1,0:T(8,128)(2,1)S(1)}, bf16[2,2,128,128]{3,2,1,0:T(8,128)(2,1)S(1)}, u32[]{:S(2)}, u32[]{:S(2)}) collective-permute-start(bf16[2,2,128,128]{3,2,1,0:T(8,128)(2,1)S(1)} %get-tuple-element.76), channel_id=1, source_target_pairs={{8,0},{10,2},{12,4},{14,6},{16,8},{18,10},{20,12},{22,14},{24,16},... | collective-permute-start | bytes 393224 | tf_op jit(solution)/shard_map/ppermute | solution.py:54
  106.2 1.9 %collective-permute-start.11 = (bf16[2,2,128,128]{3,2,1,0:T(8,128)(2,1)S(1)}, bf16[2,2,128,128]{3,2,1,0:T(8,128)(2,1)S(1)}, u32[]{:S(2)}, u32[]{:S(2)}) collective-permute-start(bf16[2,2,128,128]{3,2,1,0:T(8,128)(2,1)S(1)} %get-tuple-element.77), channel_id=1, source_target_pairs={{0,8},{2,10},{4,12},{6,14},{8,16},{10,18},{12,20},{14,22},{16,24},... | collective-permute-start | bytes 393224 | tf_op jit(solution)/shard_map/ppermute | solution.py:54
  108.2 2.3 %collective-permute-start.8 = (bf16[8,2,128,128]{3,2,1,0:T(8,128)(2,1)S(1)}, bf16[8,2,128,128]{3,2,1,0:T(8,128)(2,1)S(1)}, u32[]{:S(2)}, u32[]{:S(2)}) collective-permute-start(bf16[8,2,128,128]{3,2,1,0:T(8,128)(2,1)S(1)} %get-tuple-element.74), channel_id=1, source_target_pairs={{2,0},{4,2},{6,4},{8,6},{10,8},{12,10},{14,12},{16,14},{18,16},{20... | collective-permute-start | bytes 1572872 | tf_op jit(solution)/shard_map/ppermute | solution.py:54
  110.5 3.7 %collective-permute-start.9 = (bf16[8,2,128,128]{3,2,1,0:T(8,128)(2,1)S(1)}, bf16[8,2,128,128]{3,2,1,0:T(8,128)(2,1)S(1)}, u32[]{:S(2)}, u32[]{:S(2)}) collective-permute-start(bf16[8,2,128,128]{3,2,1,0:T(8,128)(2,1)S(1)} %get-tuple-element.75), channel_id=1, source_target_pairs={{0,2},{2,4},{4,6},{6,8},{8,10},{10,12},{12,14},{14,16},{16,18},{18... | collective-permute-start | bytes 1572872 | tf_op jit(solution)/shard_map/ppermute | solution.py:54
  114.2 18.1 %backward_far.3 = (f32[16,128,128]{2,1,0:T(8,128)S(1)}, bf16[16,2,128,128]{3,2,1,0:T(8,128)(2,1)S(1)}, bf16[16,2,128,128]{3,2,1,0:T(8,128)(2,1)S(1)}, bf16[4,2,1...) custom-call(s32[16,30]{1,0:T(8,128)S(1)} %get-tuple-element.44.refs_0_, f32[10]{0:T(128)S(1)} %stack.35.refs_1_, ...), custom_call_target="tpu_custom_call" | custom-call | flops 6710886400 | bytes 8388608 | tf_op jit(solution)/shard_map/backward_far/pallas_call | solution.py:373
  132.3 0.0 collective-permute-done.10.refs_6_
  132.3 0.0 collective-permute-done.11.refs_7_
  132.3 0.0 collective-permute-done.8.refs_4_
  132.3 0.0 collective-permute-done.9.refs_5_
  132.4 0.0 copy-start.1
  132.4 0.0 copy-start.3
  132.4 0.3 merge.1
  132.7 6.5 %collective-permute-start.12 = (bf16[16,2,128,128]{3,2,1,0:T(8,128)(2,1)S(1)}, bf16[16,2,128,128]{3,2,1,0:T(8,128)(2,1)S(1)}, u32[]{:S(2)}, u32[]{:S(2)}) collective-permute-start(bf16[16,2,128,128]{3,2,1,0:T(8,128)(2,1)S(1)} %get-tuple-element.78), channel_id=1, source_target_pairs={{2,0},{4,2},{6,4},{8,6},{10,8},{12,10},{14,12},{16,14},{18,16},{20... | collective-permute-start | bytes 3145736 | tf_op jit(solution)/shard_map/ppermute | solution.py:54
  139.3 1.9 %collective-permute-start.13 = (bf16[16,2,128,128]{3,2,1,0:T(8,128)(2,1)S(1)}, bf16[16,2,128,128]{3,2,1,0:T(8,128)(2,1)S(1)}, u32[]{:S(2)}, u32[]{:S(2)}) collective-permute-start(bf16[16,2,128,128]{3,2,1,0:T(8,128)(2,1)S(1)} %get-tuple-element.79), channel_id=1, source_target_pairs={{0,2},{2,4},{4,6},{6,8},{8,10},{10,12},{12,14},{14,16},{16,18},{18... | collective-permute-start | bytes 3145736 | tf_op jit(solution)/shard_map/ppermute | solution.py:54
  141.2 3.5 %collective-permute-start.14 = (bf16[4,2,128,128]{3,2,1,0:T(8,128)(2,1)S(1)}, bf16[4,2,128,128]{3,2,1,0:T(8,128)(2,1)S(1)}, u32[]{:S(2)}, u32[]{:S(2)}) collective-permute-start(bf16[4,2,128,128]{3,2,1,0:T(8,128)(2,1)S(1)} %get-tuple-element.80), channel_id=1, source_target_pairs={{8,0},{10,2},{12,4},{14,6},{16,8},{18,10},{20,12},{22,14},{24,16},... | collective-permute-start | bytes 786440 | tf_op jit(solution)/shard_map/ppermute | solution.py:54
  144.7 2.5 %collective-permute-start.15 = (bf16[4,2,128,128]{3,2,1,0:T(8,128)(2,1)S(1)}, bf16[4,2,128,128]{3,2,1,0:T(8,128)(2,1)S(1)}, u32[]{:S(2)}, u32[]{:S(2)}) collective-permute-start(bf16[4,2,128,128]{3,2,1,0:T(8,128)(2,1)S(1)} %get-tuple-element.81), channel_id=1, source_target_pairs={{0,8},{2,10},{4,12},{6,14},{8,16},{10,18},{12,20},{14,22},{16,24},... | collective-permute-start | bytes 786440 | tf_op jit(solution)/shard_map/ppermute | solution.py:54
  147.3 0.0 copy-done.1
  147.3 0.0 copy-done.3
  147.3 14.4 %backward_local.1 = (bf16[16,128,128]{2,1,0:T(8,128)(2,1)}, f32[16,128,128]{2,1,0:T(8,128)S(1)}, f32[16,128,128]{2,1,0:T(8,128)S(1)}) custom-call(bf16[16,128,128]{2,1,0:T(8,128)(2,1)S(1)} %bitcast.27, bf16[16,128,128]{2,1,0:T(8,128)(2,1)S(1)} %bitcast.31, f32[16,128,128]{2,1,0:T(8,128)S(1)} %get-tuple-element.63.refs_4_.lse_ref, ...), custom_call_target="tpu_custom_call" | custom-call | flops 5368709120 | bytes 8388608 | tf_op jit(solution)/shard_map/backward_local/pallas_call | solution.py:435
  161.7 4.2 %collective-permute-done.14.refs_2_ = bf16[4,2,128,128]{3,2,1,0:T(8,128)(2,1)S(1)} collective-permute-done((bf16[4,2,128,128]{3,2,1,0:T(8,128)(2,1)S(1)}, bf16[4,2,128,128]{3,2,1,0:T(8,128)(2,1)S(1)}, u32[]{:S(2)}, u32[]{:S(2)}) %collective-permute-start.14) | collective-permute-done | bytes 262176 | tf_op jit(solution)/shard_map/ppermute | solution.py:54
  165.9 0.0 collective-permute-done.15.refs_3_
  165.9 0.0 collective-permute-done.12.refs_0_
  165.9 7.7 %collective-permute-done.13.refs_1_ = bf16[16,2,128,128]{3,2,1,0:T(8,128)(2,1)S(1)} collective-permute-done((bf16[16,2,128,128]{3,2,1,0:T(8,128)(2,1)S(1)}, bf16[16,2,128,128]{3,2,1,0:T(8,128)(2,1)S(1)}, u32[]{:S(2)}, u32[]{:S(2)}) %collective-permute-start.13) | collective-permute-done | bytes 1048608 | tf_op jit(solution)/shard_map/ppermute | solution.py:54
  173.6 1.4 finish.1
  (6 shorter events, 0.0 us)
Async XLA Ops:
  0.6 1.0 copy-start
  1.7 1.0 copy-start.2
  2.7 0.7 copy-start.4
  3.4 9.7 %copy-start.5 = (bf16[2048,128]{1,0:T(8,128)(2,1)S(1)}, bf16[2048,128]{1,0:T(8,128)(2,1)}, u32[]{:S(2)}) copy-start(bf16[2048,128]{1,0:T(8,128)(2,1)} %param.5) | copy-start | bytes 1572868
  4.3 29.3 %collective-permute-start.1 = (bf16[16,2,128,128]{3,2,1,0:T(8,128)(2,1)S(1)}, bf16[16,2,128,128]{3,2,1,0:T(8,128)(2,1)S(1)}, u32[]{:S(2)}, u32[]{:S(2)}) collective-permute-start(bf16[16,2,128,128]{3,2,1,0:T(8,128)(2,1)S(1)} %get-tuple-element.49), channel_id=1, source_target_pairs={{2,0},{4,2},{6,4},{8,6},{10,8},{12,10},{14,12},{16,14},{18,16},{20... | collective-permute-start | bytes 3145736 | tf_op jit(solution)/shard_map/ppermute | solution.py:54
  11.2 30.7 %collective-permute-start = (bf16[16,2,128,128]{3,2,1,0:T(8,128)(2,1)S(1)}, bf16[16,2,128,128]{3,2,1,0:T(8,128)(2,1)S(1)}, u32[]{:S(2)}, u32[]{:S(2)}) collective-permute-start(bf16[16,2,128,128]{3,2,1,0:T(8,128)(2,1)S(1)} %get-tuple-element.49), channel_id=1, source_target_pairs={{0,2},{2,4},{4,6},{6,8},{8,10},{10,12},{12,14},{14,16},{16,18},{18... | collective-permute-start | bytes 3145736 | tf_op jit(solution)/shard_map/ppermute | solution.py:54
  20.5 1.0 copy-start.9
  21.4 21.5 %copy-start.7 = (f32[16,128,128]{2,1,0:T(8,128)}, f32[16,128,128]{2,1,0:T(8,128)S(1)}, u32[]{:S(2)}) copy-start(f32[16,128,128]{2,1,0:T(8,128)S(1)} %get-tuple-element.50.refs_3_) | copy-start | bytes 3145732
  21.4 21.5 %copy-start.11 = (f32[16,128,128]{2,1,0:T(8,128)}, f32[16,128,128]{2,1,0:T(8,128)S(1)}, u32[]{:S(2)}) copy-start(f32[16,128,128]{2,1,0:T(8,128)S(1)} %get-tuple-element.52.refs_5_) | copy-start | bytes 3145732
  43.0 36.5 %collective-permute-start.2 = (bf16[8,2,128,128]{3,2,1,0:T(8,128)(2,1)}, bf16[8,2,128,128]{3,2,1,0:T(8,128)(2,1)S(1)}, u32[]{:S(2)}, u32[]{:S(2)}) collective-permute-start(bf16[8,2,128,128]{3,2,1,0:T(8,128)(2,1)} %get-tuple-element.58), channel_id=1, source_target_pairs={{0,2},{2,4},{4,6},{6,8},{8,10},{10,12},{12,14},{14,16},{16,18},{18... | collective-permute-start | bytes 1572872 | tf_op jit(solution)/shard_map/ppermute | solution.py:54
  44.9 34.6 %collective-permute-start.3 = (bf16[8,2,128,128]{3,2,1,0:T(8,128)(2,1)}, bf16[8,2,128,128]{3,2,1,0:T(8,128)(2,1)}, u32[]{:S(2)}, u32[]{:S(2)}) collective-permute-start(bf16[8,2,128,128]{3,2,1,0:T(8,128)(2,1)} %get-tuple-element.59), channel_id=1, source_target_pairs={{2,0},{4,2},{6,4},{8,6},{10,8},{12,10},{14,12},{16,14},{18,16},{20... | collective-permute-start | bytes 1572872 | tf_op jit(solution)/shard_map/ppermute | solution.py:54
  53.0 8.5 %collective-permute-start.7 = (bf16[2,2,128,128]{3,2,1,0:T(8,128)(2,1)S(1)}, bf16[2,2,128,128]{3,2,1,0:T(8,128)(2,1)}, u32[]{:S(2)}, u32[]{:S(2)}) collective-permute-start(bf16[2,2,128,128]{3,2,1,0:T(8,128)(2,1)S(1)} %get-tuple-element.61), channel_id=1, source_target_pairs={{16,0},{18,2},{20,4},{22,6},{24,8},{26,10},{28,12},{30,14},{32,16}... | collective-permute-start | bytes 393224 | tf_op jit(solution)/shard_map/ppermute | solution.py:54
  55.0 24.5 %collective-permute-start.5 = (bf16[4,2,128,128]{3,2,1,0:T(8,128)(2,1)}, bf16[4,2,128,128]{3,2,1,0:T(8,128)(2,1)S(1)}, u32[]{:S(2)}, u32[]{:S(2)}) collective-permute-start(bf16[4,2,128,128]{3,2,1,0:T(8,128)(2,1)} %get-tuple-element.60), channel_id=1, source_target_pairs={{8,0},{10,2},{12,4},{14,6},{16,8},{18,10},{20,12},{22,14},{24,16},... | collective-permute-start | bytes 786440 | tf_op jit(solution)/shard_map/ppermute | solution.py:54
  56.9 22.5 %collective-permute-start.4 = (bf16[4,2,128,128]{3,2,1,0:T(8,128)(2,1)}, bf16[4,2,128,128]{3,2,1,0:T(8,128)(2,1)}, u32[]{:S(2)}, u32[]{:S(2)}) collective-permute-start(bf16[4,2,128,128]{3,2,1,0:T(8,128)(2,1)} %get-tuple-element.60), channel_id=1, source_target_pairs={{0,8},{2,10},{4,12},{6,14},{8,16},{10,18},{12,20},{14,22},{16,24},... | collective-permute-start | bytes 786440 | tf_op jit(solution)/shard_map/ppermute | solution.py:54
  61.5 17.9 %collective-permute-start.6 = (bf16[2,2,128,128]{3,2,1,0:T(8,128)(2,1)S(1)}, bf16[2,2,128,128]{3,2,1,0:T(8,128)(2,1)S(1)}, u32[]{:S(2)}, u32[]{:S(2)}) collective-permute-start(bf16[2,2,128,128]{3,2,1,0:T(8,128)(2,1)S(1)} %get-tuple-element.61), channel_id=1, source_target_pairs={{0,16},{2,18},{4,20},{6,22},{8,24},{10,26},{12,28},{14,30},{16,32}... | collective-permute-start | bytes 393224 | tf_op jit(solution)/shard_map/ppermute | solution.py:54
  67.1 1.2 copy-start.8
  68.3 1.2 copy-start.10
  69.5 1.2 copy-start.12
  70.8 8.7 %copy-start.6 = (bf16[2048,128]{1,0:T(8,128)(2,1)S(1)}, bf16[2048,128]{1,0:T(8,128)(2,1)}, u32[]{:S(2)}) copy-start(bf16[2048,128]{1,0:T(8,128)(2,1)} %param.8) | copy-start | bytes 1572868
  99.3 33.0 %collective-permute-start.10 = (bf16[2,2,128,128]{3,2,1,0:T(8,128)(2,1)S(1)}, bf16[2,2,128,128]{3,2,1,0:T(8,128)(2,1)S(1)}, u32[]{:S(2)}, u32[]{:S(2)}) collective-permute-start(bf16[2,2,128,128]{3,2,1,0:T(8,128)(2,1)S(1)} %get-tuple-element.76), channel_id=1, source_target_pairs={{8,0},{10,2},{12,4},{14,6},{16,8},{18,10},{20,12},{22,14},{24,16},... | collective-permute-start | bytes 393224 | tf_op jit(solution)/shard_map/ppermute | solution.py:54
  106.2 26.1 %collective-permute-start.11 = (bf16[2,2,128,128]{3,2,1,0:T(8,128)(2,1)S(1)}, bf16[2,2,128,128]{3,2,1,0:T(8,128)(2,1)S(1)}, u32[]{:S(2)}, u32[]{:S(2)}) collective-permute-start(bf16[2,2,128,128]{3,2,1,0:T(8,128)(2,1)S(1)} %get-tuple-element.77), channel_id=1, source_target_pairs={{0,8},{2,10},{4,12},{6,14},{8,16},{10,18},{12,20},{14,22},{16,24},... | collective-permute-start | bytes 393224 | tf_op jit(solution)/shard_map/ppermute | solution.py:54
  108.2 24.2 %collective-permute-start.8 = (bf16[8,2,128,128]{3,2,1,0:T(8,128)(2,1)S(1)}, bf16[8,2,128,128]{3,2,1,0:T(8,128)(2,1)S(1)}, u32[]{:S(2)}, u32[]{:S(2)}) collective-permute-start(bf16[8,2,128,128]{3,2,1,0:T(8,128)(2,1)S(1)} %get-tuple-element.74), channel_id=1, source_target_pairs={{2,0},{4,2},{6,4},{8,6},{10,8},{12,10},{14,12},{16,14},{18,16},{20... | collective-permute-start | bytes 1572872 | tf_op jit(solution)/shard_map/ppermute | solution.py:54
  110.5 21.9 %collective-permute-start.9 = (bf16[8,2,128,128]{3,2,1,0:T(8,128)(2,1)S(1)}, bf16[8,2,128,128]{3,2,1,0:T(8,128)(2,1)S(1)}, u32[]{:S(2)}, u32[]{:S(2)}) collective-permute-start(bf16[8,2,128,128]{3,2,1,0:T(8,128)(2,1)S(1)} %get-tuple-element.75), channel_id=1, source_target_pairs={{0,2},{2,4},{4,6},{6,8},{8,10},{10,12},{12,14},{14,16},{16,18},{18... | collective-permute-start | bytes 1572872 | tf_op jit(solution)/shard_map/ppermute | solution.py:54
  132.4 14.9 %copy-start.1 = (bf16[2048,128]{1,0:T(8,128)(2,1)S(1)}, bf16[2048,128]{1,0:T(8,128)(2,1)}, u32[]{:S(2)}) copy-start(bf16[2048,128]{1,0:T(8,128)(2,1)} %param.6) | copy-start | bytes 1572868
  132.4 14.9 %copy-start.3 = (bf16[2048,128]{1,0:T(8,128)(2,1)S(1)}, bf16[2048,128]{1,0:T(8,128)(2,1)}, u32[]{:S(2)}) copy-start(bf16[2048,128]{1,0:T(8,128)(2,1)} %param.7) | copy-start | bytes 1572868
  132.7 33.1 %collective-permute-start.12 = (bf16[16,2,128,128]{3,2,1,0:T(8,128)(2,1)S(1)}, bf16[16,2,128,128]{3,2,1,0:T(8,128)(2,1)S(1)}, u32[]{:S(2)}, u32[]{:S(2)}) collective-permute-start(bf16[16,2,128,128]{3,2,1,0:T(8,128)(2,1)S(1)} %get-tuple-element.78), channel_id=1, source_target_pairs={{2,0},{4,2},{6,4},{8,6},{10,8},{12,10},{14,12},{16,14},{18,16},{20... | collective-permute-start | bytes 3145736 | tf_op jit(solution)/shard_map/ppermute | solution.py:54
  139.3 34.3 %collective-permute-start.13 = (bf16[16,2,128,128]{3,2,1,0:T(8,128)(2,1)S(1)}, bf16[16,2,128,128]{3,2,1,0:T(8,128)(2,1)S(1)}, u32[]{:S(2)}, u32[]{:S(2)}) collective-permute-start(bf16[16,2,128,128]{3,2,1,0:T(8,128)(2,1)S(1)} %get-tuple-element.79), channel_id=1, source_target_pairs={{0,2},{2,4},{4,6},{6,8},{8,10},{10,12},{12,14},{14,16},{16,18},{18... | collective-permute-start | bytes 3145736 | tf_op jit(solution)/shard_map/ppermute | solution.py:54
  141.2 24.7 %collective-permute-start.14 = (bf16[4,2,128,128]{3,2,1,0:T(8,128)(2,1)S(1)}, bf16[4,2,128,128]{3,2,1,0:T(8,128)(2,1)S(1)}, u32[]{:S(2)}, u32[]{:S(2)}) collective-permute-start(bf16[4,2,128,128]{3,2,1,0:T(8,128)(2,1)S(1)} %get-tuple-element.80), channel_id=1, source_target_pairs={{8,0},{10,2},{12,4},{14,6},{16,8},{18,10},{20,12},{22,14},{24,16},... | collective-permute-start | bytes 786440 | tf_op jit(solution)/shard_map/ppermute | solution.py:54
  144.7 21.1 %collective-permute-start.15 = (bf16[4,2,128,128]{3,2,1,0:T(8,128)(2,1)S(1)}, bf16[4,2,128,128]{3,2,1,0:T(8,128)(2,1)S(1)}, u32[]{:S(2)}, u32[]{:S(2)}) collective-permute-start(bf16[4,2,128,128]{3,2,1,0:T(8,128)(2,1)S(1)} %get-tuple-element.81), channel_id=1, source_target_pairs={{0,8},{2,10},{4,12},{6,14},{8,16},{10,18},{12,20},{14,22},{16,24},... | collective-permute-start | bytes 786440 | tf_op jit(solution)/shard_map/ppermute | solution.py:54

commit v4 on v3

--- a/solution.py
+++ b/solution.py
@@ -516,9 +516,14 @@
 
     dq, *parts = back(None, 2, 4)
     hop = [shift(part, -by) for part, (band, side, by) in zip(parts, hops)]
-    dq, *parts = back(dq, 1, 3)
-    parts = merge(parts, hop)
-    returned = [shift(part, -by) for part, (band, side, by) in zip(parts, hops)]
+    returned = []
+    for n, band in ((0, 1), (2, 3)):
+        dq, *parts = back(dq, band)
+        parts, hop = lax.optimization_barrier((parts, hop))
+        parts = merge(parts, hop[n : n + 2])
+        returned += [
+            shift(part, -by) for part, (own, side, by) in zip(parts, hops[n : n + 2])
+        ]
     dq, dk, dv = backward_local(q, g, lse, delta, k, v, dq)
     gk, gv = finish(dk, dv, returned)
     flat = (NBLK * BLOCK, HEAD)

time: 176 us -> 170 us (0.966)
  waiting for transfers between devices: 32.9 us -> 25.3 us
    ppermute x16, waiting for transfers between devices: 32.9 us -> 25.3 us  [shift(): return lax.ppermute(value, 'seq', [(s, s + by) for s in range(first, last)])]
    pallas_call x2 -> x3, Pallas kernels: 28 us -> 30 us  [backward_far(): pl.pallas_call(functools.partial(backward_far_kernel, group, dq is None),...]
  transfers between devices with their start and end apart: 16 -> 16, of which waited for: 5 -> 4; matrix products, arithmetic and copies ran while one was open for 0% -> 0% of each run, Pallas kernels for 28% -> 30%
where the time goes in v4:
time: 170 us; the launch traced here: 169 us
  Pallas kernels  73.5 us (43%)
  starting transfers between devices  61.7 us (36%)
  waiting for transfers between devices  25.3 us (15%)
  local copies, waits for them, and re-layouts  7.53 us (4%)
    ppermute x16, starting transfers between devices, shift(): return lax.ppermute(value, 'seq', [(s, s + by) for s in range(first, last)])  61.7 us
    pallas_call x3, Pallas kernels, backward_far(): pl.pallas_call(functools.partial(backward_far_kernel, group, dq is None),...  30 us
    ppermute x16, waiting for transfers between devices, shift(): return lax.ppermute(value, 'seq', [(s, s + by) for s in range(first, last)])  25.3 us
    pallas_call x2, Pallas kernels, forward_far(): pl.pallas_call(functools.partial(forward_far_kernel, group, last), out_sh...  18.6 us
    pallas_call x1, Pallas kernels, backward_local(): pl.pallas_call(backward_local_kernel, out_shape=(HALF, STAT, STAT), in_sp...  14 us
    unnamed x26, local copies, waits for them, and re-layouts  7.44 us
    pallas_call x1, Pallas kernels, forward_local(): pl.pallas_call(forward_local_kernel, out_shape=(STAT, STAT, STAT), in_spe...  7.32 us
  transfers between devices with their start and end apart: 16, of which 4 were waited for; matrix products, arithmetic and copies ran while one was open for 0% of the time, Pallas kernels for 30%

profile of v4, /device:TPU:96, one launch (start us, length us, event | category | flops | bytes accessed | tf_op | source)
XLA Modules:
  0.0 169.1 jit_solution(6085677872942504939)
XLA Ops:
  0.6 0.0 copy-start
  0.6 1.0 copy-done
  1.7 0.0 copy-start.2
  1.7 1.0 copy-done.2
  2.7 0.7 copy-done.4
  3.4 0.8 pack.1
  4.3 6.9 %collective-permute-start.1 = (bf16[16,2,128,128]{3,2,1,0:T(8,128)(2,1)S(1)}, bf16[16,2,128,128]{3,2,1,0:T(8,128)(2,1)S(1)}, u32[]{:S(2)}, u32[]{:S(2)}) collective-permute-start(bf16[16,2,128,128]{3,2,1,0:T(8,128)(2,1)S(1)} %get-tuple-element.60), channel_id=1, source_target_pairs={{2,0},{4,2},{6,4},{8,6},{10,8},{12,10},{14,12},{16,14},{18,16},{20... | collective-permute-start | bytes 3145736 | tf_op jit(solution)/shard_map/ppermute | solution.py:54
  11.2 1.9 %collective-permute-start = (bf16[16,2,128,128]{3,2,1,0:T(8,128)(2,1)S(1)}, bf16[16,2,128,128]{3,2,1,0:T(8,128)(2,1)S(1)}, u32[]{:S(2)}, u32[]{:S(2)}) collective-permute-start(bf16[16,2,128,128]{3,2,1,0:T(8,128)(2,1)S(1)} %get-tuple-element.60), channel_id=1, source_target_pairs={{0,2},{2,4},{4,6},{6,8},{8,10},{10,12},{12,14},{14,16},{16,18},{18... | collective-permute-start | bytes 3145736 | tf_op jit(solution)/shard_map/ppermute | solution.py:54
  13.1 0.0 copy-done.5
  13.1 7.3 %forward_local.1 = (f32[16,128,128]{2,1,0:T(8,128)S(1)}, f32[16,128,128]{2,1,0:T(8,128)S(1)}, f32[16,128,128]{2,1,0:T(8,128)S(1)}) custom-call(bf16[16,128,128]{2,1,0:T(8,128)(2,1)S(1)} %bitcast.22, bf16[16,128,128]{2,1,0:T(8,128)(2,1)S(1)} %bitcast.17, bf16[16,128,128]{2,1,0:T(8,128)(2,1)S(1)} %bitcast.20), custom_call_target="tpu_custom_call" | custom-call | flops 2147483648 | bytes 5242880 | tf_op jit(solution)/shard_map/forward_local/pallas_call | solution.py:215
  20.5 0.0 copy-start.9
  20.5 1.0 copy-done.9
  21.5 12.1 %collective-permute-done.1.refs_7_.refs_1_ = bf16[16,2,128,128]{3,2,1,0:T(8,128)(2,1)S(1)} collective-permute-done((bf16[16,2,128,128]{3,2,1,0:T(8,128)(2,1)S(1)}, bf16[16,2,128,128]{3,2,1,0:T(8,128)(2,1)S(1)}, u32[]{:S(2)}, u32[]{:S(2)}) %collective-permute-start.1) | collective-permute-done | bytes 1048608 | tf_op jit(solution)/shard_map/ppermute | solution.py:54
  33.6 8.3 %collective-permute-done.refs_6_.refs_0_ = bf16[16,2,128,128]{3,2,1,0:T(8,128)(2,1)S(1)} collective-permute-done((bf16[16,2,128,128]{3,2,1,0:T(8,128)(2,1)S(1)}, bf16[16,2,128,128]{3,2,1,0:T(8,128)(2,1)S(1)}, u32[]{:S(2)}, u32[]{:S(2)}) %collective-permute-start) | collective-permute-done | bytes 1048608 | tf_op jit(solution)/shard_map/ppermute | solution.py:54
  41.9 1.0 hand_on.1
  43.0 0.0 copy-done.7
  43.0 0.0 copy-done.11
  43.0 1.9 %collective-permute-start.2 = (bf16[8,2,128,128]{3,2,1,0:T(8,128)(2,1)}, bf16[8,2,128,128]{3,2,1,0:T(8,128)(2,1)S(1)}, u32[]{:S(2)}, u32[]{:S(2)}) collective-permute-start(bf16[8,2,128,128]{3,2,1,0:T(8,128)(2,1)} %get-tuple-element.69), channel_id=1, source_target_pairs={{0,2},{2,4},{4,6},{6,8},{8,10},{10,12},{12,14},{14,16},{16,18},{18... | collective-permute-start | bytes 1572872 | tf_op jit(solution)/shard_map/ppermute | solution.py:54
  44.9 8.1 %collective-permute-start.3 = (bf16[8,2,128,128]{3,2,1,0:T(8,128)(2,1)}, bf16[8,2,128,128]{3,2,1,0:T(8,128)(2,1)}, u32[]{:S(2)}, u32[]{:S(2)}) collective-permute-start(bf16[8,2,128,128]{3,2,1,0:T(8,128)(2,1)} %get-tuple-element.70), channel_id=1, source_target_pairs={{2,0},{4,2},{6,4},{8,6},{10,8},{12,10},{14,12},{16,14},{18,16},{20... | collective-permute-start | bytes 1572872 | tf_op jit(solution)/shard_map/ppermute | solution.py:54
  53.0 1.9 %collective-permute-start.7 = (bf16[2,2,128,128]{3,2,1,0:T(8,128)(2,1)S(1)}, bf16[2,2,128,128]{3,2,1,0:T(8,128)(2,1)}, u32[]{:S(2)}, u32[]{:S(2)}) collective-permute-start(bf16[2,2,128,128]{3,2,1,0:T(8,128)(2,1)S(1)} %get-tuple-element.72), channel_id=1, source_target_pairs={{16,0},{18,2},{20,4},{22,6},{24,8},{26,10},{28,12},{30,14},{32,16}... | collective-permute-start | bytes 393224 | tf_op jit(solution)/shard_map/ppermute | solution.py:54
  55.0 1.9 %collective-permute-start.5 = (bf16[4,2,128,128]{3,2,1,0:T(8,128)(2,1)}, bf16[4,2,128,128]{3,2,1,0:T(8,128)(2,1)S(1)}, u32[]{:S(2)}, u32[]{:S(2)}) collective-permute-start(bf16[4,2,128,128]{3,2,1,0:T(8,128)(2,1)} %get-tuple-element.71), channel_id=1, source_target_pairs={{8,0},{10,2},{12,4},{14,6},{16,8},{18,10},{20,12},{22,14},{24,16},... | collective-permute-start | bytes 786440 | tf_op jit(solution)/shard_map/ppermute | solution.py:54
  56.9 3.9 %collective-permute-start.4 = (bf16[4,2,128,128]{3,2,1,0:T(8,128)(2,1)}, bf16[4,2,128,128]{3,2,1,0:T(8,128)(2,1)}, u32[]{:S(2)}, u32[]{:S(2)}) collective-permute-start(bf16[4,2,128,128]{3,2,1,0:T(8,128)(2,1)} %get-tuple-element.71), channel_id=1, source_target_pairs={{0,8},{2,10},{4,12},{6,14},{8,16},{10,18},{12,20},{14,22},{16,24},... | collective-permute-start | bytes 786440 | tf_op jit(solution)/shard_map/ppermute | solution.py:54
  60.9 0.1 stack.35.refs_1_
  61.0 0.5 collective-permute-done.7.refs_11_.refs_9_
  61.5 5.5 %collective-permute-start.6 = (bf16[2,2,128,128]{3,2,1,0:T(8,128)(2,1)S(1)}, bf16[2,2,128,128]{3,2,1,0:T(8,128)(2,1)S(1)}, u32[]{:S(2)}, u32[]{:S(2)}) collective-permute-start(bf16[2,2,128,128]{3,2,1,0:T(8,128)(2,1)S(1)} %get-tuple-element.72), channel_id=1, source_target_pairs={{0,16},{2,18},{4,20},{6,22},{8,24},{10,26},{12,28},{14,30},{16,32}... | collective-permute-start | bytes 393224 | tf_op jit(solution)/shard_map/ppermute | solution.py:54
  67.1 0.0 copy-start.8
  67.1 1.2 copy-done.8
  68.3 1.2 copy-done.10
  69.5 1.2 copy-done.12
  70.8 8.7 %forward_far.2 = (f32[16,128,128]{2,1,0:T(8,128)S(1)}, f32[16,128,128]{2,1,0:T(8,128)S(1)}, f32[16,128,128]{2,1,0:T(8,128)S(1)}) custom-call(s32[16,30]{1,0:T(8,128)S(1)} %get-tuple-element.55.refs_0_, f32[10]{0:T(128)S(1)} %stack.35.refs_1_, bf16[16,128,128]{2,1,0:T(8,128)(2,1)S(1)} %bitcast.23, f32[16,128,128]{2,1,0:T(8,128)S(1)} %copy-done.8, ...), custom_call_target="tpu_custom_call" | custom-call | flops 2147483648 | bytes 8388608 | tf_op jit(solution)/shard_map/forward_far/pallas_call | solution.py:297
  79.4 0.0 collective-permute-done.6.refs_10_.refs_8_
  79.4 0.0 collective-permute-done.5.refs_9_.refs_7_
  79.4 0.0 collective-permute-done.4.refs_8_.refs_6_
  79.4 0.0 collective-permute-done.2.refs_6_
  79.5 0.0 collective-permute-done.3.refs_7_
  79.5 0.0 copy-done.6
  79.5 9.9 %forward_far.3 = (bf16[16,128,128]{2,1,0:T(8,128)(2,1)}, f32[16,128,128]{2,1,0:T(8,128)S(1)}, f32[16,128,128]{2,1,0:T(8,128)S(1)}) custom-call(s32[16,30]{1,0:T(8,128)S(1)} %get-tuple-element.55.refs_0_, f32[10]{0:T(128)S(1)} %stack.35.refs_1_, bf16[16,128,128]{2,1,0:T(8,128)(2,1)S(1)} %bitcast.24, f32[16,128,128]{2,1,0:T(8,128)S(1)} %get-tuple-element.66.refs_3_, ...), custom_call_target="tpu_custom_call" | custom-call | flops 1879048192 | bytes 8388608 | tf_op jit(solution)/shard_map/forward_far/pallas_call | solution.py:297
  89.4 9.6 %backward_far.3 = (f32[16,128,128]{2,1,0:T(8,128)S(1)}, bf16[8,2,128,128]{3,2,1,0:T(8,128)(2,1)S(1)}, bf16[8,2,128,128]{3,2,1,0:T(8,128)(2,1)S(1)}, bf16[2,2,128...) custom-call(s32[16,30]{1,0:T(8,128)S(1)} %get-tuple-element.55.refs_0_, f32[10]{0:T(128)S(1)} %stack.35.refs_1_, ...), custom_call_target="tpu_custom_call" | custom-call | flops 3355443200 | bytes 8388608 | tf_op jit(solution)/shard_map/backward_far/pallas_call | solution.py:373
  99.1 3.2 %collective-permute-start.8 = (bf16[8,2,128,128]{3,2,1,0:T(8,128)(2,1)S(1)}, bf16[8,2,128,128]{3,2,1,0:T(8,128)(2,1)S(1)}, u32[]{:S(2)}, u32[]{:S(2)}) collective-permute-start(bf16[8,2,128,128]{3,2,1,0:T(8,128)(2,1)S(1)} %get-tuple-element.84), channel_id=1, source_target_pairs={{2,0},{4,2},{6,4},{8,6},{10,8},{12,10},{14,12},{16,14},{18,16},{20... | collective-permute-start | bytes 1572872 | tf_op jit(solution)/shard_map/ppermute | solution.py:54
  102.3 2.6 %collective-permute-start.9 = (bf16[8,2,128,128]{3,2,1,0:T(8,128)(2,1)S(1)}, bf16[8,2,128,128]{3,2,1,0:T(8,128)(2,1)S(1)}, u32[]{:S(2)}, u32[]{:S(2)}) collective-permute-start(bf16[8,2,128,128]{3,2,1,0:T(8,128)(2,1)S(1)} %get-tuple-element.85), channel_id=1, source_target_pairs={{0,2},{2,4},{4,6},{6,8},{8,10},{10,12},{12,14},{14,16},{16,18},{18... | collective-permute-start | bytes 1572872 | tf_op jit(solution)/shard_map/ppermute | solution.py:54
  104.9 6.9 %collective-permute-start.10 = (bf16[2,2,128,128]{3,2,1,0:T(8,128)(2,1)S(1)}, bf16[2,2,128,128]{3,2,1,0:T(8,128)(2,1)S(1)}, u32[]{:S(2)}, u32[]{:S(2)}) collective-permute-start(bf16[2,2,128,128]{3,2,1,0:T(8,128)(2,1)S(1)} %get-tuple-element.86), channel_id=1, source_target_pairs={{8,0},{10,2},{12,4},{14,6},{16,8},{18,10},{20,12},{22,14},{24,16},... | collective-permute-start | bytes 393224 | tf_op jit(solution)/shard_map/ppermute | solution.py:54
  111.9 2.1 %collective-permute-start.11 = (bf16[2,2,128,128]{3,2,1,0:T(8,128)(2,1)S(1)}, bf16[2,2,128,128]{3,2,1,0:T(8,128)(2,1)S(1)}, u32[]{:S(2)}, u32[]{:S(2)}) collective-permute-start(bf16[2,2,128,128]{3,2,1,0:T(8,128)(2,1)S(1)} %get-tuple-element.87), channel_id=1, source_target_pairs={{0,8},{2,10},{4,12},{6,14},{8,16},{10,18},{12,20},{14,22},{16,24},... | collective-permute-start | bytes 393224 | tf_op jit(solution)/shard_map/ppermute | solution.py:54
  114.0 15.3 %backward_far.4 = (f32[16,128,128]{2,1,0:T(8,128)S(1)}, bf16[16,2,128,128]{3,2,1,0:T(8,128)(2,1)S(1)}, bf16[16,2,128,128]{3,2,1,0:T(8,128)(2,1)S(1)}) custom-call(s32[16,30]{1,0:T(8,128)S(1)} %get-tuple-element.55.refs_0_, f32[10]{0:T(128)S(1)} %stack.35.refs_1_, bf16[16,128,128]{2,1,0:T(8,128)(2,1)S(1)} %bitcast.26, bf16[16,128,128]{2,1,0:T(8,128)(2,1)S(1)} %bitcast.31, ...), custom_call_target="tpu_custom_call" | custom-call | flops 5368709120 | bytes 8388608 | tf_op jit(solution)/shard_map/backward_far/pallas_call | solution.py:373
  129.2 0.0 collective-permute-done.10.refs_2_
  129.2 0.0 collective-permute-done.11.refs_3_
  129.3 0.0 collective-permute-done.8.refs_2_
  129.3 0.0 collective-permute-done.9.refs_3_
  129.3 0.3 merge.2
  129.6 6.5 %collective-permute-start.12 = (bf16[16,2,128,128]{3,2,1,0:T(8,128)(2,1)S(1)}, bf16[16,2,128,128]{3,2,1,0:T(8,128)(2,1)S(1)}, u32[]{:S(2)}, u32[]{:S(2)}) collective-permute-start(bf16[16,2,128,128]{3,2,1,0:T(8,128)(2,1)S(1)} %get-tuple-element.92), channel_id=1, source_target_pairs={{2,0},{4,2},{6,4},{8,6},{10,8},{12,10},{14,12},{16,14},{18,16},{20... | collective-permute-start | bytes 3145736 | tf_op jit(solution)/shard_map/ppermute | solution.py:54
  136.1 1.9 %collective-permute-start.13 = (bf16[16,2,128,128]{3,2,1,0:T(8,128)(2,1)S(1)}, bf16[16,2,128,128]{3,2,1,0:T(8,128)(2,1)S(1)}, u32[]{:S(2)}, u32[]{:S(2)}) collective-permute-start(bf16[16,2,128,128]{3,2,1,0:T(8,128)(2,1)S(1)} %get-tuple-element.93), channel_id=1, source_target_pairs={{0,2},{2,4},{4,6},{6,8},{8,10},{10,12},{12,14},{14,16},{16,18},{18... | collective-permute-start | bytes 3145736 | tf_op jit(solution)/shard_map/ppermute | solution.py:54
  138.0 0.0 copy-start.3
  138.0 5.1 %backward_far.5 = (f32[16,128,128]{2,1,0:T(8,128)S(1)}, bf16[4,2,128,128]{3,2,1,0:T(8,128)(2,1)S(1)}, bf16[4,2,128,128]{3,2,1,0:T(8,128)(2,1)S(1)}) custom-call(s32[16,30]{1,0:T(8,128)S(1)} %get-tuple-element.55.refs_0_, f32[10]{0:T(128)S(1)} %stack.35.refs_1_, bf16[16,128,128]{2,1,0:T(8,128)(2,1)S(1)} %bitcast.27, bf16[16,128,128]{2,1,0:T(8,128)(2,1)S(1)} %bitcast.32, ...), custom_call_target="tpu_custom_call" | custom-call | flops 1342177280 | bytes 8388608 | tf_op jit(solution)/shard_map/backward_far/pallas_call | solution.py:373
  143.1 0.0 copy-start.1
  143.1 0.1 merge.3
  143.2 3.6 %collective-permute-start.14 = (bf16[4,2,128,128]{3,2,1,0:T(8,128)(2,1)S(1)}, bf16[4,2,128,128]{3,2,1,0:T(8,128)(2,1)S(1)}, u32[]{:S(2)}, u32[]{:S(2)}) collective-permute-start(bf16[4,2,128,128]{3,2,1,0:T(8,128)(2,1)S(1)} %get-tuple-element.102), channel_id=1, source_target_pairs={{8,0},{10,2},{12,4},{14,6},{16,8},{18,10},{20,12},{22,14},{24,16},... | collective-permute-start | bytes 786440 | tf_op jit(solution)/shard_map/ppermute | solution.py:54
  146.8 2.6 %collective-permute-start.15 = (bf16[4,2,128,128]{3,2,1,0:T(8,128)(2,1)S(1)}, bf16[4,2,128,128]{3,2,1,0:T(8,128)(2,1)S(1)}, u32[]{:S(2)}, u32[]{:S(2)}) collective-permute-start(bf16[4,2,128,128]{3,2,1,0:T(8,128)(2,1)S(1)} %get-tuple-element.103), channel_id=1, source_target_pairs={{0,8},{2,10},{4,12},{6,14},{8,16},{10,18},{12,20},{14,22},{16,24},... | collective-permute-start | bytes 786440 | tf_op jit(solution)/shard_map/ppermute | solution.py:54
  149.4 0.0 copy-done.3
  149.4 0.0 copy-done.1
  149.4 14.0 %backward_local.1 = (bf16[16,128,128]{2,1,0:T(8,128)(2,1)}, f32[16,128,128]{2,1,0:T(8,128)S(1)}, f32[16,128,128]{2,1,0:T(8,128)S(1)}) custom-call(bf16[16,128,128]{2,1,0:T(8,128)(2,1)S(1)} %bitcast.28, bf16[16,128,128]{2,1,0:T(8,128)(2,1)S(1)} %bitcast.33, f32[16,128,128]{2,1,0:T(8,128)S(1)} %get-tuple-element.74.refs_4_.lse_ref, ...), custom_call_target="tpu_custom_call" | custom-call | flops 5368709120 | bytes 8388608 | tf_op jit(solution)/shard_map/backward_local/pallas_call | solution.py:435
  163.4 0.0 collective-permute-done.14.refs_2_
  163.5 0.0 collective-permute-done.15.refs_3_
  163.5 0.0 collective-permute-done.12.refs_0_
  163.5 4.2 %collective-permute-done.13.refs_1_ = bf16[16,2,128,128]{3,2,1,0:T(8,128)(2,1)S(1)} collective-permute-done((bf16[16,2,128,128]{3,2,1,0:T(8,128)(2,1)S(1)}, bf16[16,2,128,128]{3,2,1,0:T(8,128)(2,1)S(1)}, u32[]{:S(2)}, u32[]{:S(2)}) %collective-permute-start.13) | collective-permute-done | bytes 1048608 | tf_op jit(solution)/shard_map/ppermute | solution.py:54
  167.7 1.4 finish.1
  (8 shorter events, 0.0 us)
Async XLA Ops:
  0.6 1.0 copy-start
  1.7 1.0 copy-start.2
  2.7 0.7 copy-start.4
  3.4 9.7 %copy-start.5 = (bf16[2048,128]{1,0:T(8,128)(2,1)S(1)}, bf16[2048,128]{1,0:T(8,128)(2,1)}, u32[]{:S(2)}) copy-start(bf16[2048,128]{1,0:T(8,128)(2,1)} %param.5) | copy-start | bytes 1572868
  4.3 29.3 %collective-permute-start.1 = (bf16[16,2,128,128]{3,2,1,0:T(8,128)(2,1)S(1)}, bf16[16,2,128,128]{3,2,1,0:T(8,128)(2,1)S(1)}, u32[]{:S(2)}, u32[]{:S(2)}) collective-permute-start(bf16[16,2,128,128]{3,2,1,0:T(8,128)(2,1)S(1)} %get-tuple-element.60), channel_id=1, source_target_pairs={{2,0},{4,2},{6,4},{8,6},{10,8},{12,10},{14,12},{16,14},{18,16},{20... | collective-permute-start | bytes 3145736 | tf_op jit(solution)/shard_map/ppermute | solution.py:54
  11.2 30.7 %collective-permute-start = (bf16[16,2,128,128]{3,2,1,0:T(8,128)(2,1)S(1)}, bf16[16,2,128,128]{3,2,1,0:T(8,128)(2,1)S(1)}, u32[]{:S(2)}, u32[]{:S(2)}) collective-permute-start(bf16[16,2,128,128]{3,2,1,0:T(8,128)(2,1)S(1)} %get-tuple-element.60), channel_id=1, source_target_pairs={{0,2},{2,4},{4,6},{6,8},{8,10},{10,12},{12,14},{14,16},{16,18},{18... | collective-permute-start | bytes 3145736 | tf_op jit(solution)/shard_map/ppermute | solution.py:54
  20.5 1.0 copy-start.9
  21.5 21.5 %copy-start.7 = (f32[16,128,128]{2,1,0:T(8,128)}, f32[16,128,128]{2,1,0:T(8,128)S(1)}, u32[]{:S(2)}) copy-start(f32[16,128,128]{2,1,0:T(8,128)S(1)} %get-tuple-element.61.refs_3_) | copy-start | bytes 3145732
  21.5 21.5 %copy-start.11 = (f32[16,128,128]{2,1,0:T(8,128)}, f32[16,128,128]{2,1,0:T(8,128)S(1)}, u32[]{:S(2)}) copy-start(f32[16,128,128]{2,1,0:T(8,128)S(1)} %get-tuple-element.63.refs_5_) | copy-start | bytes 3145732
  43.0 36.5 %collective-permute-start.2 = (bf16[8,2,128,128]{3,2,1,0:T(8,128)(2,1)}, bf16[8,2,128,128]{3,2,1,0:T(8,128)(2,1)S(1)}, u32[]{:S(2)}, u32[]{:S(2)}) collective-permute-start(bf16[8,2,128,128]{3,2,1,0:T(8,128)(2,1)} %get-tuple-element.69), channel_id=1, source_target_pairs={{0,2},{2,4},{4,6},{6,8},{8,10},{10,12},{12,14},{14,16},{16,18},{18... | collective-permute-start | bytes 1572872 | tf_op jit(solution)/shard_map/ppermute | solution.py:54
  44.9 34.6 %collective-permute-start.3 = (bf16[8,2,128,128]{3,2,1,0:T(8,128)(2,1)}, bf16[8,2,128,128]{3,2,1,0:T(8,128)(2,1)}, u32[]{:S(2)}, u32[]{:S(2)}) collective-permute-start(bf16[8,2,128,128]{3,2,1,0:T(8,128)(2,1)} %get-tuple-element.70), channel_id=1, source_target_pairs={{2,0},{4,2},{6,4},{8,6},{10,8},{12,10},{14,12},{16,14},{18,16},{20... | collective-permute-start | bytes 1572872 | tf_op jit(solution)/shard_map/ppermute | solution.py:54
  53.0 8.5 %collective-permute-start.7 = (bf16[2,2,128,128]{3,2,1,0:T(8,128)(2,1)S(1)}, bf16[2,2,128,128]{3,2,1,0:T(8,128)(2,1)}, u32[]{:S(2)}, u32[]{:S(2)}) collective-permute-start(bf16[2,2,128,128]{3,2,1,0:T(8,128)(2,1)S(1)} %get-tuple-element.72), channel_id=1, source_target_pairs={{16,0},{18,2},{20,4},{22,6},{24,8},{26,10},{28,12},{30,14},{32,16}... | collective-permute-start | bytes 393224 | tf_op jit(solution)/shard_map/ppermute | solution.py:54
  55.0 24.4 %collective-permute-start.5 = (bf16[4,2,128,128]{3,2,1,0:T(8,128)(2,1)}, bf16[4,2,128,128]{3,2,1,0:T(8,128)(2,1)S(1)}, u32[]{:S(2)}, u32[]{:S(2)}) collective-permute-start(bf16[4,2,128,128]{3,2,1,0:T(8,128)(2,1)} %get-tuple-element.71), channel_id=1, source_target_pairs={{8,0},{10,2},{12,4},{14,6},{16,8},{18,10},{20,12},{22,14},{24,16},... | collective-permute-start | bytes 786440 | tf_op jit(solution)/shard_map/ppermute | solution.py:54
  56.9 22.5 %collective-permute-start.4 = (bf16[4,2,128,128]{3,2,1,0:T(8,128)(2,1)}, bf16[4,2,128,128]{3,2,1,0:T(8,128)(2,1)}, u32[]{:S(2)}, u32[]{:S(2)}) collective-permute-start(bf16[4,2,128,128]{3,2,1,0:T(8,128)(2,1)} %get-tuple-element.71), channel_id=1, source_target_pairs={{0,8},{2,10},{4,12},{6,14},{8,16},{10,18},{12,20},{14,22},{16,24},... | collective-permute-start | bytes 786440 | tf_op jit(solution)/shard_map/ppermute | solution.py:54
  61.5 17.9 %collective-permute-start.6 = (bf16[2,2,128,128]{3,2,1,0:T(8,128)(2,1)S(1)}, bf16[2,2,128,128]{3,2,1,0:T(8,128)(2,1)S(1)}, u32[]{:S(2)}, u32[]{:S(2)}) collective-permute-start(bf16[2,2,128,128]{3,2,1,0:T(8,128)(2,1)S(1)} %get-tuple-element.72), channel_id=1, source_target_pairs={{0,16},{2,18},{4,20},{6,22},{8,24},{10,26},{12,28},{14,30},{16,32}... | collective-permute-start | bytes 393224 | tf_op jit(solution)/shard_map/ppermute | solution.py:54
  67.1 1.2 copy-start.8
  68.3 1.2 copy-start.10
  69.5 1.2 copy-start.12
  70.7 8.7 %copy-start.6 = (bf16[2048,128]{1,0:T(8,128)(2,1)S(1)}, bf16[2048,128]{1,0:T(8,128)(2,1)}, u32[]{:S(2)}) copy-start(bf16[2048,128]{1,0:T(8,128)(2,1)} %param.8) | copy-start | bytes 1572868
  99.1 30.2 %collective-permute-start.8 = (bf16[8,2,128,128]{3,2,1,0:T(8,128)(2,1)S(1)}, bf16[8,2,128,128]{3,2,1,0:T(8,128)(2,1)S(1)}, u32[]{:S(2)}, u32[]{:S(2)}) collective-permute-start(bf16[8,2,128,128]{3,2,1,0:T(8,128)(2,1)S(1)} %get-tuple-element.84), channel_id=1, source_target_pairs={{2,0},{4,2},{6,4},{8,6},{10,8},{12,10},{14,12},{16,14},{18,16},{20... | collective-permute-start | bytes 1572872 | tf_op jit(solution)/shard_map/ppermute | solution.py:54
  102.3 27.0 %collective-permute-start.9 = (bf16[8,2,128,128]{3,2,1,0:T(8,128)(2,1)S(1)}, bf16[8,2,128,128]{3,2,1,0:T(8,128)(2,1)S(1)}, u32[]{:S(2)}, u32[]{:S(2)}) collective-permute-start(bf16[8,2,128,128]{3,2,1,0:T(8,128)(2,1)S(1)} %get-tuple-element.85), channel_id=1, source_target_pairs={{0,2},{2,4},{4,6},{6,8},{8,10},{10,12},{12,14},{14,16},{16,18},{18... | collective-permute-start | bytes 1572872 | tf_op jit(solution)/shard_map/ppermute | solution.py:54
  104.9 24.3 %collective-permute-start.10 = (bf16[2,2,128,128]{3,2,1,0:T(8,128)(2,1)S(1)}, bf16[2,2,128,128]{3,2,1,0:T(8,128)(2,1)S(1)}, u32[]{:S(2)}, u32[]{:S(2)}) collective-permute-start(bf16[2,2,128,128]{3,2,1,0:T(8,128)(2,1)S(1)} %get-tuple-element.86), channel_id=1, source_target_pairs={{8,0},{10,2},{12,4},{14,6},{16,8},{18,10},{20,12},{22,14},{24,16},... | collective-permute-start | bytes 393224 | tf_op jit(solution)/shard_map/ppermute | solution.py:54
  111.9 17.4 %collective-permute-start.11 = (bf16[2,2,128,128]{3,2,1,0:T(8,128)(2,1)S(1)}, bf16[2,2,128,128]{3,2,1,0:T(8,128)(2,1)S(1)}, u32[]{:S(2)}, u32[]{:S(2)}) collective-permute-start(bf16[2,2,128,128]{3,2,1,0:T(8,128)(2,1)S(1)} %get-tuple-element.87), channel_id=1, source_target_pairs={{0,8},{2,10},{4,12},{6,14},{8,16},{10,18},{12,20},{14,22},{16,24},... | collective-permute-start | bytes 393224 | tf_op jit(solution)/shard_map/ppermute | solution.py:54
  129.6 33.9 %collective-permute-start.12 = (bf16[16,2,128,128]{3,2,1,0:T(8,128)(2,1)S(1)}, bf16[16,2,128,128]{3,2,1,0:T(8,128)(2,1)S(1)}, u32[]{:S(2)}, u32[]{:S(2)}) collective-permute-start(bf16[16,2,128,128]{3,2,1,0:T(8,128)(2,1)S(1)} %get-tuple-element.92), channel_id=1, source_target_pairs={{2,0},{4,2},{6,4},{8,6},{10,8},{12,10},{14,12},{16,14},{18,16},{20... | collective-permute-start | bytes 3145736 | tf_op jit(solution)/shard_map/ppermute | solution.py:54
  136.1 31.6 %collective-permute-start.13 = (bf16[16,2,128,128]{3,2,1,0:T(8,128)(2,1)S(1)}, bf16[16,2,128,128]{3,2,1,0:T(8,128)(2,1)S(1)}, u32[]{:S(2)}, u32[]{:S(2)}) collective-permute-start(bf16[16,2,128,128]{3,2,1,0:T(8,128)(2,1)S(1)} %get-tuple-element.93), channel_id=1, source_target_pairs={{0,2},{2,4},{4,6},{6,8},{8,10},{10,12},{12,14},{14,16},{16,18},{18... | collective-permute-start | bytes 3145736 | tf_op jit(solution)/shard_map/ppermute | solution.py:54
  138.0 11.4 %copy-start.3 = (bf16[2048,128]{1,0:T(8,128)(2,1)S(1)}, bf16[2048,128]{1,0:T(8,128)(2,1)}, u32[]{:S(2)}) copy-start(bf16[2048,128]{1,0:T(8,128)(2,1)} %param.7) | copy-start | bytes 1572868
  143.1 6.3 %copy-start.1 = (bf16[2048,128]{1,0:T(8,128)(2,1)S(1)}, bf16[2048,128]{1,0:T(8,128)(2,1)}, u32[]{:S(2)}) copy-start(bf16[2048,128]{1,0:T(8,128)(2,1)} %param.6) | copy-start | bytes 1572868
  143.2 20.2 %collective-permute-start.14 = (bf16[4,2,128,128]{3,2,1,0:T(8,128)(2,1)S(1)}, bf16[4,2,128,128]{3,2,1,0:T(8,128)(2,1)S(1)}, u32[]{:S(2)}, u32[]{:S(2)}) collective-permute-start(bf16[4,2,128,128]{3,2,1,0:T(8,128)(2,1)S(1)} %get-tuple-element.102), channel_id=1, source_target_pairs={{8,0},{10,2},{12,4},{14,6},{16,8},{18,10},{20,12},{22,14},{24,16},... | collective-permute-start | bytes 786440 | tf_op jit(solution)/shard_map/ppermute | solution.py:54
  146.8 16.7 %collective-permute-start.15 = (bf16[4,2,128,128]{3,2,1,0:T(8,128)(2,1)S(1)}, bf16[4,2,128,128]{3,2,1,0:T(8,128)(2,1)S(1)}, u32[]{:S(2)}, u32[]{:S(2)}) collective-permute-start(bf16[4,2,128,128]{3,2,1,0:T(8,128)(2,1)S(1)} %get-tuple-element.103), channel_id=1, source_target_pairs={{0,8},{2,10},{4,12},{6,14},{8,16},{10,18},{12,20},{14,22},{16,24},... | collective-permute-start | bytes 786440 | tf_op jit(solution)/shard_map/ppermute | solution.py:54

commit v5 on v4

--- a/solution.py
+++ b/solution.py
@@ -422,8 +422,11 @@
             dq_ref[pl.ds(first, LOCAL_ROWS)] = (
                 (dq * SCALE).astype(jnp.bfloat16).reshape(LOCAL_ROWS, BLOCK, HEAD)
             )
-            dk_ref[...] += tn(ds_ref[...], here(q_ref, u)).reshape(NBLK, BLOCK, HEAD)
-            dv_ref[...] += tn(p_ref[...], here(g_ref, u)).reshape(NBLK, BLOCK, HEAD)
+            q = here(q_ref, u)
+            g = here(g_ref, u)
+            for e in range(NBLK):
+                dk_ref[e] += tn(ds_ref[:, block(e)], q)
+                dv_ref[e] += tn(p_ref[:, block(e)], g)
 
         staggered((weights, sums), LOCAL_COPIES)
         return carry

time: 170 us -> 170 us (level)
  no operation moved by 1% of the time
where the time goes in v5:
time: 170 us; the launch traced here: 169 us
  Pallas kernels  73.5 us (43%)
  starting transfers between devices  61.7 us (36%)
  waiting for transfers between devices  25.3 us (15%)
  local copies, waits for them, and re-layouts  7.53 us (4%)
    ppermute x16, starting transfers between devices, shift(): return lax.ppermute(value, 'seq', [(s, s + by) for s in range(first, last)])  61.7 us
    pallas_call x3, Pallas kernels, backward_far(): pl.pallas_call(functools.partial(backward_far_kernel, group, dq is None),...  30 us
    ppermute x16, waiting for transfers between devices, shift(): return lax.ppermute(value, 'seq', [(s, s + by) for s in range(first, last)])  25.3 us
    pallas_call x2, Pallas kernels, forward_far(): pl.pallas_call(functools.partial(forward_far_kernel, group, last), out_sh...  18.6 us
    pallas_call x1, Pallas kernels, backward_local(): pl.pallas_call(backward_local_kernel, out_shape=(HALF, STAT, STAT), in_sp...  14 us
    unnamed x26, local copies, waits for them, and re-layouts  7.44 us
    pallas_call x1, Pallas kernels, forward_local(): pl.pallas_call(forward_local_kernel, out_shape=(STAT, STAT, STAT), in_spe...  7.32 us
  transfers between devices with their start and end apart: 16, of which 4 were waited for; matrix products, arithmetic and copies ran while one was open for 0% of the time, Pallas kernels for 30%

profile of v5, /device:TPU:96, one launch (start us, length us, event | category | flops | bytes accessed | tf_op | source)
XLA Modules:
  0.0 169.1 jit_solution(2366854837455086481)
XLA Ops:
  0.6 0.0 copy-start
  0.6 1.0 copy-done
  1.7 0.0 copy-start.2
  1.7 1.0 copy-done.2
  2.7 0.7 copy-done.4
  3.4 0.8 pack.1
  4.3 6.9 %collective-permute-start.1 = (bf16[16,2,128,128]{3,2,1,0:T(8,128)(2,1)S(1)}, bf16[16,2,128,128]{3,2,1,0:T(8,128)(2,1)S(1)}, u32[]{:S(2)}, u32[]{:S(2)}) collective-permute-start(bf16[16,2,128,128]{3,2,1,0:T(8,128)(2,1)S(1)} %get-tuple-element.60), channel_id=1, source_target_pairs={{2,0},{4,2},{6,4},{8,6},{10,8},{12,10},{14,12},{16,14},{18,16},{20... | collective-permute-start | bytes 3145736 | tf_op jit(solution)/shard_map/ppermute | solution.py:54
  11.2 1.9 %collective-permute-start = (bf16[16,2,128,128]{3,2,1,0:T(8,128)(2,1)S(1)}, bf16[16,2,128,128]{3,2,1,0:T(8,128)(2,1)S(1)}, u32[]{:S(2)}, u32[]{:S(2)}) collective-permute-start(bf16[16,2,128,128]{3,2,1,0:T(8,128)(2,1)S(1)} %get-tuple-element.60), channel_id=1, source_target_pairs={{0,2},{2,4},{4,6},{6,8},{8,10},{10,12},{12,14},{14,16},{16,18},{18... | collective-permute-start | bytes 3145736 | tf_op jit(solution)/shard_map/ppermute | solution.py:54
  13.1 0.0 copy-done.5
  13.1 7.3 %forward_local.1 = (f32[16,128,128]{2,1,0:T(8,128)S(1)}, f32[16,128,128]{2,1,0:T(8,128)S(1)}, f32[16,128,128]{2,1,0:T(8,128)S(1)}) custom-call(bf16[16,128,128]{2,1,0:T(8,128)(2,1)S(1)} %bitcast.22, bf16[16,128,128]{2,1,0:T(8,128)(2,1)S(1)} %bitcast.17, bf16[16,128,128]{2,1,0:T(8,128)(2,1)S(1)} %bitcast.20), custom_call_target="tpu_custom_call" | custom-call | flops 2147483648 | bytes 5242880 | tf_op jit(solution)/shard_map/forward_local/pallas_call | solution.py:215
  20.5 0.0 copy-start.9
  20.5 1.0 copy-done.9
  21.5 12.1 %collective-permute-done.1.refs_7_.refs_1_ = bf16[16,2,128,128]{3,2,1,0:T(8,128)(2,1)S(1)} collective-permute-done((bf16[16,2,128,128]{3,2,1,0:T(8,128)(2,1)S(1)}, bf16[16,2,128,128]{3,2,1,0:T(8,128)(2,1)S(1)}, u32[]{:S(2)}, u32[]{:S(2)}) %collective-permute-start.1) | collective-permute-done | bytes 1048608 | tf_op jit(solution)/shard_map/ppermute | solution.py:54
  33.6 8.3 %collective-permute-done.refs_6_.refs_0_ = bf16[16,2,128,128]{3,2,1,0:T(8,128)(2,1)S(1)} collective-permute-done((bf16[16,2,128,128]{3,2,1,0:T(8,128)(2,1)S(1)}, bf16[16,2,128,128]{3,2,1,0:T(8,128)(2,1)S(1)}, u32[]{:S(2)}, u32[]{:S(2)}) %collective-permute-start) | collective-permute-done | bytes 1048608 | tf_op jit(solution)/shard_map/ppermute | solution.py:54
  41.9 1.0 hand_on.1
  43.0 0.0 copy-done.7
  43.0 0.0 copy-done.11
  43.0 1.9 %collective-permute-start.2 = (bf16[8,2,128,128]{3,2,1,0:T(8,128)(2,1)}, bf16[8,2,128,128]{3,2,1,0:T(8,128)(2,1)S(1)}, u32[]{:S(2)}, u32[]{:S(2)}) collective-permute-start(bf16[8,2,128,128]{3,2,1,0:T(8,128)(2,1)} %get-tuple-element.69), channel_id=1, source_target_pairs={{0,2},{2,4},{4,6},{6,8},{8,10},{10,12},{12,14},{14,16},{16,18},{18... | collective-permute-start | bytes 1572872 | tf_op jit(solution)/shard_map/ppermute | solution.py:54
  44.9 8.1 %collective-permute-start.3 = (bf16[8,2,128,128]{3,2,1,0:T(8,128)(2,1)}, bf16[8,2,128,128]{3,2,1,0:T(8,128)(2,1)}, u32[]{:S(2)}, u32[]{:S(2)}) collective-permute-start(bf16[8,2,128,128]{3,2,1,0:T(8,128)(2,1)} %get-tuple-element.70), channel_id=1, source_target_pairs={{2,0},{4,2},{6,4},{8,6},{10,8},{12,10},{14,12},{16,14},{18,16},{20... | collective-permute-start | bytes 1572872 | tf_op jit(solution)/shard_map/ppermute | solution.py:54
  53.0 1.9 %collective-permute-start.7 = (bf16[2,2,128,128]{3,2,1,0:T(8,128)(2,1)S(1)}, bf16[2,2,128,128]{3,2,1,0:T(8,128)(2,1)}, u32[]{:S(2)}, u32[]{:S(2)}) collective-permute-start(bf16[2,2,128,128]{3,2,1,0:T(8,128)(2,1)S(1)} %get-tuple-element.72), channel_id=1, source_target_pairs={{16,0},{18,2},{20,4},{22,6},{24,8},{26,10},{28,12},{30,14},{32,16}... | collective-permute-start | bytes 393224 | tf_op jit(solution)/shard_map/ppermute | solution.py:54
  55.0 1.9 %collective-permute-start.5 = (bf16[4,2,128,128]{3,2,1,0:T(8,128)(2,1)}, bf16[4,2,128,128]{3,2,1,0:T(8,128)(2,1)S(1)}, u32[]{:S(2)}, u32[]{:S(2)}) collective-permute-start(bf16[4,2,128,128]{3,2,1,0:T(8,128)(2,1)} %get-tuple-element.71), channel_id=1, source_target_pairs={{8,0},{10,2},{12,4},{14,6},{16,8},{18,10},{20,12},{22,14},{24,16},... | collective-permute-start | bytes 786440 | tf_op jit(solution)/shard_map/ppermute | solution.py:54
  56.9 3.9 %collective-permute-start.4 = (bf16[4,2,128,128]{3,2,1,0:T(8,128)(2,1)}, bf16[4,2,128,128]{3,2,1,0:T(8,128)(2,1)}, u32[]{:S(2)}, u32[]{:S(2)}) collective-permute-start(bf16[4,2,128,128]{3,2,1,0:T(8,128)(2,1)} %get-tuple-element.71), channel_id=1, source_target_pairs={{0,8},{2,10},{4,12},{6,14},{8,16},{10,18},{12,20},{14,22},{16,24},... | collective-permute-start | bytes 786440 | tf_op jit(solution)/shard_map/ppermute | solution.py:54
  60.9 0.1 stack.35.refs_1_
  61.0 0.5 collective-permute-done.7.refs_11_.refs_9_
  61.5 5.5 %collective-permute-start.6 = (bf16[2,2,128,128]{3,2,1,0:T(8,128)(2,1)S(1)}, bf16[2,2,128,128]{3,2,1,0:T(8,128)(2,1)S(1)}, u32[]{:S(2)}, u32[]{:S(2)}) collective-permute-start(bf16[2,2,128,128]{3,2,1,0:T(8,128)(2,1)S(1)} %get-tuple-element.72), channel_id=1, source_target_pairs={{0,16},{2,18},{4,20},{6,22},{8,24},{10,26},{12,28},{14,30},{16,32}... | collective-permute-start | bytes 393224 | tf_op jit(solution)/shard_map/ppermute | solution.py:54
  67.1 0.0 copy-start.8
  67.1 1.2 copy-done.8
  68.3 1.2 copy-done.10
  69.5 1.2 copy-done.12
  70.8 8.7 %forward_far.2 = (f32[16,128,128]{2,1,0:T(8,128)S(1)}, f32[16,128,128]{2,1,0:T(8,128)S(1)}, f32[16,128,128]{2,1,0:T(8,128)S(1)}) custom-call(s32[16,30]{1,0:T(8,128)S(1)} %get-tuple-element.55.refs_0_, f32[10]{0:T(128)S(1)} %stack.35.refs_1_, bf16[16,128,128]{2,1,0:T(8,128)(2,1)S(1)} %bitcast.23, f32[16,128,128]{2,1,0:T(8,128)S(1)} %copy-done.8, ...), custom_call_target="tpu_custom_call" | custom-call | flops 2147483648 | bytes 8388608 | tf_op jit(solution)/shard_map/forward_far/pallas_call | solution.py:297
  79.4 0.0 collective-permute-done.6.refs_10_.refs_8_
  79.4 0.0 collective-permute-done.5.refs_9_.refs_7_
  79.4 0.0 collective-permute-done.4.refs_8_.refs_6_
  79.4 0.0 collective-permute-done.2.refs_6_
  79.5 0.0 collective-permute-done.3.refs_7_
  79.5 0.0 copy-done.6
  79.5 9.9 %forward_far.3 = (bf16[16,128,128]{2,1,0:T(8,128)(2,1)}, f32[16,128,128]{2,1,0:T(8,128)S(1)}, f32[16,128,128]{2,1,0:T(8,128)S(1)}) custom-call(s32[16,30]{1,0:T(8,128)S(1)} %get-tuple-element.55.refs_0_, f32[10]{0:T(128)S(1)} %stack.35.refs_1_, bf16[16,128,128]{2,1,0:T(8,128)(2,1)S(1)} %bitcast.24, f32[16,128,128]{2,1,0:T(8,128)S(1)} %get-tuple-element.66.refs_3_, ...), custom_call_target="tpu_custom_call" | custom-call | flops 1879048192 | bytes 8388608 | tf_op jit(solution)/shard_map/forward_far/pallas_call | solution.py:297
  89.4 9.6 %backward_far.3 = (f32[16,128,128]{2,1,0:T(8,128)S(1)}, bf16[8,2,128,128]{3,2,1,0:T(8,128)(2,1)S(1)}, bf16[8,2,128,128]{3,2,1,0:T(8,128)(2,1)S(1)}, bf16[2,2,128...) custom-call(s32[16,30]{1,0:T(8,128)S(1)} %get-tuple-element.55.refs_0_, f32[10]{0:T(128)S(1)} %stack.35.refs_1_, ...), custom_call_target="tpu_custom_call" | custom-call | flops 3355443200 | bytes 8388608 | tf_op jit(solution)/shard_map/backward_far/pallas_call | solution.py:373
  99.1 3.2 %collective-permute-start.8 = (bf16[8,2,128,128]{3,2,1,0:T(8,128)(2,1)S(1)}, bf16[8,2,128,128]{3,2,1,0:T(8,128)(2,1)S(1)}, u32[]{:S(2)}, u32[]{:S(2)}) collective-permute-start(bf16[8,2,128,128]{3,2,1,0:T(8,128)(2,1)S(1)} %get-tuple-element.84), channel_id=1, source_target_pairs={{2,0},{4,2},{6,4},{8,6},{10,8},{12,10},{14,12},{16,14},{18,16},{20... | collective-permute-start | bytes 1572872 | tf_op jit(solution)/shard_map/ppermute | solution.py:54
  102.3 2.6 %collective-permute-start.9 = (bf16[8,2,128,128]{3,2,1,0:T(8,128)(2,1)S(1)}, bf16[8,2,128,128]{3,2,1,0:T(8,128)(2,1)S(1)}, u32[]{:S(2)}, u32[]{:S(2)}) collective-permute-start(bf16[8,2,128,128]{3,2,1,0:T(8,128)(2,1)S(1)} %get-tuple-element.85), channel_id=1, source_target_pairs={{0,2},{2,4},{4,6},{6,8},{8,10},{10,12},{12,14},{14,16},{16,18},{18... | collective-permute-start | bytes 1572872 | tf_op jit(solution)/shard_map/ppermute | solution.py:54
  104.9 6.9 %collective-permute-start.10 = (bf16[2,2,128,128]{3,2,1,0:T(8,128)(2,1)S(1)}, bf16[2,2,128,128]{3,2,1,0:T(8,128)(2,1)S(1)}, u32[]{:S(2)}, u32[]{:S(2)}) collective-permute-start(bf16[2,2,128,128]{3,2,1,0:T(8,128)(2,1)S(1)} %get-tuple-element.86), channel_id=1, source_target_pairs={{8,0},{10,2},{12,4},{14,6},{16,8},{18,10},{20,12},{22,14},{24,16},... | collective-permute-start | bytes 393224 | tf_op jit(solution)/shard_map/ppermute | solution.py:54
  111.9 2.1 %collective-permute-start.11 = (bf16[2,2,128,128]{3,2,1,0:T(8,128)(2,1)S(1)}, bf16[2,2,128,128]{3,2,1,0:T(8,128)(2,1)S(1)}, u32[]{:S(2)}, u32[]{:S(2)}) collective-permute-start(bf16[2,2,128,128]{3,2,1,0:T(8,128)(2,1)S(1)} %get-tuple-element.87), channel_id=1, source_target_pairs={{0,8},{2,10},{4,12},{6,14},{8,16},{10,18},{12,20},{14,22},{16,24},... | collective-permute-start | bytes 393224 | tf_op jit(solution)/shard_map/ppermute | solution.py:54
  114.0 15.3 %backward_far.4 = (f32[16,128,128]{2,1,0:T(8,128)S(1)}, bf16[16,2,128,128]{3,2,1,0:T(8,128)(2,1)S(1)}, bf16[16,2,128,128]{3,2,1,0:T(8,128)(2,1)S(1)}) custom-call(s32[16,30]{1,0:T(8,128)S(1)} %get-tuple-element.55.refs_0_, f32[10]{0:T(128)S(1)} %stack.35.refs_1_, bf16[16,128,128]{2,1,0:T(8,128)(2,1)S(1)} %bitcast.26, bf16[16,128,128]{2,1,0:T(8,128)(2,1)S(1)} %bitcast.31, ...), custom_call_target="tpu_custom_call" | custom-call | flops 5368709120 | bytes 8388608 | tf_op jit(solution)/shard_map/backward_far/pallas_call | solution.py:373
  129.2 0.0 collective-permute-done.10.refs_2_
  129.2 0.0 collective-permute-done.11.refs_3_
  129.3 0.0 collective-permute-done.8.refs_2_
  129.3 0.0 collective-permute-done.9.refs_3_
  129.3 0.3 merge.2
  129.6 6.5 %collective-permute-start.12 = (bf16[16,2,128,128]{3,2,1,0:T(8,128)(2,1)S(1)}, bf16[16,2,128,128]{3,2,1,0:T(8,128)(2,1)S(1)}, u32[]{:S(2)}, u32[]{:S(2)}) collective-permute-start(bf16[16,2,128,128]{3,2,1,0:T(8,128)(2,1)S(1)} %get-tuple-element.92), channel_id=1, source_target_pairs={{2,0},{4,2},{6,4},{8,6},{10,8},{12,10},{14,12},{16,14},{18,16},{20... | collective-permute-start | bytes 3145736 | tf_op jit(solution)/shard_map/ppermute | solution.py:54
  136.1 1.9 %collective-permute-start.13 = (bf16[16,2,128,128]{3,2,1,0:T(8,128)(2,1)S(1)}, bf16[16,2,128,128]{3,2,1,0:T(8,128)(2,1)S(1)}, u32[]{:S(2)}, u32[]{:S(2)}) collective-permute-start(bf16[16,2,128,128]{3,2,1,0:T(8,128)(2,1)S(1)} %get-tuple-element.93), channel_id=1, source_target_pairs={{0,2},{2,4},{4,6},{6,8},{8,10},{10,12},{12,14},{14,16},{16,18},{18... | collective-permute-start | bytes 3145736 | tf_op jit(solution)/shard_map/ppermute | solution.py:54
  138.0 0.0 copy-start.3
  138.0 5.1 %backward_far.5 = (f32[16,128,128]{2,1,0:T(8,128)S(1)}, bf16[4,2,128,128]{3,2,1,0:T(8,128)(2,1)S(1)}, bf16[4,2,128,128]{3,2,1,0:T(8,128)(2,1)S(1)}) custom-call(s32[16,30]{1,0:T(8,128)S(1)} %get-tuple-element.55.refs_0_, f32[10]{0:T(128)S(1)} %stack.35.refs_1_, bf16[16,128,128]{2,1,0:T(8,128)(2,1)S(1)} %bitcast.27, bf16[16,128,128]{2,1,0:T(8,128)(2,1)S(1)} %bitcast.32, ...), custom_call_target="tpu_custom_call" | custom-call | flops 1342177280 | bytes 8388608 | tf_op jit(solution)/shard_map/backward_far/pallas_call | solution.py:373
  143.1 0.0 copy-start.1
  143.1 0.1 merge.3
  143.2 3.6 %collective-permute-start.14 = (bf16[4,2,128,128]{3,2,1,0:T(8,128)(2,1)S(1)}, bf16[4,2,128,128]{3,2,1,0:T(8,128)(2,1)S(1)}, u32[]{:S(2)}, u32[]{:S(2)}) collective-permute-start(bf16[4,2,128,128]{3,2,1,0:T(8,128)(2,1)S(1)} %get-tuple-element.102), channel_id=1, source_target_pairs={{8,0},{10,2},{12,4},{14,6},{16,8},{18,10},{20,12},{22,14},{24,16},... | collective-permute-start | bytes 786440 | tf_op jit(solution)/shard_map/ppermute | solution.py:54
  146.8 2.6 %collective-permute-start.15 = (bf16[4,2,128,128]{3,2,1,0:T(8,128)(2,1)S(1)}, bf16[4,2,128,128]{3,2,1,0:T(8,128)(2,1)S(1)}, u32[]{:S(2)}, u32[]{:S(2)}) collective-permute-start(bf16[4,2,128,128]{3,2,1,0:T(8,128)(2,1)S(1)} %get-tuple-element.103), channel_id=1, source_target_pairs={{0,8},{2,10},{4,12},{6,14},{8,16},{10,18},{12,20},{14,22},{16,24},... | collective-permute-start | bytes 786440 | tf_op jit(solution)/shard_map/ppermute | solution.py:54
  149.4 0.0 copy-done.3
  149.4 0.0 copy-done.1
  149.4 14.0 %backward_local.1 = (bf16[16,128,128]{2,1,0:T(8,128)(2,1)}, f32[16,128,128]{2,1,0:T(8,128)S(1)}, f32[16,128,128]{2,1,0:T(8,128)S(1)}) custom-call(bf16[16,128,128]{2,1,0:T(8,128)(2,1)S(1)} %bitcast.28, bf16[16,128,128]{2,1,0:T(8,128)(2,1)S(1)} %bitcast.33, f32[16,128,128]{2,1,0:T(8,128)S(1)} %get-tuple-element.74.refs_4_.lse_ref, ...), custom_call_target="tpu_custom_call" | custom-call | flops 5368709120 | bytes 8388608 | tf_op jit(solution)/shard_map/backward_local/pallas_call | solution.py:438
  163.4 0.0 collective-permute-done.14.refs_2_
  163.4 0.0 collective-permute-done.15.refs_3_
  163.5 0.0 collective-permute-done.12.refs_0_
  163.5 4.2 %collective-permute-done.13.refs_1_ = bf16[16,2,128,128]{3,2,1,0:T(8,128)(2,1)S(1)} collective-permute-done((bf16[16,2,128,128]{3,2,1,0:T(8,128)(2,1)S(1)}, bf16[16,2,128,128]{3,2,1,0:T(8,128)(2,1)S(1)}, u32[]{:S(2)}, u32[]{:S(2)}) %collective-permute-start.13) | collective-permute-done | bytes 1048608 | tf_op jit(solution)/shard_map/ppermute | solution.py:54
  167.7 1.4 finish.1
  (8 shorter events, 0.0 us)
Async XLA Ops:
  0.6 1.0 copy-start
  1.7 1.0 copy-start.2
  2.7 0.7 copy-start.4
  3.4 9.7 %copy-start.5 = (bf16[2048,128]{1,0:T(8,128)(2,1)S(1)}, bf16[2048,128]{1,0:T(8,128)(2,1)}, u32[]{:S(2)}) copy-start(bf16[2048,128]{1,0:T(8,128)(2,1)} %param.5) | copy-start | bytes 1572868
  4.3 29.3 %collective-permute-start.1 = (bf16[16,2,128,128]{3,2,1,0:T(8,128)(2,1)S(1)}, bf16[16,2,128,128]{3,2,1,0:T(8,128)(2,1)S(1)}, u32[]{:S(2)}, u32[]{:S(2)}) collective-permute-start(bf16[16,2,128,128]{3,2,1,0:T(8,128)(2,1)S(1)} %get-tuple-element.60), channel_id=1, source_target_pairs={{2,0},{4,2},{6,4},{8,6},{10,8},{12,10},{14,12},{16,14},{18,16},{20... | collective-permute-start | bytes 3145736 | tf_op jit(solution)/shard_map/ppermute | solution.py:54
  11.2 30.7 %collective-permute-start = (bf16[16,2,128,128]{3,2,1,0:T(8,128)(2,1)S(1)}, bf16[16,2,128,128]{3,2,1,0:T(8,128)(2,1)S(1)}, u32[]{:S(2)}, u32[]{:S(2)}) collective-permute-start(bf16[16,2,128,128]{3,2,1,0:T(8,128)(2,1)S(1)} %get-tuple-element.60), channel_id=1, source_target_pairs={{0,2},{2,4},{4,6},{6,8},{8,10},{10,12},{12,14},{14,16},{16,18},{18... | collective-permute-start | bytes 3145736 | tf_op jit(solution)/shard_map/ppermute | solution.py:54
  20.5 1.0 copy-start.9
  21.5 21.5 %copy-start.7 = (f32[16,128,128]{2,1,0:T(8,128)}, f32[16,128,128]{2,1,0:T(8,128)S(1)}, u32[]{:S(2)}) copy-start(f32[16,128,128]{2,1,0:T(8,128)S(1)} %get-tuple-element.61.refs_3_) | copy-start | bytes 3145732
  21.5 21.5 %copy-start.11 = (f32[16,128,128]{2,1,0:T(8,128)}, f32[16,128,128]{2,1,0:T(8,128)S(1)}, u32[]{:S(2)}) copy-start(f32[16,128,128]{2,1,0:T(8,128)S(1)} %get-tuple-element.63.refs_5_) | copy-start | bytes 3145732
  43.0 36.5 %collective-permute-start.2 = (bf16[8,2,128,128]{3,2,1,0:T(8,128)(2,1)}, bf16[8,2,128,128]{3,2,1,0:T(8,128)(2,1)S(1)}, u32[]{:S(2)}, u32[]{:S(2)}) collective-permute-start(bf16[8,2,128,128]{3,2,1,0:T(8,128)(2,1)} %get-tuple-element.69), channel_id=1, source_target_pairs={{0,2},{2,4},{4,6},{6,8},{8,10},{10,12},{12,14},{14,16},{16,18},{18... | collective-permute-start | bytes 1572872 | tf_op jit(solution)/shard_map/ppermute | solution.py:54
  44.9 34.6 %collective-permute-start.3 = (bf16[8,2,128,128]{3,2,1,0:T(8,128)(2,1)}, bf16[8,2,128,128]{3,2,1,0:T(8,128)(2,1)}, u32[]{:S(2)}, u32[]{:S(2)}) collective-permute-start(bf16[8,2,128,128]{3,2,1,0:T(8,128)(2,1)} %get-tuple-element.70), channel_id=1, source_target_pairs={{2,0},{4,2},{6,4},{8,6},{10,8},{12,10},{14,12},{16,14},{18,16},{20... | collective-permute-start | bytes 1572872 | tf_op jit(solution)/shard_map/ppermute | solution.py:54
  53.0 8.5 %collective-permute-start.7 = (bf16[2,2,128,128]{3,2,1,0:T(8,128)(2,1)S(1)}, bf16[2,2,128,128]{3,2,1,0:T(8,128)(2,1)}, u32[]{:S(2)}, u32[]{:S(2)}) collective-permute-start(bf16[2,2,128,128]{3,2,1,0:T(8,128)(2,1)S(1)} %get-tuple-element.72), channel_id=1, source_target_pairs={{16,0},{18,2},{20,4},{22,6},{24,8},{26,10},{28,12},{30,14},{32,16}... | collective-permute-start | bytes 393224 | tf_op jit(solution)/shard_map/ppermute | solution.py:54
  55.0 24.4 %collective-permute-start.5 = (bf16[4,2,128,128]{3,2,1,0:T(8,128)(2,1)}, bf16[4,2,128,128]{3,2,1,0:T(8,128)(2,1)S(1)}, u32[]{:S(2)}, u32[]{:S(2)}) collective-permute-start(bf16[4,2,128,128]{3,2,1,0:T(8,128)(2,1)} %get-tuple-element.71), channel_id=1, source_target_pairs={{8,0},{10,2},{12,4},{14,6},{16,8},{18,10},{20,12},{22,14},{24,16},... | collective-permute-start | bytes 786440 | tf_op jit(solution)/shard_map/ppermute | solution.py:54
  56.9 22.5 %collective-permute-start.4 = (bf16[4,2,128,128]{3,2,1,0:T(8,128)(2,1)}, bf16[4,2,128,128]{3,2,1,0:T(8,128)(2,1)}, u32[]{:S(2)}, u32[]{:S(2)}) collective-permute-start(bf16[4,2,128,128]{3,2,1,0:T(8,128)(2,1)} %get-tuple-element.71), channel_id=1, source_target_pairs={{0,8},{2,10},{4,12},{6,14},{8,16},{10,18},{12,20},{14,22},{16,24},... | collective-permute-start | bytes 786440 | tf_op jit(solution)/shard_map/ppermute | solution.py:54
  61.5 17.9 %collective-permute-start.6 = (bf16[2,2,128,128]{3,2,1,0:T(8,128)(2,1)S(1)}, bf16[2,2,128,128]{3,2,1,0:T(8,128)(2,1)S(1)}, u32[]{:S(2)}, u32[]{:S(2)}) collective-permute-start(bf16[2,2,128,128]{3,2,1,0:T(8,128)(2,1)S(1)} %get-tuple-element.72), channel_id=1, source_target_pairs={{0,16},{2,18},{4,20},{6,22},{8,24},{10,26},{12,28},{14,30},{16,32}... | collective-permute-start | bytes 393224 | tf_op jit(solution)/shard_map/ppermute | solution.py:54
  67.1 1.2 copy-start.8
  68.3 1.2 copy-start.10
  69.5 1.2 copy-start.12
  70.7 8.7 %copy-start.6 = (bf16[2048,128]{1,0:T(8,128)(2,1)S(1)}, bf16[2048,128]{1,0:T(8,128)(2,1)}, u32[]{:S(2)}) copy-start(bf16[2048,128]{1,0:T(8,128)(2,1)} %param.8) | copy-start | bytes 1572868
  99.1 30.2 %collective-permute-start.8 = (bf16[8,2,128,128]{3,2,1,0:T(8,128)(2,1)S(1)}, bf16[8,2,128,128]{3,2,1,0:T(8,128)(2,1)S(1)}, u32[]{:S(2)}, u32[]{:S(2)}) collective-permute-start(bf16[8,2,128,128]{3,2,1,0:T(8,128)(2,1)S(1)} %get-tuple-element.84), channel_id=1, source_target_pairs={{2,0},{4,2},{6,4},{8,6},{10,8},{12,10},{14,12},{16,14},{18,16},{20... | collective-permute-start | bytes 1572872 | tf_op jit(solution)/shard_map/ppermute | solution.py:54
  102.3 27.0 %collective-permute-start.9 = (bf16[8,2,128,128]{3,2,1,0:T(8,128)(2,1)S(1)}, bf16[8,2,128,128]{3,2,1,0:T(8,128)(2,1)S(1)}, u32[]{:S(2)}, u32[]{:S(2)}) collective-permute-start(bf16[8,2,128,128]{3,2,1,0:T(8,128)(2,1)S(1)} %get-tuple-element.85), channel_id=1, source_target_pairs={{0,2},{2,4},{4,6},{6,8},{8,10},{10,12},{12,14},{14,16},{16,18},{18... | collective-permute-start | bytes 1572872 | tf_op jit(solution)/shard_map/ppermute | solution.py:54
  104.9 24.3 %collective-permute-start.10 = (bf16[2,2,128,128]{3,2,1,0:T(8,128)(2,1)S(1)}, bf16[2,2,128,128]{3,2,1,0:T(8,128)(2,1)S(1)}, u32[]{:S(2)}, u32[]{:S(2)}) collective-permute-start(bf16[2,2,128,128]{3,2,1,0:T(8,128)(2,1)S(1)} %get-tuple-element.86), channel_id=1, source_target_pairs={{8,0},{10,2},{12,4},{14,6},{16,8},{18,10},{20,12},{22,14},{24,16},... | collective-permute-start | bytes 393224 | tf_op jit(solution)/shard_map/ppermute | solution.py:54
  111.9 17.4 %collective-permute-start.11 = (bf16[2,2,128,128]{3,2,1,0:T(8,128)(2,1)S(1)}, bf16[2,2,128,128]{3,2,1,0:T(8,128)(2,1)S(1)}, u32[]{:S(2)}, u32[]{:S(2)}) collective-permute-start(bf16[2,2,128,128]{3,2,1,0:T(8,128)(2,1)S(1)} %get-tuple-element.87), channel_id=1, source_target_pairs={{0,8},{2,10},{4,12},{6,14},{8,16},{10,18},{12,20},{14,22},{16,24},... | collective-permute-start | bytes 393224 | tf_op jit(solution)/shard_map/ppermute | solution.py:54
  129.6 33.9 %collective-permute-start.12 = (bf16[16,2,128,128]{3,2,1,0:T(8,128)(2,1)S(1)}, bf16[16,2,128,128]{3,2,1,0:T(8,128)(2,1)S(1)}, u32[]{:S(2)}, u32[]{:S(2)}) collective-permute-start(bf16[16,2,128,128]{3,2,1,0:T(8,128)(2,1)S(1)} %get-tuple-element.92), channel_id=1, source_target_pairs={{2,0},{4,2},{6,4},{8,6},{10,8},{12,10},{14,12},{16,14},{18,16},{20... | collective-permute-start | bytes 3145736 | tf_op jit(solution)/shard_map/ppermute | solution.py:54
  136.1 31.6 %collective-permute-start.13 = (bf16[16,2,128,128]{3,2,1,0:T(8,128)(2,1)S(1)}, bf16[16,2,128,128]{3,2,1,0:T(8,128)(2,1)S(1)}, u32[]{:S(2)}, u32[]{:S(2)}) collective-permute-start(bf16[16,2,128,128]{3,2,1,0:T(8,128)(2,1)S(1)} %get-tuple-element.93), channel_id=1, source_target_pairs={{0,2},{2,4},{4,6},{6,8},{8,10},{10,12},{12,14},{14,16},{16,18},{18... | collective-permute-start | bytes 3145736 | tf_op jit(solution)/shard_map/ppermute | solution.py:54
  138.0 11.4 %copy-start.3 = (bf16[2048,128]{1,0:T(8,128)(2,1)S(1)}, bf16[2048,128]{1,0:T(8,128)(2,1)}, u32[]{:S(2)}) copy-start(bf16[2048,128]{1,0:T(8,128)(2,1)} %param.7) | copy-start | bytes 1572868
  143.1 6.3 %copy-start.1 = (bf16[2048,128]{1,0:T(8,128)(2,1)S(1)}, bf16[2048,128]{1,0:T(8,128)(2,1)}, u32[]{:S(2)}) copy-start(bf16[2048,128]{1,0:T(8,128)(2,1)} %param.6) | copy-start | bytes 1572868
  143.2 20.2 %collective-permute-start.14 = (bf16[4,2,128,128]{3,2,1,0:T(8,128)(2,1)S(1)}, bf16[4,2,128,128]{3,2,1,0:T(8,128)(2,1)S(1)}, u32[]{:S(2)}, u32[]{:S(2)}) collective-permute-start(bf16[4,2,128,128]{3,2,1,0:T(8,128)(2,1)S(1)} %get-tuple-element.102), channel_id=1, source_target_pairs={{8,0},{10,2},{12,4},{14,6},{16,8},{18,10},{20,12},{22,14},{24,16},... | collective-permute-start | bytes 786440 | tf_op jit(solution)/shard_map/ppermute | solution.py:54
  146.8 16.7 %collective-permute-start.15 = (bf16[4,2,128,128]{3,2,1,0:T(8,128)(2,1)S(1)}, bf16[4,2,128,128]{3,2,1,0:T(8,128)(2,1)S(1)}, u32[]{:S(2)}, u32[]{:S(2)}) collective-permute-start(bf16[4,2,128,128]{3,2,1,0:T(8,128)(2,1)S(1)} %get-tuple-element.103), channel_id=1, source_target_pairs={{0,8},{2,10},{4,12},{6,14},{8,16},{10,18},{12,20},{14,22},{16,24},... | collective-permute-start | bytes 786440 | tf_op jit(solution)/shard_map/ppermute | solution.py:54
